TPU v7x, 256 devices: a whole 4x4x8 slice. The times are simulated.
256 devices in a mesh: seq: 64 (over x_lo, z, y), ch: 4 (over x_hi, core).
Axes of the slice: x: 4 (x_hi: 2, x_lo: 2; x = x_hi * 2 + x_lo), y: 4, z: 8, core: 2. Of those that a mesh axis runs over, the one named last changes fastest.
Arguments:
- tokens: bfloat16 [32768, 1024], P('seq', 'ch'), may hold values from -400 to 400
- norm_gain: float32 [1024], replicated, may hold values from 0.5 to 1.5
- w_in: bfloat16 [1024, 3, 1024], P(None, None, 'ch'), may hold values from -0.1875 to 0.1875
- short_filter: float32 [3, 3, 1024], P(None, None, 'ch'), may hold values from -3 to 3
- rates: float32 [16, 1024], P(None, 'ch'), may hold values from 7.6293945e-06 to 0.05
- residues: float32 [16, 1024], P(None, 'ch'), may hold values from -1.5 to 1.5
- skip_gain: float32 [1024], P('ch'), may hold values from -4 to 4
- w_out: bfloat16 [1024, 1024], P('ch'), may hold values from -0.1875 to 0.1875
Outputs:
- mixed: bfloat16 [32768, 1024], P('seq', 'ch')
All inputs are finite; a program needn't handle non-finite values.
Results may differ from a plain program's by a relative error of at most 0.009.
Values may be sent and summed in bfloat16 or wider, within the bound.
No kernel may reach another device: no remote copies, remote signals or barrier semaphores. Data moves between devices by JAX's collectives and lax.ppermute only.
A program may use at most 64 MiB of HBM per device.

v0:
```python
import math

import jax
import jax.numpy as jnp
from jax import lax
from jax.sharding import PartitionSpec as P

EPSILON = 1e-06
HIGHEST = lax.Precision.HIGHEST
TWO_PI = 2.0 * math.pi


def swapped(array, axis, distance):
    return lax.ppermute(array, axis, [(i, i ^ 1 << distance) for i in range(lax.axis_size(axis))])


def passed_along(array, axis, by):
    count = lax.axis_size(axis)
    pairs = [(i, i + by) for i in range(count) if 0 <= i + by < count]
    return lax.ppermute(array, axis, pairs)


def mat_dot(left, right):
    return jnp.dot(left, right, precision=HIGHEST, preferred_element_type=jnp.float32)


def left_dot(left, right):
    return lax.dot_general(
        left, right, (((0,), (0,)), ((), ())), precision=HIGHEST, preferred_element_type=jnp.float32
    )


def bit_reverse(device, bit_count):
    result = jnp.zeros((), jnp.int32)
    for bit_level in range(bit_count):
        digit = jnp.bitwise_and(jnp.right_shift(device, bit_level), 1)
        result = result + jnp.left_shift(digit, bit_count - 1 - bit_level)
    return result


def pair_twiddle(device, bit_level):
    half_size = 1 << bit_level
    upper = jnp.bitwise_and(jnp.right_shift(device, bit_level), 1) == 1
    phase_angle = jnp.remainder(device, half_size).astype(jnp.float32) * (TWO_PI / (2 * half_size))
    return (upper, jnp.cos(phase_angle), jnp.sin(phase_angle))


def forward_sections(data_re, data_im, device, bit_count):
    for bit_level in range(bit_count - 1, -1, -1):
        other_re, other_im = (
            swapped(data_re.astype(jnp.bfloat16), "seq", bit_level).astype(data_re.dtype),
            swapped(data_im.astype(jnp.bfloat16), "seq", bit_level).astype(data_im.dtype),
        )
        upper, cosine, sine = pair_twiddle(device, bit_level)
        diff_re = other_re - data_re
        diff_im = other_im - data_im
        turned_re = diff_re * cosine + diff_im * sine
        turned_im = diff_im * cosine - diff_re * sine
        data_re = jnp.where(upper, turned_re, data_re + other_re)
        data_im = jnp.where(upper, turned_im, data_im + other_im)
    return (data_re, data_im)


def inverse_sections(data_re, data_im, device, bit_count):
    for bit_level in range(bit_count):
        other_re, other_im = swapped((data_re, data_im), "seq", bit_level)
        upper, cosine, sine = pair_twiddle(device, bit_level)
        source_re = jnp.where(upper, data_re, other_re)
        source_im = jnp.where(upper, data_im, other_im)
        anchor_re = jnp.where(upper, other_re, data_re)
        anchor_im = jnp.where(upper, other_im, data_im)
        turned_re = source_re * cosine - source_im * sine
        turned_im = source_im * cosine + source_re * sine
        signed = jnp.where(upper, -1.0, 1.0).astype(jnp.float32)
        data_re = anchor_re + signed * turned_re
        data_im = anchor_im + signed * turned_im
    return (data_re, data_im)


def local_tables(first_freq, row_count, device_count, seq_len):
    across = jnp.arange(row_count, dtype=jnp.int32)
    product = across[None, :] * (first_freq + device_count * across[:, None])
    phase_angle = jnp.remainder(product, seq_len).astype(jnp.float32) * (TWO_PI / seq_len)
    return (jnp.cos(phase_angle), jnp.sin(phase_angle))


def modal_spectrum(rates, residues, frequencies, padded_len, seq_len):
    centred = jnp.where(frequencies >= seq_len, frequencies - padded_len, frequencies).astype(
        jnp.float32
    )
    phase_angle = centred * (TWO_PI / padded_len)
    half_sine = jnp.sin(0.5 * phase_angle)
    full_sine = jnp.sin(phase_angle)
    parity_sign = 1.0 - 2.0 * jnp.remainder(frequencies, 2).astype(jnp.float32)
    out_shape = (frequencies.shape[0], 2, rates.shape[1])

    def add_mode(mode_index, totals):
        sum_real, sum_imag = totals
        rate_row = lax.dynamic_index_in_dim(rates, mode_index, 0, keepdims=True)[None]
        residue_row = lax.dynamic_index_in_dim(residues, mode_index, 0, keepdims=True)[None]
        decay = jnp.exp(-rate_row)
        decay_gap = -jnp.expm1(-rate_row)
        real_den = decay_gap + 2.0 * decay * half_sine * half_sine
        imag_den = decay * full_sine
        numerator = (
            residue_row * jnp.sqrt(rate_row) * (1.0 - parity_sign * jnp.exp(-rate_row * seq_len))
        )
        weight_term = numerator / (real_den * real_den + imag_den * imag_den)
        return (sum_real + weight_term * real_den, sum_imag - weight_term * imag_den)

    zeros_init = jnp.zeros(out_shape, jnp.float32)
    sum_real, sum_imag = lax.fori_loop(0, rates.shape[0], add_mode, (zeros_init, zeros_init))
    return (sum_real.reshape(out_shape[0], -1), sum_imag.reshape(out_shape[0], -1))


def spectral_convolve(gated_product, rates, residues):
    row_count, channels = gated_product.shape
    device_count = lax.axis_size("seq")
    device = lax.axis_index("seq")
    bit_count = device_count.bit_length() - 1
    seq_len = row_count * device_count
    padded_len = 2 * seq_len
    positions = device * row_count + jnp.arange(row_count, dtype=jnp.int32)
    phase_shift = positions.astype(jnp.float32)[:, None] * (TWO_PI / padded_len)
    cos_shift = jnp.cos(phase_shift)
    sin_shift = jnp.sin(phase_shift)
    data_re = jnp.concatenate([gated_product, gated_product * cos_shift], axis=1)
    data_im = jnp.concatenate([jnp.zeros_like(gated_product), -gated_product * sin_shift], axis=1)
    data_re, data_im = forward_sections(data_re, data_im, device, bit_count)
    first_freq = bit_reverse(device, bit_count)
    cos_table, sin_table = local_tables(first_freq, row_count, device_count, seq_len)
    spec_re = mat_dot(cos_table, data_re) + mat_dot(sin_table, data_im)
    spec_im = mat_dot(cos_table, data_im) - mat_dot(sin_table, data_re)
    freq_base = first_freq + device_count * jnp.arange(row_count, dtype=jnp.int32)
    frequencies = (2 * freq_base[:, None] + jnp.arange(2, dtype=jnp.int32)[None, :])[:, :, None]
    gain_re, gain_im = modal_spectrum(rates, residues, frequencies, padded_len, seq_len)
    prod_re = spec_re * gain_re - spec_im * gain_im
    prod_im = spec_re * gain_im + spec_im * gain_re
    back_re = left_dot(cos_table, prod_re) - left_dot(sin_table, prod_im)
    back_im = left_dot(cos_table, prod_im) + left_dot(sin_table, prod_re)
    back_re, back_im = inverse_sections(back_re, back_im, device, bit_count)
    return (
        back_re[:, :channels]
        + cos_shift * back_re[:, channels:]
        - sin_shift * back_im[:, channels:]
    ) * (1.0 / padded_len)


def body(tokens, norm_gain, w_in, short_filter, rates, residues, skip_gain, w_out):
    whole = lax.all_gather(tokens, "ch", axis=1, tiled=True)
    values = whole.astype(jnp.float32)
    mean_square = jnp.mean(values * values, axis=-1, keepdims=True)
    normed = (values * lax.rsqrt(mean_square + EPSILON) * norm_gain).astype(jnp.bfloat16)
    row_count, slab_width = normed.shape
    channels = w_in.shape[2]
    tap_count = short_filter.shape[0]
    projected = jnp.dot(
        normed, w_in.reshape(slab_width, 3 * channels), preferred_element_type=jnp.float32
    ).astype(jnp.bfloat16)
    earlier = passed_along(projected[row_count - (tap_count - 1) :], "seq", 1)
    padded = jnp.concatenate([earlier, projected], axis=0).astype(jnp.float32)
    taps_flat = short_filter.reshape(tap_count, 3 * channels)
    filtered = jnp.zeros((row_count, 3 * channels), jnp.float32)
    for tap_index in range(tap_count):
        start_row = tap_count - 1 - tap_index
        filtered = filtered + taps_flat[tap_index] * padded[start_row : start_row + row_count]
    queries = filtered[:, :channels]
    gated_product = filtered[:, channels : 2 * channels] * filtered[:, 2 * channels :]
    convolved = spectral_convolve(gated_product, rates, residues)
    mixed_in = (queries * (convolved + skip_gain * gated_product)).astype(jnp.bfloat16)
    partial_sums = jnp.dot(mixed_in, w_out, preferred_element_type=jnp.float32)
    return lax.psum_scatter(partial_sums, "ch", scatter_dimension=1, tiled=True).astype(
        jnp.bfloat16
    )


def solution(mesh):
    return jax.shard_map(
        body,
        mesh=mesh,
        in_specs=(
            P("seq", "ch"),
            P(),
            P(None, None, "ch"),
            P(None, None, "ch"),
            P(None, "ch"),
            P(None, "ch"),
            P("ch"),
            P("ch", None),
        ),
        out_specs=P("seq", "ch"),
        check_vma=False,
    )
```

profile of v0, /device:TPU:1, one launch (start us, length us, event | category | flops | bytes accessed | tf_op | source)
XLA Modules:
  0.0 843.9 jit_solution(14466392886620231436)
XLA Ops:
  9.1 27.7 %all-gather.2.cloned.1.call-done = bf16[512,1024]{1,0:T(8,128)(2,1)} async-done(((bf16[512,256]{1,0:T(8,128)(2,1)}), bf16[512,1024]{1,0:T(8,128)(2,1)}) %all-gather.2.cloned.1.call-update) | async-done | bytes 1048592 | tf_op jit(solution)/shard_map/all_gather | solution.py:150
  63.8 10.5 %collective-permute-done.2 = bf16[512,512]{1,0:T(8,128)(2,1)} collective-permute-done((bf16[512,512]{1,0:T(8,128)(2,1)}, bf16[512,512]{1,0:T(8,128)(2,1)}, u32[]{:S(2)}, u32[]{:S(2)}) %collective-permute-start.2) | collective-permute-done | bytes 524320 | tf_op jit(solution)/shard_map/ppermute | solution.py:14
  82.8 26.8 %collective-permute-done.3 = bf16[512,512]{1,0:T(8,128)(2,1)S(1)} collective-permute-done((bf16[512,512]{1,0:T(8,128)(2,1)}, bf16[512,512]{1,0:T(8,128)(2,1)S(1)}, u32[]{:S(2)}, u32[]{:S(2)}) %collective-permute-start.3) | collective-permute-done | bytes 524320 | tf_op jit(solution)/shard_map/ppermute | solution.py:14
  109.6 17.9 %collective-permute-done.4 = bf16[512,512]{1,0:T(8,128)(2,1)S(1)} collective-permute-done((bf16[512,512]{1,0:T(8,128)(2,1)}, bf16[512,512]{1,0:T(8,128)(2,1)S(1)}, u32[]{:S(2)}, u32[]{:S(2)}) %collective-permute-start.4) | collective-permute-done | bytes 524320 | tf_op jit(solution)/shard_map/ppermute | solution.py:14
  133.9 31.9 %collective-permute-done.5 = bf16[512,512]{1,0:T(8,128)(2,1)S(1)} collective-permute-done((bf16[512,512]{1,0:T(8,128)(2,1)}, bf16[512,512]{1,0:T(8,128)(2,1)S(1)}, u32[]{:S(2)}, u32[]{:S(2)}) %collective-permute-start.5) | collective-permute-done | bytes 524320 | tf_op jit(solution)/shard_map/ppermute | solution.py:14
  165.8 11.2 %collective-permute-done.6 = bf16[512,512]{1,0:T(8,128)(2,1)S(1)} collective-permute-done((bf16[512,512]{1,0:T(8,128)(2,1)}, bf16[512,512]{1,0:T(8,128)(2,1)S(1)}, u32[]{:S(2)}, u32[]{:S(2)}) %collective-permute-start.6) | collective-permute-done | bytes 524320 | tf_op jit(solution)/shard_map/ppermute | solution.py:14
  182.6 11.6 %collective-permute-done.7 = bf16[512,512]{1,0:T(8,128)(2,1)S(1)} collective-permute-done((bf16[512,512]{1,0:T(8,128)(2,1)}, bf16[512,512]{1,0:T(8,128)(2,1)S(1)}, u32[]{:S(2)}, u32[]{:S(2)}) %collective-permute-start.7) | collective-permute-done | bytes 524320 | tf_op jit(solution)/shard_map/ppermute | solution.py:14
  194.2 11.2 %collective-permute-done.8 = bf16[512,512]{1,0:T(8,128)(2,1)S(1)} collective-permute-done((bf16[512,512]{1,0:T(8,128)(2,1)}, bf16[512,512]{1,0:T(8,128)(2,1)S(1)}, u32[]{:S(2)}, u32[]{:S(2)}) %collective-permute-start.8) | collective-permute-done | bytes 524320 | tf_op jit(solution)/shard_map/ppermute | solution.py:14
  210.8 12.3 %collective-permute-start.9 = (bf16[512,512]{1,0:T(8,128)(2,1)}, bf16[512,512]{1,0:T(8,128)(2,1)}, u32[]{:S(2)}, u32[]{:S(2)}) collective-permute-start(bf16[512,512]{1,0:T(8,128)(2,1)} %get-tuple-element.279), channel_id=1, source_target_pairs={{0,8},{4,12},{8,0},{12,4},{16,24},{20,28},{24,16},{28,20},{32,40},... | collective-permute-start | bytes 1572872 | tf_op jit(solution)/shard_map/ppermute | solution.py:14
  223.3 12.5 %collective-permute-done.9 = bf16[512,512]{1,0:T(8,128)(2,1)} collective-permute-done((bf16[512,512]{1,0:T(8,128)(2,1)}, bf16[512,512]{1,0:T(8,128)(2,1)}, u32[]{:S(2)}, u32[]{:S(2)}) %collective-permute-start.9) | collective-permute-done | bytes 524320 | tf_op jit(solution)/shard_map/ppermute | solution.py:14
  241.1 122.0 %while.18 = (s32[]{:T(128)}, f32[512,2,256]{2,1,0:T(2,128)S(1)}, f32[512,2,256]{2,1,0:T(2,128)S(1)}, f32[16,256]{1,0:T(8,128)}, f32[16,256]{1,0:T(8,128)}, /*index=5*/s32[512]{0:T(512)S(1)}, s32[]{:T(128)}, s32[]{:T(128)}) while((s32[]{:T(128)}, f32[512,2,256]{2,1,0:T(2,128)S(1)}, ...), condition=%wide.region_2.3_spmd.clone.clone.clone, body=%wide.region_1.2_spmd.clone.clone.clone.sunk | while | flops 4479235 | bytes 4234339 | solution.py:112
  416.0 13.1 %collective-permute-done.14 = f32[512,512]{1,0:T(8,128)S(1)} collective-permute-done((f32[512,512]{1,0:T(8,128)S(1)}, f32[512,512]{1,0:T(8,128)S(1)}, u32[]{:S(2)}, u32[]{:S(2)}) %collective-permute-start.14) | collective-permute-done | bytes 1048608 | tf_op jit(solution)/shard_map/ppermute | solution.py:14
  430.1 21.6 %collective-permute-done.13 = f32[512,512]{1,0:T(8,128)} collective-permute-done((f32[512,512]{1,0:T(8,128)}, f32[512,512]{1,0:T(8,128)}, u32[]{:S(2)}, u32[]{:S(2)}) %collective-permute-start.13) | collective-permute-done | bytes 1048608 | tf_op jit(solution)/shard_map/ppermute | solution.py:14
  457.6 19.3 %collective-permute-done.15 = f32[512,512]{1,0:T(8,128)} collective-permute-done((f32[512,512]{1,0:T(8,128)S(1)}, f32[512,512]{1,0:T(8,128)}, u32[]{:S(2)}, u32[]{:S(2)}) %collective-permute-start.15) | collective-permute-done | bytes 1048608 | tf_op jit(solution)/shard_map/ppermute | solution.py:14
  476.9 22.5 %collective-permute-done.16 = f32[512,512]{1,0:T(8,128)} collective-permute-done((f32[512,512]{1,0:T(8,128)S(1)}, f32[512,512]{1,0:T(8,128)}, u32[]{:S(2)}, u32[]{:S(2)}) %collective-permute-start.16) | collective-permute-done | bytes 1048608 | tf_op jit(solution)/shard_map/ppermute | solution.py:14
  503.6 18.4 %collective-permute-done.17 = f32[512,512]{1,0:T(8,128)} collective-permute-done((f32[512,512]{1,0:T(8,128)S(1)}, f32[512,512]{1,0:T(8,128)}, u32[]{:S(2)}, u32[]{:S(2)}) %collective-permute-start.17) | collective-permute-done | bytes 1048608 | tf_op jit(solution)/shard_map/ppermute | solution.py:14
  522.0 22.5 %collective-permute-done.18 = f32[512,512]{1,0:T(8,128)} collective-permute-done((f32[512,512]{1,0:T(8,128)S(1)}, f32[512,512]{1,0:T(8,128)}, u32[]{:S(2)}, u32[]{:S(2)}) %collective-permute-start.18) | collective-permute-done | bytes 1048608 | tf_op jit(solution)/shard_map/ppermute | solution.py:14
  550.3 67.4 %collective-permute-done.19 = f32[512,512]{1,0:T(8,128)S(1)} collective-permute-done((f32[512,512]{1,0:T(8,128)}, f32[512,512]{1,0:T(8,128)S(1)}, u32[]{:S(2)}, u32[]{:S(2)}) %collective-permute-start.19) | collective-permute-done | bytes 1048608 | tf_op jit(solution)/shard_map/ppermute | solution.py:14
  618.7 21.6 %collective-permute-done.20 = f32[512,512]{1,0:T(8,128)} collective-permute-done((f32[512,512]{1,0:T(8,128)}, f32[512,512]{1,0:T(8,128)}, u32[]{:S(2)}, u32[]{:S(2)}) %collective-permute-start.20) | collective-permute-done | bytes 1048608 | tf_op jit(solution)/shard_map/ppermute | solution.py:14
  648.5 68.1 %collective-permute-done.21 = f32[512,512]{1,0:T(8,128)} collective-permute-done((f32[512,512]{1,0:T(8,128)S(1)}, f32[512,512]{1,0:T(8,128)}, u32[]{:S(2)}, u32[]{:S(2)}) %collective-permute-start.21) | collective-permute-done | bytes 1048608 | tf_op jit(solution)/shard_map/ppermute | solution.py:14
  716.6 22.5 %collective-permute-done.22 = f32[512,512]{1,0:T(8,128)} collective-permute-done((f32[512,512]{1,0:T(8,128)S(1)}, f32[512,512]{1,0:T(8,128)}, u32[]{:S(2)}, u32[]{:S(2)}) %collective-permute-start.22) | collective-permute-done | bytes 1048608 | tf_op jit(solution)/shard_map/ppermute | solution.py:14
  744.0 22.3 %collective-permute-done.23 = f32[512,512]{1,0:T(8,128)} collective-permute-done((f32[512,512]{1,0:T(8,128)}, f32[512,512]{1,0:T(8,128)}, u32[]{:S(2)}, u32[]{:S(2)}) %collective-permute-start.23) | collective-permute-done | bytes 1048608 | tf_op jit(solution)/shard_map/ppermute | solution.py:14
  766.2 22.4 %collective-permute-done.24 = f32[512,512]{1,0:T(8,128)S(1)} collective-permute-done((f32[512,512]{1,0:T(8,128)S(1)}, f32[512,512]{1,0:T(8,128)S(1)}, u32[]{:S(2)}, u32[]{:S(2)}) %collective-permute-start.24) | collective-permute-done | bytes 1048608 | tf_op jit(solution)/shard_map/ppermute | solution.py:14
  793.8 41.1 %reduce-scatter.2.cloned.1.call-done = f32[512,256]{1,0:T(8,128)} async-done(((f32[512,1024]{1,0:T(8,128)}), f32[512,256]{1,0:T(8,128)}) %reduce-scatter.2.cloned.1.call-update) | async-done | bytes 524304 | tf_op jit(solution)/shard_map/reduce_scatter | solution.py:172
  (178 shorter events, 271.9 us)
Async XLA Ops:
  6.5 30.3 %all-gather.2.cloned.1.call-start = ((), (), s32[]{:S(2)}) async-start(), calls=%async_computation.1 | async-start | bytes 1310720 | tf_op jit(solution)/shard_map/all_gather | solution.py:150
  7.3 827.6 %reduce-scatter.2.cloned.1.call-start = ((), (), s32[]{:S(2)}) async-start(), calls=%async_computation.2 | async-start | bytes 2621440 | tf_op jit(solution)/shard_map/reduce_scatter | solution.py:172
  46.3 16.7 %collective-permute-start.1 = (bf16[512,512]{1,0:T(8,128)(2,1)S(1)}, bf16[512,512]{1,0:T(8,128)(2,1)S(1)}, u32[]{:S(2)}, u32[]{:S(2)}) collective-permute-start(bf16[512,512]{1,0:T(8,128)(2,1)S(1)} %fusion.46), channel_id=1, source_target_pairs={{0,128},{4,132},{8,136},{12,140},{16,144},{20,148},{24,152},{28,15... | collective-permute-start | bytes 1572872 | tf_op jit(solution)/shard_map/ppermute | solution.py:14
  52.7 21.6 %collective-permute-start.2 = (bf16[512,512]{1,0:T(8,128)(2,1)}, bf16[512,512]{1,0:T(8,128)(2,1)}, u32[]{:S(2)}, u32[]{:S(2)}) collective-permute-start(bf16[512,512]{1,0:T(8,128)(2,1)} %pad_convert_fusion), channel_id=1, source_target_pairs={{0,128},{4,132},{8,136},{12,140},{16,144},{20,148},{24,152},{28,15... | collective-permute-start | bytes 1572872 | tf_op jit(solution)/shard_map/ppermute | solution.py:14
  77.2 32.4 %collective-permute-start.3 = (bf16[512,512]{1,0:T(8,128)(2,1)}, bf16[512,512]{1,0:T(8,128)(2,1)S(1)}, u32[]{:S(2)}, u32[]{:S(2)}) collective-permute-start(bf16[512,512]{1,0:T(8,128)(2,1)} %get-tuple-element.285), channel_id=1, source_target_pairs={{0,64},{4,68},{8,72},{12,76},{16,80},{20,84},{24,88},{28,92},{32,9... | collective-permute-start | bytes 1572872 | tf_op jit(solution)/shard_map/ppermute | solution.py:14
  81.9 45.5 %collective-permute-start.4 = (bf16[512,512]{1,0:T(8,128)(2,1)}, bf16[512,512]{1,0:T(8,128)(2,1)S(1)}, u32[]{:S(2)}, u32[]{:S(2)}) collective-permute-start(bf16[512,512]{1,0:T(8,128)(2,1)} %get-tuple-element.248), channel_id=1, source_target_pairs={{0,64},{4,68},{8,72},{12,76},{16,80},{20,84},{24,88},{28,92},{32,9... | collective-permute-start | bytes 1572872 | tf_op jit(solution)/shard_map/ppermute | solution.py:14
  131.4 34.4 %collective-permute-start.5 = (bf16[512,512]{1,0:T(8,128)(2,1)}, bf16[512,512]{1,0:T(8,128)(2,1)S(1)}, u32[]{:S(2)}, u32[]{:S(2)}) collective-permute-start(bf16[512,512]{1,0:T(8,128)(2,1)} %get-tuple-element.283), channel_id=1, source_target_pairs={{0,32},{4,36},{8,40},{12,44},{16,48},{20,52},{24,56},{28,60},{32,0... | collective-permute-start | bytes 1572872 | tf_op jit(solution)/shard_map/ppermute | solution.py:14
  131.4 45.6 %collective-permute-start.6 = (bf16[512,512]{1,0:T(8,128)(2,1)}, bf16[512,512]{1,0:T(8,128)(2,1)S(1)}, u32[]{:S(2)}, u32[]{:S(2)}) collective-permute-start(bf16[512,512]{1,0:T(8,128)(2,1)} %get-tuple-element.244), channel_id=1, source_target_pairs={{0,32},{4,36},{8,40},{12,44},{16,48},{20,52},{24,56},{28,60},{32,0... | collective-permute-start | bytes 1572872 | tf_op jit(solution)/shard_map/ppermute | solution.py:14
  181.0 24.4 %collective-permute-start.8 = (bf16[512,512]{1,0:T(8,128)(2,1)}, bf16[512,512]{1,0:T(8,128)(2,1)S(1)}, u32[]{:S(2)}, u32[]{:S(2)}) collective-permute-start(bf16[512,512]{1,0:T(8,128)(2,1)} %get-tuple-element.240), channel_id=1, source_target_pairs={{0,16},{4,20},{8,24},{12,28},{16,0},{20,4},{24,8},{28,12},{32,48},... | collective-permute-start | bytes 1572872 | tf_op jit(solution)/shard_map/ppermute | solution.py:14
  210.8 25.0 %collective-permute-start.9 = (bf16[512,512]{1,0:T(8,128)(2,1)}, bf16[512,512]{1,0:T(8,128)(2,1)}, u32[]{:S(2)}, u32[]{:S(2)}) collective-permute-start(bf16[512,512]{1,0:T(8,128)(2,1)} %get-tuple-element.279), channel_id=1, source_target_pairs={{0,8},{4,12},{8,0},{12,4},{16,24},{20,28},{24,16},{28,20},{32,40},... | collective-permute-start | bytes 1572872 | tf_op jit(solution)/shard_map/ppermute | solution.py:14
  239.6 123.7 %collective-permute-start.11 = (bf16[512,512]{1,0:T(8,128)(2,1)}, bf16[512,512]{1,0:T(8,128)(2,1)}, u32[]{:S(2)}, u32[]{:S(2)}) collective-permute-start(bf16[512,512]{1,0:T(8,128)(2,1)} %get-tuple-element.277), channel_id=1, source_target_pairs={{0,4},{4,0},{8,12},{12,8},{16,20},{20,16},{24,28},{28,24},{32,36},... | collective-permute-start | bytes 1572872 | tf_op jit(solution)/shard_map/ppermute | solution.py:14
  239.7 123.6 %collective-permute-start.12 = (bf16[512,512]{1,0:T(8,128)(2,1)}, bf16[512,512]{1,0:T(8,128)(2,1)}, u32[]{:S(2)}, u32[]{:S(2)}) collective-permute-start(bf16[512,512]{1,0:T(8,128)(2,1)} %get-tuple-element.232), channel_id=1, source_target_pairs={{0,4},{4,0},{8,12},{12,8},{16,20},{20,16},{24,28},{28,24},{32,36},... | collective-permute-start | bytes 1572872 | tf_op jit(solution)/shard_map/ppermute | solution.py:14
  407.5 21.7 %collective-permute-start.14 = (f32[512,512]{1,0:T(8,128)S(1)}, f32[512,512]{1,0:T(8,128)S(1)}, u32[]{:S(2)}, u32[]{:S(2)}) collective-permute-start(f32[512,512]{1,0:T(8,128)S(1)} %convolution_add_fusion), channel_id=1, source_target_pairs={{0,4},{4,0},{8,12},{12,8},{16,20},{20,16},{24,28},{28,24},{32,36},... | collective-permute-start | bytes 3145736 | tf_op jit(solution)/shard_map/ppermute | solution.py:14
  414.4 37.3 %collective-permute-start.13 = (f32[512,512]{1,0:T(8,128)}, f32[512,512]{1,0:T(8,128)}, u32[]{:S(2)}, u32[]{:S(2)}) collective-permute-start(f32[512,512]{1,0:T(8,128)} %convolution_subtract_fusion), channel_id=1, source_target_pairs={{0,4},{4,0},{8,12},{12,8},{16,20},{20,16},{24,28},{28,24},{32,36},... | collective-permute-start | bytes 3145736 | tf_op jit(solution)/shard_map/ppermute | solution.py:14
  454.5 22.4 %collective-permute-start.15 = (f32[512,512]{1,0:T(8,128)S(1)}, f32[512,512]{1,0:T(8,128)}, u32[]{:S(2)}, u32[]{:S(2)}) collective-permute-start(f32[512,512]{1,0:T(8,128)S(1)} %get-tuple-element.271), channel_id=1, source_target_pairs={{0,8},{4,12},{8,0},{12,4},{16,24},{20,28},{24,16},{28,20},{32,40},... | collective-permute-start | bytes 3145736 | tf_op jit(solution)/shard_map/ppermute | solution.py:14
  455.4 43.9 %collective-permute-start.16 = (f32[512,512]{1,0:T(8,128)S(1)}, f32[512,512]{1,0:T(8,128)}, u32[]{:S(2)}, u32[]{:S(2)}) collective-permute-start(f32[512,512]{1,0:T(8,128)S(1)} %get-tuple-element.272), channel_id=1, source_target_pairs={{0,8},{4,12},{8,0},{12,4},{16,24},{20,28},{24,16},{28,20},{32,40},... | collective-permute-start | bytes 3145736 | tf_op jit(solution)/shard_map/ppermute | solution.py:14
  502.1 19.9 %collective-permute-start.17 = (f32[512,512]{1,0:T(8,128)S(1)}, f32[512,512]{1,0:T(8,128)}, u32[]{:S(2)}, u32[]{:S(2)}) collective-permute-start(f32[512,512]{1,0:T(8,128)S(1)} %get-tuple-element.269), channel_id=1, source_target_pairs={{0,16},{4,20},{8,24},{12,28},{16,0},{20,4},{24,8},{28,12},{32,48},... | collective-permute-start | bytes 3145736 | tf_op jit(solution)/shard_map/ppermute | solution.py:14
  503.4 41.0 %collective-permute-start.18 = (f32[512,512]{1,0:T(8,128)S(1)}, f32[512,512]{1,0:T(8,128)}, u32[]{:S(2)}, u32[]{:S(2)}) collective-permute-start(f32[512,512]{1,0:T(8,128)S(1)} %get-tuple-element.270), channel_id=1, source_target_pairs={{0,16},{4,20},{8,24},{12,28},{16,0},{20,4},{24,8},{28,12},{32,48},... | collective-permute-start | bytes 3145736 | tf_op jit(solution)/shard_map/ppermute | solution.py:14
  547.9 69.8 %collective-permute-start.19 = (f32[512,512]{1,0:T(8,128)}, f32[512,512]{1,0:T(8,128)S(1)}, u32[]{:S(2)}, u32[]{:S(2)}) collective-permute-start(f32[512,512]{1,0:T(8,128)} %get-tuple-element.267), channel_id=1, source_target_pairs={{0,32},{4,36},{8,40},{12,44},{16,48},{20,52},{24,56},{28,60},{32,0... | collective-permute-start | bytes 3145736 | tf_op jit(solution)/shard_map/ppermute | solution.py:14
  547.9 92.3 %collective-permute-start.20 = (f32[512,512]{1,0:T(8,128)}, f32[512,512]{1,0:T(8,128)}, u32[]{:S(2)}, u32[]{:S(2)}) collective-permute-start(f32[512,512]{1,0:T(8,128)} %get-tuple-element.268), channel_id=1, source_target_pairs={{0,32},{4,36},{8,40},{12,44},{16,48},{20,52},{24,56},{28,60},{32,0... | collective-permute-start | bytes 3145736 | tf_op jit(solution)/shard_map/ppermute | solution.py:14
  643.0 73.6 %collective-permute-start.21 = (f32[512,512]{1,0:T(8,128)S(1)}, f32[512,512]{1,0:T(8,128)}, u32[]{:S(2)}, u32[]{:S(2)}) collective-permute-start(f32[512,512]{1,0:T(8,128)S(1)} %get-tuple-element.265), channel_id=1, source_target_pairs={{0,64},{4,68},{8,72},{12,76},{16,80},{20,84},{24,88},{28,92},{32,9... | collective-permute-start | bytes 3145736 | tf_op jit(solution)/shard_map/ppermute | solution.py:14
  646.8 92.3 %collective-permute-start.22 = (f32[512,512]{1,0:T(8,128)S(1)}, f32[512,512]{1,0:T(8,128)}, u32[]{:S(2)}, u32[]{:S(2)}) collective-permute-start(f32[512,512]{1,0:T(8,128)S(1)} %get-tuple-element.266), channel_id=1, source_target_pairs={{0,64},{4,68},{8,72},{12,76},{16,80},{20,84},{24,88},{28,92},{32,9... | collective-permute-start | bytes 3145736 | tf_op jit(solution)/shard_map/ppermute | solution.py:14
  742.5 23.7 %collective-permute-start.23 = (f32[512,512]{1,0:T(8,128)}, f32[512,512]{1,0:T(8,128)}, u32[]{:S(2)}, u32[]{:S(2)}) collective-permute-start(f32[512,512]{1,0:T(8,128)} %get-tuple-element.263), channel_id=1, source_target_pairs={{0,128},{4,132},{8,136},{12,140},{16,144},{20,148},{24,152},{28,15... | collective-permute-start | bytes 3145736 | tf_op jit(solution)/shard_map/ppermute | solution.py:14
  743.1 45.5 %collective-permute-start.24 = (f32[512,512]{1,0:T(8,128)S(1)}, f32[512,512]{1,0:T(8,128)S(1)}, u32[]{:S(2)}, u32[]{:S(2)}) collective-permute-start(f32[512,512]{1,0:T(8,128)S(1)} %get-tuple-element.264), channel_id=1, source_target_pairs={{0,128},{4,132},{8,136},{12,140},{16,144},{20,148},{24,152},{28,15... | collective-permute-start | bytes 3145736 | tf_op jit(solution)/shard_map/ppermute | solution.py:14
  (21 other events, 1104.7 us)
Sparse Core Ops, SparseCore 0:
  9.2 27.6 all-gather.1
  793.9 40.9 reduce-scatter.1
where the time goes:
time: 854 us; the launch traced here: 844 us
  waiting for transfers between devices  555 us (65%)
  other arithmetic  161 us (19%)
  matrix products  53.2 us (6%)
  starting transfers between devices  49.4 us (6%)
  between operations  15.1 us (2%)
  local copies, waits for them, and re-layouts  9.46 us (1%)
    ppermute x24, waiting for transfers between devices, swapped(): lax.ppermute(array, axis, [(i, i ^ 1 << distance) for i in range(lax.axis...  485 us
    sub x16, other arithmetic, add_mode(): sum_imag - weight_term * imag_den  78.9 us
    ppermute x24, starting transfers between devices, swapped(): lax.ppermute(array, axis, [(i, i ^ 1 << distance) for i in range(lax.axis...  46.2 us
    reduce_scatter x1, waiting for transfers between devices, body(): lax.psum_scatter(partial_sums, 'ch', scatter_dimension=1, tiled=True)  41.1 us
    mul x16, other arithmetic, add_mode(): parity_sign * jnp.exp(-rate_row * seq_len)  30.6 us
    all_gather x1, waiting for transfers between devices, body(): whole = lax.all_gather(tokens, 'ch', axis=1, tiled=True)  27.7 us
    dot_general x4, matrix products, left_dot(): lax.dot_general(left, right, (((0,), (0,)), ((), ())), precision=HIGHEST,...  24.3 us
    dot_general x4, matrix products, mat_dot(): jnp.dot(left, right, precision=HIGHEST, preferred_element_type=jnp.float32)  23.6 us
  transfers between devices with their start and end apart: 27, of which 24 were waited for; matrix products, arithmetic and copies ran while one was open for 16% of the time, Pallas kernels for 0%

commit v1 on v0

v1 whole, which is shorter than its diff:
```python
import functools

import jax
import jax.numpy as jnp
from jax import lax
from jax.experimental import pallas as pl
from jax.experimental.pallas import tpu as pltpu
from jax.sharding import PartitionSpec as P

EPSILON = 1e-06
F32 = jnp.float32
BF16 = jnp.bfloat16
LANES = 128
SUBS = 8
HALO = 16
VMEM_LIMIT = 48 * 1024 * 1024

SCAN_MASKS = (1, 3, 4, 8, 24, 32)


def ch_swap(array, mask):
    return lax.ppermute(array, "ch", [(i, i ^ mask) for i in range(lax.axis_size("ch"))])


def seq_swap(array, mask):
    return lax.ppermute(array, "seq", [(i, i ^ mask) for i in range(lax.axis_size("seq"))])


def vmem_specs(count):
    return [pl.BlockSpec(memory_space=pltpu.VMEM)] * count


def row(ref, index, lanes):
    return jnp.broadcast_to(ref[pl.ds(index, 1), lanes], (SUBS, LANES))


def front_kernel(
    own, far, side, side_far, halo, gain, w_in, taps, rates, residues, skip,
    queries, local, carry, ends, projected,
):
    me = lax.axis_index("ch")
    rows = own.shape[0]
    width = own.shape[1]
    span = rows // SUBS
    modes = rates.shape[0]
    blocks = [jnp.concatenate([halo[i], block[...]], axis=0) for i, block in enumerate((own, side, far, side_far))]
    square = jnp.zeros((rows + HALO, LANES), F32)
    for block in blocks:
        for lane in range(0, width, LANES):
            piece = block[:, lane : lane + LANES].astype(F32)
            square = square + piece * piece
    scale = lax.rsqrt(jnp.sum(square, axis=1, keepdims=True) * (1.0 / (4 * width)) + EPSILON)
    total = jnp.zeros((rows + HALO, w_in.shape[1]), F32)
    for order, block in enumerate(blocks):
        part = jnp.bitwise_xor(me, order)
        normed = (block.astype(F32) * scale * gain[pl.ds(part, 1), :]).astype(BF16)
        start = pl.multiple_of(part * width, width)
        total = total + jnp.dot(normed, w_in[pl.ds(start, width), :], preferred_element_type=F32)
    total = total.astype(BF16).astype(F32)
    for tile in range(total.shape[1] // LANES):
        projected[tile] = total[:, tile * LANES : (tile + 1) * LANES]

    sub = lax.broadcasted_iota(jnp.int32, (SUBS, LANES), 0)
    for lane in range(0, width, LANES):
        lanes = pl.ds(lane, LANES)
        rate = [row(rates, m, lanes) for m in range(modes)]
        decay = [jnp.exp(-r) for r in rate]
        weight = [row(residues, m, lanes) * jnp.sqrt(rate[m]) for m in range(modes)]
        tap = [[row(taps, 3 * s + g, lanes) for s in range(3)] for g in range(3)]
        skip_row = row(skip, 0, lanes)

        def read(start, group):
            return projected[(group * width + lane) // LANES, pl.ds(start, SUBS, stride=span), :]

        def step(index, held):
            before, state = held
            now = [read(HALO + index, g) for g in range(3)]
            filtered = [
                tap[g][0] * now[g] + tap[g][1] * before[0][g] + tap[g][2] * before[1][g] for g in range(3)
            ]
            gated = filtered[1] * filtered[2]
            state = [decay[m] * state[m] + gated for m in range(modes)]
            terms = [weight[m] * state[m] for m in range(modes)] + [skip_row * gated]
            while len(terms) > 1:
                terms = [sum(terms[i : i + 2][1:], terms[i]) for i in range(0, len(terms), 2)]
            at = pl.ds(pl.multiple_of(index * SUBS, SUBS), SUBS)
            queries[at, lanes] = filtered[0]
            local[at, lanes] = terms[0]
            return ((now, before[0]), state)

        first = ([read(HALO - 1, g) for g in range(3)], [read(HALO - 2, g) for g in range(3)])
        zeros = [jnp.zeros((SUBS, LANES), F32)] * modes
        _, state = lax.fori_loop(0, span, step, (first, zeros), unroll=4)
        for m in range(modes):
            upto = state[m]
            for reach in (1, 2, 4):
                moved = pltpu.roll(upto, reach, 0) * jnp.exp(rate[m] * (-float(span * reach)))
                upto = upto + jnp.where(sub >= reach, moved, 0.0)
            carry[m, :, lanes] = jnp.where(sub >= 1, pltpu.roll(upto, 1, 0), 0.0)
            ends[pl.ds(m, 1), lanes] = upto[SUBS - 1 :, :]


def back_kernel(queries, local, carry, entry, rates, residues, w_out, kept, sent, mixed):
    me = lax.axis_index("ch")
    rows, width = queries.shape
    span = rows // SUBS
    modes = rates.shape[0]
    sub = lax.broadcasted_iota(jnp.int32, (SUBS, LANES), 0).astype(F32)
    for lane in range(0, width, LANES):
        lanes = pl.ds(lane, LANES)
        rate = [row(rates, m, lanes) for m in range(modes)]
        decay = [jnp.exp(-r) for r in rate]
        state = []
        for m in range(modes):
            weight = row(residues, m, lanes) * jnp.sqrt(rate[m]) * decay[m]
            entering = carry[m, :, lanes] + jnp.exp(rate[m] * sub * (-float(span))) * row(entry, m, lanes)
            state.append(weight * entering)

        def step(index, held):
            at = pl.ds(pl.multiple_of(index * SUBS, SUBS), SUBS)
            terms = list(held) + [local[at, lanes]]
            while len(terms) > 1:
                terms = [sum(terms[i : i + 2][1:], terms[i]) for i in range(0, len(terms), 2)]
            mixed[lane // LANES, pl.ds(index, SUBS, stride=span), :] = queries[at, lanes] * terms[0]
            return [decay[m] * held[m] for m in range(modes)]

        lax.fori_loop(0, span, step, state, unroll=4)
    mixed_in = jnp.concatenate([mixed[tile] for tile in range(width // LANES)], axis=1).astype(BF16)
    for order in range(4):
        start = pl.multiple_of(jnp.bitwise_xor(me, order) * width, width)
        share = jnp.dot(mixed_in, w_out[:, pl.ds(start, width)], preferred_element_type=F32)
        if order % 2 == 0:
            kept[order // 2] = share
        else:
            sent[order // 2] = share.astype(BF16)


def halo_tokens(tokens):
    blocks, chs = lax.axis_size("seq"), lax.axis_size("ch")
    tail = tokens[tokens.shape[0] - HALO :]
    pair = jnp.stack([tail, ch_swap(tail, 1)])
    moves = [
        (chs * block + c, chs * (block + 1) + (c if c % 2 == 0 else c ^ 2))
        for block in range(blocks - 1)
        for c in range(chs)
    ]
    mine = lax.ppermute(pair, ("seq", "ch"), moves)
    other = ch_swap(mine, 1)
    even = lax.axis_index("ch") % 2 == 0
    low = jnp.where(even, mine, other[::-1])
    high = jnp.where(even, other[::-1], mine)
    return jnp.concatenate([low, high], axis=0)


def scan_blocks(ends, rates, rows):
    block = lax.axis_index("seq")
    rounds = lax.axis_size("seq").bit_length() - 1
    total = ends
    entry = jnp.zeros_like(ends)
    for level in range(rounds):
        other = seq_swap(total, SCAN_MASKS[level])
        upper = jnp.bitwise_and(jnp.right_shift(block, level), 1) == 1
        ahead = jnp.remainder(block, 1 << level).astype(F32) * float(rows)
        across = jnp.exp(-rates * float(rows << level))
        entry = jnp.where(upper, entry + jnp.exp(-rates * ahead) * other, entry)
        total = jnp.where(upper, across * other + total, across * total + other)
    return entry


def body(tokens, norm_gain, w_in, short_filter, rates, residues, skip_gain, w_out):
    rows, width = tokens.shape
    slab = w_in.shape[0]
    channels = w_in.shape[2]
    modes = rates.shape[0]
    taps = short_filter.reshape(-1, channels)
    far = ch_swap(tokens, 2)
    halo = halo_tokens(tokens)
    side = ch_swap(tokens, 1)
    side_far = ch_swap(far, 1)
    queries, local, carry, ends = pl.pallas_call(
        front_kernel,
        out_shape=(
            jax.ShapeDtypeStruct((rows, channels), F32),
            jax.ShapeDtypeStruct((rows, channels), F32),
            jax.ShapeDtypeStruct((modes, SUBS, channels), F32),
            jax.ShapeDtypeStruct((modes, channels), F32),
        ),
        in_specs=vmem_specs(11),
        out_specs=tuple(vmem_specs(4)),
        scratch_shapes=[pltpu.VMEM((3 * channels // LANES, rows + HALO, LANES), F32)],
        compiler_params=pltpu.CompilerParams(vmem_limit_bytes=VMEM_LIMIT),
        name="front",
    )(
        tokens, far, side, side_far, halo, norm_gain.reshape(-1, width), w_in.reshape(slab, 3 * channels),
        taps, rates, residues, skip_gain.reshape(1, channels),
    )
    entry = scan_blocks(ends, rates, rows)
    kept, sent = pl.pallas_call(
        back_kernel,
        out_shape=(
            jax.ShapeDtypeStruct((2, rows, width), F32),
            jax.ShapeDtypeStruct((2, rows, width), BF16),
        ),
        in_specs=vmem_specs(7),
        out_specs=tuple(vmem_specs(2)),
        scratch_shapes=[pltpu.VMEM((channels // LANES, rows, LANES), F32)],
        compiler_params=pltpu.CompilerParams(vmem_limit_bytes=VMEM_LIMIT),
        name="back",
    )(queries, local, carry, entry, rates, residues, w_out)
    both = kept + ch_swap(sent, 1).astype(F32)
    away = ch_swap(both[1].astype(BF16), 2)
    return (both[0] + away.astype(F32)).astype(BF16)


def solution(mesh):
    return jax.shard_map(
        body,
        mesh=mesh,
        in_specs=(
            P("seq", "ch"),
            P(),
            P(None, None, "ch"),
            P(None, None, "ch"),
            P(None, "ch"),
            P(None, "ch"),
            P("ch"),
            P("ch", None),
        ),
        out_specs=P("seq", "ch"),
        check_vma=False,
    )
```

time: 854 us -> 77.3 us (0.09); the launches traced: 844 us -> 76.5 us
  waiting for transfers between devices: 555 us -> 17.8 us
  other arithmetic: 161 us -> 1.68 us
  matrix products: 53.2 us -> 0 us
  between operations: 15.1 us -> 0.15 us
  starting transfers between devices: 49.4 us -> 38 us
    ppermute x25 -> x14, waiting for transfers between devices: 486 us -> 17.8 us  [the longest x7 9.89 us: ch_swap(): lax.ppermute(array, 'ch', [(i, i ^ mask) for i in range(lax.axis_size('ch...]
    sub x16 -> x0, other arithmetic: 78.9 us -> none  [add_mode(): sum_imag - weight_term * imag_den]
    dot_general x10 -> x0, matrix products: 53.2 us -> none  [the longest x4 24.3 us: left_dot(): lax.dot_general(left, right, (((0,), (0,)), ((), ())), precision=HIGHEST,...]
    mul x51 -> x0, other arithmetic: 42.7 us -> none  [the longest x16 30.6 us: add_mode(): parity_sign * jnp.exp(-rate_row * seq_len)]
    reduce_scatter x1 -> x0, waiting for transfers between devices: 41.1 us -> none  [body(): lax.psum_scatter(partial_sums, 'ch', scatter_dimension=1, tiled=True)]
    all_gather x1 -> x0, waiting for transfers between devices: 27.7 us -> none  [body(): whole = lax.all_gather(tokens, 'ch', axis=1, tiled=True)]
    add x8 -> x1, other arithmetic: 17.6 us -> 0.1 us  [body(): both = kept + ch_swap(sent, 1).astype(F32)]
    convert_element_type x8 -> x1, other arithmetic: 18.2 us -> 0.76 us  [body(): return (both[0] + away.astype(F32)).astype(BF16)]
  transfers between devices with their start and end apart: 27 -> 14, of which waited for: 24 -> 10; matrix products, arithmetic and copies ran while one was open for 16% -> 8% of each run, Pallas kernels for 0% -> 0%
where the time goes in v1:
time: 77.3 us; the launch traced here: 76.5 us
  starting transfers between devices  38 us (49%)
  waiting for transfers between devices  17.8 us (23%)
  local copies, waits for them, and re-layouts  13.1 us (17%)
  Pallas kernels  5.76 us (7%)
  other arithmetic  1.68 us (2%)
    ppermute x6, starting transfers between devices, seq_swap(): lax.ppermute(array, 'seq', [(i, i ^ mask) for i in range(lax.axis_size('s...  20.2 us
    ppermute x7, starting transfers between devices, ch_swap(): lax.ppermute(array, 'ch', [(i, i ^ mask) for i in range(lax.axis_size('ch...  14.7 us
    ppermute x7, waiting for transfers between devices, ch_swap(): lax.ppermute(array, 'ch', [(i, i ^ mask) for i in range(lax.axis_size('ch...  9.89 us
    unnamed x29, local copies, waits for them, and re-layouts  9.42 us
    ppermute x6, waiting for transfers between devices, seq_swap(): lax.ppermute(array, 'seq', [(i, i ^ mask) for i in range(lax.axis_size('s...  6.98 us
    pallas_call x1, Pallas kernels, body(): pl.pallas_call(front_kernel, out_shape=(jax.ShapeDtypeStruct((rows, chann...  4.49 us
    ppermute x1, starting transfers between devices, halo_tokens(): mine = lax.ppermute(pair, ('seq', 'ch'), moves)  3.13 us
    reshape x1, local copies, waits for them, and re-layouts, body(): w_in.reshape(slab, 3 * channels)  1.76 us
  transfers between devices with their start and end apart: 14, of which 10 were waited for; matrix products, arithmetic and copies ran while one was open for 8% of the time, Pallas kernels for 0%

profile of v1, /device:TPU:1, one launch (start us, length us, event | category | flops | bytes accessed | tf_op | source)
XLA Modules:
  0.0 76.5 jit_solution(15095325886429234233)
XLA Ops:
  0.0 3.6 %collective-permute-start = (bf16[512,256]{1,0:T(8,128)(2,1)}, bf16[512,256]{1,0:T(8,128)(2,1)S(1)}, u32[]{:S(2)}, u32[]{:S(2)}) collective-permute-start(bf16[512,256]{1,0:T(8,128)(2,1)} %own.1), channel_id=1, source_target_pairs={{0,2},{1,3},{2,0},{3,1},{4,6},{5,7},{6,4},{7,5},{8,10},{9,11},{10,... | collective-permute-start | bytes 786440 | tf_op jit(solution)/shard_map/ppermute | solution.py:22
  4.3 1.0 %collective-permute-start.3 = (bf16[16,256]{1,0:T(8,128)(2,1)S(1)}, bf16[16,256]{1,0:T(8,128)(2,1)S(1)}, u32[]{:S(2)}, u32[]{:S(2)}) collective-permute-start(bf16[16,256]{1,0:T(8,128)(2,1)S(1)} %get-tuple-element.18), channel_id=1, source_target_pairs={{0,1},{1,0},{2,3},{3,2},{4,5},{5,4},{6,7},{7,6},{8,9},{9,8},{10,11... | collective-permute-start | bytes 24584 | tf_op jit(solution)/shard_map/ppermute | solution.py:22
  6.1 3.1 %collective-permute-start.4 = (bf16[2,16,256]{2,1,0:T(8,128)(2,1)S(1)}, bf16[2,16,256]{2,1,0:T(8,128)(2,1)S(1)}, u32[]{:S(2)}, u32[]{:S(2)}) collective-permute-start(bf16[2,16,256]{2,1,0:T(8,128)(2,1)S(1)} %pad_maximum_fusion.1), channel_id=1, source_target_pairs={{0,4},{1,7},{2,6},{3,5},{4,8},{5,11},{6,10},{7,9},{8,12},{9,15},{1... | collective-permute-start | bytes 49160 | tf_op jit(solution)/shard_map/ppermute | solution.py:147
  10.1 1.2 %collective-permute-start.5 = (bf16[2,16,256]{2,1,0:T(8,128)(2,1)S(1)}, bf16[2,16,256]{2,1,0:T(8,128)(2,1)S(1)}, u32[]{:S(2)}, u32[]{:S(2)}) collective-permute-start(bf16[2,16,256]{2,1,0:T(8,128)(2,1)S(1)} %collective-permute-done.4), channel_id=1, source_target_pairs={{0,1},{1,0},{2,3},{3,2},{4,5},{5,4},{6,7},{7,6},{8,9},{9,8},{10,11... | collective-permute-start | bytes 49160 | tf_op jit(solution)/shard_map/ppermute | solution.py:22
  11.3 2.6 %copy.10 = bf16[1024,3,256]{0,2,1:T(8,128)(2,1)} copy(bf16[1024,3,256]{2,0,1:T(8,128)(2,1)} %param.10) | data formatting | bytes 3145728 | tf_op args[2]
  14.0 1.8 %copy.11.w_in = bf16[1024,768]{1,0:T(8,128)(2,1)S(1)} copy(bf16[1024,768]{0,1:T(8,128)(2,1)} %bitcast.14) | data formatting | bytes 3145728 | tf_op jit(solution)/shard_map/reshape | solution.py:194
  23.6 4.5 %front.1 = (f32[512,256]{1,0:T(8,128)S(1)}, f32[512,256]{1,0:T(8,128)S(1)}, f32[16,8,256]{2,1,0:T(8,128)S(1)}, f32[16,256]{1,0:T(8,128)}) custom-call(bf16[512,256]{1,0:T(8,128)(2,1)S(1)} %copy-done.2, bf16[512,256]{1,0:T(8,128)(2,1)S(1)} %copy-done.4, bf16[512,256]{1,0:T(8,128)(2,1)S(1)} %copy-done.6, bf16[512,256]{1,0:T(8,128)(2,1)S(1)} %collective-permute-done.2.side_far, ...), custom_call_target="tpu_custom_call" | custom-call | tf_op jit(solution)/shard_map/front/pallas_call | solution.py:180
  28.1 3.0 %collective-permute-start.6 = (f32[16,256]{1,0:T(8,128)}, f32[16,256]{1,0:T(8,128)S(1)}, u32[]{:S(2)}, u32[]{:S(2)}) collective-permute-start(f32[16,256]{1,0:T(8,128)} %get-tuple-element.14), channel_id=1, source_target_pairs={{0,4},{4,0},{8,12},{12,8},{16,20},{20,16},{24,28},{28,24},{32,36},... | collective-permute-start | bytes 49160 | tf_op jit(solution)/shard_map/ppermute | solution.py:26
  31.1 1.3 %collective-permute-done.6 = f32[16,256]{1,0:T(8,128)S(1)} collective-permute-done((f32[16,256]{1,0:T(8,128)}, f32[16,256]{1,0:T(8,128)S(1)}, u32[]{:S(2)}, u32[]{:S(2)}) %collective-permute-start.6) | collective-permute-done | bytes 16416 | tf_op jit(solution)/shard_map/ppermute | solution.py:26
  33.2 3.0 %collective-permute-start.7 = (f32[16,256]{1,0:T(8,128)S(1)}, f32[16,256]{1,0:T(8,128)S(1)}, u32[]{:S(2)}, u32[]{:S(2)}) collective-permute-start(f32[16,256]{1,0:T(8,128)S(1)} %add_select_fusion.9), channel_id=1, source_target_pairs={{0,12},{4,8},{8,4},{12,0},{16,28},{20,24},{24,20},{28,16},{32,44},... | collective-permute-start | bytes 49160 | tf_op jit(solution)/shard_map/ppermute | solution.py:26
  36.2 1.1 %collective-permute-done.7 = f32[16,256]{1,0:T(8,128)S(1)} collective-permute-done((f32[16,256]{1,0:T(8,128)S(1)}, f32[16,256]{1,0:T(8,128)S(1)}, u32[]{:S(2)}, u32[]{:S(2)}) %collective-permute-start.7) | collective-permute-done | bytes 16416 | tf_op jit(solution)/shard_map/ppermute | solution.py:26
  37.3 3.8 %collective-permute-start.8 = (f32[16,256]{1,0:T(8,128)S(1)}, f32[16,256]{1,0:T(8,128)S(1)}, u32[]{:S(2)}, u32[]{:S(2)}) collective-permute-start(f32[16,256]{1,0:T(8,128)S(1)} %add_select_fusion.8), channel_id=1, source_target_pairs={{0,16},{4,20},{8,24},{12,28},{16,0},{20,4},{24,8},{28,12},{32,48},... | collective-permute-start | bytes 49160 | tf_op jit(solution)/shard_map/ppermute | solution.py:26
  41.1 1.1 %collective-permute-done.8 = f32[16,256]{1,0:T(8,128)S(1)} collective-permute-done((f32[16,256]{1,0:T(8,128)S(1)}, f32[16,256]{1,0:T(8,128)S(1)}, u32[]{:S(2)}, u32[]{:S(2)}) %collective-permute-start.8) | collective-permute-done | bytes 16416 | tf_op jit(solution)/shard_map/ppermute | solution.py:26
  42.2 3.1 %collective-permute-start.9 = (f32[16,256]{1,0:T(8,128)S(1)}, f32[16,256]{1,0:T(8,128)S(1)}, u32[]{:S(2)}, u32[]{:S(2)}) collective-permute-start(f32[16,256]{1,0:T(8,128)S(1)} %add_select_fusion.7), channel_id=1, source_target_pairs={{0,32},{4,36},{8,40},{12,44},{16,48},{20,52},{24,56},{28,60},{32,0... | collective-permute-start | bytes 49160 | tf_op jit(solution)/shard_map/ppermute | solution.py:26
  45.3 1.1 %collective-permute-done.9 = f32[16,256]{1,0:T(8,128)S(1)} collective-permute-done((f32[16,256]{1,0:T(8,128)S(1)}, f32[16,256]{1,0:T(8,128)S(1)}, u32[]{:S(2)}, u32[]{:S(2)}) %collective-permute-start.9) | collective-permute-done | bytes 16416 | tf_op jit(solution)/shard_map/ppermute | solution.py:26
  46.5 5.3 %collective-permute-start.10 = (f32[16,256]{1,0:T(8,128)S(1)}, f32[16,256]{1,0:T(8,128)S(1)}, u32[]{:S(2)}, u32[]{:S(2)}) collective-permute-start(f32[16,256]{1,0:T(8,128)S(1)} %add_select_fusion.6), channel_id=1, source_target_pairs={{0,96},{4,100},{8,104},{12,108},{16,112},{20,116},{24,120},{28,124... | collective-permute-start | bytes 49160 | tf_op jit(solution)/shard_map/ppermute | solution.py:26
  51.8 1.1 %collective-permute-done.10 = f32[16,256]{1,0:T(8,128)S(1)} collective-permute-done((f32[16,256]{1,0:T(8,128)S(1)}, f32[16,256]{1,0:T(8,128)S(1)}, u32[]{:S(2)}, u32[]{:S(2)}) %collective-permute-start.10) | collective-permute-done | bytes 16416 | tf_op jit(solution)/shard_map/ppermute | solution.py:26
  52.9 2.0 %collective-permute-start.11 = (f32[16,256]{1,0:T(8,128)S(1)}, f32[16,256]{1,0:T(8,128)S(1)}, u32[]{:S(2)}, u32[]{:S(2)}) collective-permute-start(f32[16,256]{1,0:T(8,128)S(1)} %add_select_fusion.5), channel_id=1, source_target_pairs={{0,128},{4,132},{8,136},{12,140},{16,144},{20,148},{24,152},{28,15... | collective-permute-start | bytes 49160 | tf_op jit(solution)/shard_map/ppermute | solution.py:26
  54.9 1.1 %collective-permute-done.11 = f32[16,256]{1,0:T(8,128)S(1)} collective-permute-done((f32[16,256]{1,0:T(8,128)S(1)}, f32[16,256]{1,0:T(8,128)S(1)}, u32[]{:S(2)}, u32[]{:S(2)}) %collective-permute-start.11) | collective-permute-done | bytes 16416 | tf_op jit(solution)/shard_map/ppermute | solution.py:26
  56.8 1.3 %back.1 = (f32[2,512,256]{2,1,0:T(8,128)S(1)}, bf16[2,512,256]{2,1,0:T(8,128)(2,1)S(1)}) custom-call(f32[512,256]{1,0:T(8,128)S(1)} %get-tuple-element.11.queries, f32[512,256]{1,0:T(8,128)S(1)} %get-tuple-element.12.local, f32[16,8,256]{2,1,0:T(8,128)S(1)} %get-tuple-element.13.carry, f32[16,256]{1,0:T(8,128)S(1)} %add_select_fusion.entry, ...), custom_call_target="tpu_custom_call" | custom-call | tf_op jit(solution)/shard_map/back/pallas_call | solution.py:198
  58.1 6.9 %collective-permute-start.12 = (bf16[2,512,256]{2,1,0:T(8,128)(2,1)S(1)}, bf16[2,512,256]{2,1,0:T(8,128)(2,1)S(1)}, u32[]{:S(2)}, u32[]{:S(2)}) collective-permute-start(bf16[2,512,256]{2,1,0:T(8,128)(2,1)S(1)} %get-tuple-element.16), channel_id=1, source_target_pairs={{0,1},{1,0},{2,3},{3,2},{4,5},{5,4},{6,7},{7,6},{8,9},{9,8},{10,11... | collective-permute-start | bytes 1572872 | tf_op jit(solution)/shard_map/ppermute | solution.py:22
  65.0 1.5 %collective-permute-done.12 = bf16[2,512,256]{2,1,0:T(8,128)(2,1)S(1)} collective-permute-done((bf16[2,512,256]{2,1,0:T(8,128)(2,1)S(1)}, bf16[2,512,256]{2,1,0:T(8,128)(2,1)S(1)}, u32[]{:S(2)}, u32[]{:S(2)}) %collective-permute-start.12) | collective-permute-done | bytes 524320 | tf_op jit(solution)/shard_map/ppermute | solution.py:22
  66.7 1.6 %collective-permute-start.13 = (bf16[512,256]{1,0:T(8,128)(2,1)S(1)}, bf16[512,256]{1,0:T(8,128)(2,1)S(1)}, u32[]{:S(2)}, u32[]{:S(2)}) collective-permute-start(bf16[512,256]{1,0:T(8,128)(2,1)S(1)} %fusion.2), channel_id=1, source_target_pairs={{0,2},{1,3},{2,0},{3,1},{4,6},{5,7},{6,4},{7,5},{8,10},{9,11},{10,... | collective-permute-start | bytes 786440 | tf_op jit(solution)/shard_map/ppermute | solution.py:22
  68.3 7.5 %collective-permute-done.13 = bf16[512,256]{1,0:T(8,128)(2,1)S(1)} collective-permute-done((bf16[512,256]{1,0:T(8,128)(2,1)S(1)}, bf16[512,256]{1,0:T(8,128)(2,1)S(1)}, u32[]{:S(2)}, u32[]{:S(2)}) %collective-permute-start.13) | collective-permute-done | bytes 262176 | tf_op jit(solution)/shard_map/ppermute | solution.py:22
  (51 shorter events, 12.7 us)
Async XLA Ops:
  0.0 17.0 %collective-permute-start = (bf16[512,256]{1,0:T(8,128)(2,1)}, bf16[512,256]{1,0:T(8,128)(2,1)S(1)}, u32[]{:S(2)}, u32[]{:S(2)}) collective-permute-start(bf16[512,256]{1,0:T(8,128)(2,1)} %own.1), channel_id=1, source_target_pairs={{0,2},{1,3},{2,0},{3,1},{4,6},{5,7},{6,4},{7,5},{8,10},{9,11},{10,... | collective-permute-start | bytes 786440 | tf_op jit(solution)/shard_map/ppermute | solution.py:22
  4.3 1.8 %collective-permute-start.3 = (bf16[16,256]{1,0:T(8,128)(2,1)S(1)}, bf16[16,256]{1,0:T(8,128)(2,1)S(1)}, u32[]{:S(2)}, u32[]{:S(2)}) collective-permute-start(bf16[16,256]{1,0:T(8,128)(2,1)S(1)} %get-tuple-element.18), channel_id=1, source_target_pairs={{0,1},{1,0},{2,3},{3,2},{4,5},{5,4},{6,7},{7,6},{8,9},{9,8},{10,11... | collective-permute-start | bytes 24584 | tf_op jit(solution)/shard_map/ppermute | solution.py:22
  6.1 4.0 %collective-permute-start.4 = (bf16[2,16,256]{2,1,0:T(8,128)(2,1)S(1)}, bf16[2,16,256]{2,1,0:T(8,128)(2,1)S(1)}, u32[]{:S(2)}, u32[]{:S(2)}) collective-permute-start(bf16[2,16,256]{2,1,0:T(8,128)(2,1)S(1)} %pad_maximum_fusion.1), channel_id=1, source_target_pairs={{0,4},{1,7},{2,6},{3,5},{4,8},{5,11},{6,10},{7,9},{8,12},{9,15},{1... | collective-permute-start | bytes 49160 | tf_op jit(solution)/shard_map/ppermute | solution.py:147
  10.1 8.0 %collective-permute-start.5 = (bf16[2,16,256]{2,1,0:T(8,128)(2,1)S(1)}, bf16[2,16,256]{2,1,0:T(8,128)(2,1)S(1)}, u32[]{:S(2)}, u32[]{:S(2)}) collective-permute-start(bf16[2,16,256]{2,1,0:T(8,128)(2,1)S(1)} %collective-permute-done.4), channel_id=1, source_target_pairs={{0,1},{1,0},{2,3},{3,2},{4,5},{5,4},{6,7},{7,6},{8,9},{9,8},{10,11... | collective-permute-start | bytes 49160 | tf_op jit(solution)/shard_map/ppermute | solution.py:22
  11.3 6.9 %collective-permute-start.1 = (bf16[512,256]{1,0:T(8,128)(2,1)}, bf16[512,256]{1,0:T(8,128)(2,1)S(1)}, u32[]{:S(2)}, u32[]{:S(2)}) collective-permute-start(bf16[512,256]{1,0:T(8,128)(2,1)} %own.1), channel_id=1, source_target_pairs={{0,1},{1,0},{2,3},{3,2},{4,5},{5,4},{6,7},{7,6},{8,9},{9,8},{10,11... | collective-permute-start | bytes 786440 | tf_op jit(solution)/shard_map/ppermute | solution.py:22
  14.0 1.8 %copy-start.12 = (f32[3,3,256]{2,1,0:T(4,128)S(1)}, f32[3,3,256]{2,1,0:T(4,128)}, u32[]{:S(2)}) copy-start(f32[3,3,256]{2,1,0:T(4,128)} %param.11) | copy-start | bytes 27652
  14.0 2.4 %copy-start.13 = (f32[1024]{0:T(1024)S(1)}, f32[1024]{0:T(1024)}, u32[]{:S(2)}) copy-start(f32[1024]{0:T(1024)} %param.9) | copy-start | bytes 12292
  14.0 5.0 %copy-start = (f32[16,256]{1,0:T(8,128)S(1)}, f32[16,256]{1,0:T(8,128)}, u32[]{:S(2)}) copy-start(f32[16,256]{1,0:T(8,128)} %rates.3) | copy-start | bytes 49156
  14.0 5.0 %copy-start.2 = (bf16[512,256]{1,0:T(8,128)(2,1)S(1)}, bf16[512,256]{1,0:T(8,128)(2,1)}, u32[]{:S(2)}) copy-start(bf16[512,256]{1,0:T(8,128)(2,1)} %own.1) | copy-start | bytes 786436
  17.0 2.0 %collective-permute-start.2 = (bf16[512,256]{1,0:T(8,128)(2,1)S(1)}, bf16[512,256]{1,0:T(8,128)(2,1)S(1)}, u32[]{:S(2)}, u32[]{:S(2)}) collective-permute-start(bf16[512,256]{1,0:T(8,128)(2,1)S(1)} %collective-permute-done.far), channel_id=1, source_target_pairs={{0,1},{1,0},{2,3},{3,2},{4,5},{5,4},{6,7},{7,6},{8,9},{9,8},{10,11... | collective-permute-start | bytes 786440 | tf_op jit(solution)/shard_map/ppermute | solution.py:22
  18.9 1.0 %copy-start.4 = (bf16[512,256]{1,0:T(8,128)(2,1)S(1)}, bf16[512,256]{1,0:T(8,128)(2,1)}, u32[]{:S(2)}) copy-start(bf16[512,256]{1,0:T(8,128)(2,1)} %copy-done.3) | copy-start | bytes 786436
  19.9 0.9 %copy-start.6 = (bf16[512,256]{1,0:T(8,128)(2,1)S(1)}, bf16[512,256]{1,0:T(8,128)(2,1)}, u32[]{:S(2)}) copy-start(bf16[512,256]{1,0:T(8,128)(2,1)} %copy-done.5) | copy-start | bytes 786436
  20.8 0.7 copy-start.7
  21.5 0.7 copy-start.9
  23.6 32.5 %copy-start.1 = (bf16[256,1024]{1,0:T(8,128)(2,1)S(1)}, bf16[256,1024]{1,0:T(8,128)(2,1)}, u32[]{:S(2)}) copy-start(bf16[256,1024]{1,0:T(8,128)(2,1)} %w_out.1) | copy-start | bytes 1572868
  28.1 4.3 %collective-permute-start.6 = (f32[16,256]{1,0:T(8,128)}, f32[16,256]{1,0:T(8,128)S(1)}, u32[]{:S(2)}, u32[]{:S(2)}) collective-permute-start(f32[16,256]{1,0:T(8,128)} %get-tuple-element.14), channel_id=1, source_target_pairs={{0,4},{4,0},{8,12},{12,8},{16,20},{20,16},{24,28},{28,24},{32,36},... | collective-permute-start | bytes 49160 | tf_op jit(solution)/shard_map/ppermute | solution.py:26
  33.2 4.1 %collective-permute-start.7 = (f32[16,256]{1,0:T(8,128)S(1)}, f32[16,256]{1,0:T(8,128)S(1)}, u32[]{:S(2)}, u32[]{:S(2)}) collective-permute-start(f32[16,256]{1,0:T(8,128)S(1)} %add_select_fusion.9), channel_id=1, source_target_pairs={{0,12},{4,8},{8,4},{12,0},{16,28},{20,24},{24,20},{28,16},{32,44},... | collective-permute-start | bytes 49160 | tf_op jit(solution)/shard_map/ppermute | solution.py:26
  37.3 4.9 %collective-permute-start.8 = (f32[16,256]{1,0:T(8,128)S(1)}, f32[16,256]{1,0:T(8,128)S(1)}, u32[]{:S(2)}, u32[]{:S(2)}) collective-permute-start(f32[16,256]{1,0:T(8,128)S(1)} %add_select_fusion.8), channel_id=1, source_target_pairs={{0,16},{4,20},{8,24},{12,28},{16,0},{20,4},{24,8},{28,12},{32,48},... | collective-permute-start | bytes 49160 | tf_op jit(solution)/shard_map/ppermute | solution.py:26
  42.2 4.2 %collective-permute-start.9 = (f32[16,256]{1,0:T(8,128)S(1)}, f32[16,256]{1,0:T(8,128)S(1)}, u32[]{:S(2)}, u32[]{:S(2)}) collective-permute-start(f32[16,256]{1,0:T(8,128)S(1)} %add_select_fusion.7), channel_id=1, source_target_pairs={{0,32},{4,36},{8,40},{12,44},{16,48},{20,52},{24,56},{28,60},{32,0... | collective-permute-start | bytes 49160 | tf_op jit(solution)/shard_map/ppermute | solution.py:26
  46.5 6.5 %collective-permute-start.10 = (f32[16,256]{1,0:T(8,128)S(1)}, f32[16,256]{1,0:T(8,128)S(1)}, u32[]{:S(2)}, u32[]{:S(2)}) collective-permute-start(f32[16,256]{1,0:T(8,128)S(1)} %add_select_fusion.6), channel_id=1, source_target_pairs={{0,96},{4,100},{8,104},{12,108},{16,112},{20,116},{24,120},{28,124... | collective-permute-start | bytes 49160 | tf_op jit(solution)/shard_map/ppermute | solution.py:26
  52.9 3.1 %collective-permute-start.11 = (f32[16,256]{1,0:T(8,128)S(1)}, f32[16,256]{1,0:T(8,128)S(1)}, u32[]{:S(2)}, u32[]{:S(2)}) collective-permute-start(f32[16,256]{1,0:T(8,128)S(1)} %add_select_fusion.5), channel_id=1, source_target_pairs={{0,128},{4,132},{8,136},{12,140},{16,144},{20,148},{24,152},{28,15... | collective-permute-start | bytes 49160 | tf_op jit(solution)/shard_map/ppermute | solution.py:26
  56.1 0.7 copy-start.8
  58.1 8.4 %collective-permute-start.12 = (bf16[2,512,256]{2,1,0:T(8,128)(2,1)S(1)}, bf16[2,512,256]{2,1,0:T(8,128)(2,1)S(1)}, u32[]{:S(2)}, u32[]{:S(2)}) collective-permute-start(bf16[2,512,256]{2,1,0:T(8,128)(2,1)S(1)} %get-tuple-element.16), channel_id=1, source_target_pairs={{0,1},{1,0},{2,3},{3,2},{4,5},{5,4},{6,7},{7,6},{8,9},{9,8},{10,11... | collective-permute-start | bytes 1572872 | tf_op jit(solution)/shard_map/ppermute | solution.py:22
  66.7 9.1 %collective-permute-start.13 = (bf16[512,256]{1,0:T(8,128)(2,1)S(1)}, bf16[512,256]{1,0:T(8,128)(2,1)S(1)}, u32[]{:S(2)}, u32[]{:S(2)}) collective-permute-start(bf16[512,256]{1,0:T(8,128)(2,1)S(1)} %fusion.2), channel_id=1, source_target_pairs={{0,2},{1,3},{2,0},{3,1},{4,6},{5,7},{6,4},{7,5},{8,10},{9,11},{10,... | collective-permute-start | bytes 786440 | tf_op jit(solution)/shard_map/ppermute | solution.py:22
  (4 other events, 2.8 us)

commit v2 on v1

v2 whole, which is shorter than its diff:
```python
import jax
import jax.numpy as jnp
from jax import lax
from jax.experimental import pallas as pl
from jax.experimental.pallas import tpu as pltpu
from jax.sharding import PartitionSpec as P

EPSILON = 1e-06
F32 = jnp.float32
BF16 = jnp.bfloat16
LANES = 128
SUBS = 8
HALO = 16
STAGE_VMEM = 2 * 1024 * 1024
FRONT_VMEM = 16 * 1024 * 1024
SCAN_VMEM = 8 * 1024 * 1024
BACK_VMEM = 12 * 1024 * 1024

SCAN_MASKS = (1, 3, 4, 8, 24, 32)


def ch_swap(array, mask):
    return lax.ppermute(array, "ch", [(i, i ^ mask) for i in range(lax.axis_size("ch"))])


def seq_swap(array, mask):
    return lax.ppermute(array, "seq", [(i, i ^ mask) for i in range(lax.axis_size("seq"))])


def vmem_specs(count):
    return [pl.BlockSpec(memory_space=pltpu.VMEM)] * count


def row(ref, index, lanes):
    return jnp.broadcast_to(ref[pl.ds(index, 1), lanes], (SUBS, LANES))


def tree_sum(terms):
    while len(terms) > 1:
        terms = [sum(terms[i : i + 2][1:], terms[i]) for i in range(0, len(terms), 2)]
    return terms[0]


def stage_kernel(own, w_in, taps, rates, gain, own_v, w_in_v, taps_v, rates_v, gain_v, sems):
    pairs = ((own, own_v), (w_in, w_in_v), (taps, taps_v), (rates, rates_v), (gain, gain_v))
    copies = [pltpu.make_async_copy(src, dst, sems.at[i]) for i, (src, dst) in enumerate(pairs)]
    for copy in copies:
        copy.start()
    for copy in copies:
        copy.wait()


def front_kernel(
    own, far, side, side_far, gain, w_in, taps, rates,
    queries, gated, message, projected,
):
    me = lax.axis_index("ch")
    rows, width = own.shape
    span = rows // SUBS
    modes = rates.shape[0]
    tiles = width // LANES
    square = jnp.zeros((rows, LANES), F32)
    blocks = (own, side, far, side_far)
    for block in blocks:
        for lane in range(0, width, LANES):
            piece = block[:, lane : lane + LANES].astype(F32)
            square = square + piece * piece
    scale = lax.rsqrt(jnp.sum(square, axis=1, keepdims=True) * (1.0 / (4 * width)) + EPSILON)
    normed = []
    for order, block in enumerate(blocks):
        part = jnp.bitwise_xor(me, order)
        pieces = [
            block[:, tile * LANES : (tile + 1) * LANES].astype(F32) * scale * gain[pl.ds(part * tiles + tile, 1), :]
            for tile in range(tiles)
        ]
        normed.append(jnp.concatenate(pieces, axis=1).astype(BF16))
    for group in range(3):
        total = jnp.zeros((rows, width), F32)
        for order in range(4):
            start = pl.multiple_of(jnp.bitwise_xor(me, order) * width, width)
            total = total + jnp.dot(
                normed[order], w_in[group, pl.ds(start, width), :], preferred_element_type=F32
            )
        total = total.astype(BF16).astype(F32)
        for tile in range(tiles):
            projected[group * tiles + tile, :HALO] = jnp.zeros((HALO, LANES), F32)
            projected[group * tiles + tile, HALO:] = total[:, tile * LANES : (tile + 1) * LANES]

    sub = lax.broadcasted_iota(jnp.int32, (SUBS, LANES), 0)
    message[...] = jnp.zeros_like(message)
    for tile in range(tiles):
        lanes = pl.ds(tile * LANES, LANES)
        rate = [row(rates, m, lanes) for m in range(modes)]
        decay = [jnp.exp(-r) for r in rate]
        tap = [[jnp.broadcast_to(taps[s, pl.ds(g, 1), lanes], (SUBS, LANES)) for s in range(3)] for g in range(3)]

        def read(start, group):
            return projected[group * tiles + tile, pl.ds(start, SUBS, stride=span), :]

        def step(index, held):
            before, state = held
            now = [read(HALO + index, g) for g in range(3)]
            filtered = [
                tap[g][0] * now[g] + tap[g][1] * before[0][g] + tap[g][2] * before[1][g] for g in range(3)
            ]
            product = filtered[1] * filtered[2]
            at = pl.ds(pl.multiple_of(index * SUBS, SUBS), SUBS)
            queries[at, lanes] = filtered[0]
            gated[at, lanes] = product
            return ((now, before[0]), [decay[m] * state[m] + product for m in range(modes)])

        first = ([read(HALO - 1, g) for g in range(3)], [read(HALO - 2, g) for g in range(3)])
        zeros = [jnp.zeros((SUBS, LANES), F32)] * modes
        _, state = lax.fori_loop(0, span, step, (first, zeros), unroll=8)
        for m in range(modes):
            upto = state[m] * jnp.exp(rate[m] * (float(span) * (sub - (SUBS - 1)).astype(F32)))
            message[pl.ds(m, 1), lanes] = jnp.sum(upto, axis=0, keepdims=True)
        for group in range(3):
            t = [taps[s, pl.ds(group, 1), lanes] for s in range(3)]
            p = [projected[group * tiles + tile, pl.ds(HALO + i, 1), :] for i in (0, 1, rows - 2, rows - 1)]
            if group > 0:
                message[pl.ds(modes + 2 * group - 2, 1), lanes] = t[0] * p[0]
                message[pl.ds(modes + 2 * group - 1, 1), lanes] = t[0] * p[1] + t[1] * p[0]
            to = modes + SUBS + 2 * ((group - 1) % 3)
            message[pl.ds(to, 1), lanes] = t[1] * p[3] + t[2] * p[2]
            message[pl.ds(to + 1, 1), lanes] = t[2] * p[3]


def scan_kernel(gated, rates, residues, skip, local, carry):
    rows, width = gated.shape
    span = rows // SUBS
    modes = rates.shape[0]
    sub = lax.broadcasted_iota(jnp.int32, (SUBS, LANES), 0)
    for lane in range(0, width, LANES):
        lanes = pl.ds(lane, LANES)
        rate = [row(rates, m, lanes) for m in range(modes)]
        decay = [jnp.exp(-r) for r in rate]
        weight = [row(residues, m, lanes) * jnp.sqrt(rate[m]) for m in range(modes)]
        skip_row = row(skip, 0, lanes)

        def step(index, state):
            at = pl.ds(pl.multiple_of(index * SUBS, SUBS), SUBS)
            product = gated[at, lanes]
            state = [decay[m] * state[m] + product for m in range(modes)]
            local[at, lanes] = tree_sum([weight[m] * state[m] for m in range(modes)] + [skip_row * product])
            return state

        state = lax.fori_loop(0, span, step, [jnp.zeros((SUBS, LANES), F32)] * modes, unroll=8)
        for m in range(modes):
            upto = state[m]
            for reach in (1, 2, 4):
                moved = pltpu.roll(upto, reach, 0) * jnp.exp(rate[m] * (-float(span * reach)))
                upto = upto + jnp.where(sub >= reach, moved, 0.0)
            carry[m, :, lanes] = jnp.where(sub >= 1, pltpu.roll(upto, 1, 0), 0.0)


def back_kernel(
    queries, local, carry, entry, fix, rates, residues, skip, w_out, kept, sent, mixed
):
    me = lax.axis_index("ch")
    rows, width = queries.shape
    span = rows // SUBS
    modes = rates.shape[0]
    sub = lax.broadcasted_iota(jnp.int32, (SUBS, LANES), 0)
    for lane in range(0, width, LANES):
        lanes = pl.ds(lane, LANES)
        rate = [row(rates, m, lanes) for m in range(modes)]
        decay = [jnp.exp(-r) for r in rate]
        state, lead = [], []
        for m in range(modes):
            weight = row(residues, m, lanes) * jnp.sqrt(rate[m])
            entering = carry[m, :, lanes]
            entering = entering + jnp.exp(rate[m] * sub.astype(F32) * (-float(span))) * row(entry, m, lanes)
            state.append(weight * decay[m] * entering)
            lead.append(weight * jnp.exp(rate[m]))

        def token(index, held, more_local=None, more_query=None):
            at = pl.ds(pl.multiple_of(index * SUBS, SUBS), SUBS)
            value, query = local[at, lanes], queries[at, lanes]
            if more_local is not None:
                value = value + jnp.where(sub == 0, more_local, 0.0)
                query = query + jnp.where(sub == 0, more_query, 0.0)
            mixed[lane // LANES, pl.ds(index, SUBS, stride=span), :] = query * tree_sum(list(held) + [value])
            return [decay[m] * held[m] for m in range(modes)]

        skip_row = row(skip, 0, lanes)
        more = [row(fix, i, lanes) for i in range(4)]
        state = token(0, state, skip_row * more[0] - tree_sum(lead) * more[1], more[2])
        state = token(1, state, skip_row * more[1], more[3])
        lax.fori_loop(2, span, token, state, unroll=2)
    mixed_in = jnp.concatenate([mixed[tile] for tile in range(width // LANES)], axis=1).astype(BF16)
    for order in range(4):
        start = pl.multiple_of(jnp.bitwise_xor(me, order) * width, width)
        share = jnp.dot(mixed_in, w_out[:, pl.ds(start, width)], preferred_element_type=F32)
        if order % 2 == 0:
            kept[order // 2] = share
        else:
            sent[order // 2] = share.astype(BF16)


def scan_blocks(message, rates, rows):
    block = lax.axis_index("seq")
    rounds = lax.axis_size("seq").bit_length() - 1
    modes = rates.shape[0]
    back_one, back_two = jnp.exp(rates), jnp.exp(2.0 * rates)
    entry = jnp.zeros_like(rates)
    fix = jnp.zeros((4,) + rates.shape[1:], F32)
    for level in range(rounds):
        other = seq_swap(message, SCAN_MASKS[level])
        upper = jnp.bitwise_and(jnp.right_shift(block, level), 1) == 1
        ahead = jnp.bitwise_and(block, (1 << level) - 1)
        decay_ahead = jnp.exp(-rates * (ahead.astype(F32) * float(rows)))
        across = jnp.exp(-rates * float(rows << level))
        first = jnp.where(upper, other, message)
        second = jnp.where(upper, message, other)
        start = second[modes : modes + SUBS]
        end = first[modes + SUBS :]
        added = start[0:2] * end[2:4] + end[0:2] * (start[2:4] + end[2:4])
        joined = first[:modes] + back_one * added[0:1] + back_two * added[1:2]
        entry = jnp.where(upper, entry + decay_ahead * joined, entry)
        fix = jnp.where(
            jnp.logical_and(upper, ahead == 0), jnp.concatenate([added, end[4:6]], axis=0), fix
        )
        message = jnp.concatenate(
            [across * joined + second[:modes], first[modes : modes + SUBS], second[modes + SUBS :]], axis=0
        )
    return entry, fix


def body(tokens, norm_gain, w_in, short_filter, rates, residues, skip_gain, w_out):
    rows, width = tokens.shape
    channels = w_in.shape[2]
    modes = rates.shape[0]
    skip = skip_gain.reshape(1, channels)
    far = ch_swap(tokens, 2)
    side = ch_swap(tokens, 1)
    weights = jnp.transpose(w_in, (1, 0, 2))
    gains = norm_gain.reshape(-1, LANES)
    staged = (tokens, weights, short_filter, rates, gains)
    staged = pl.pallas_call(
        stage_kernel,
        out_shape=tuple(jax.ShapeDtypeStruct(a.shape, a.dtype) for a in staged),
        in_specs=[pl.BlockSpec(memory_space=pl.ANY)] * len(staged),
        out_specs=tuple(vmem_specs(len(staged))),
        scratch_shapes=[pltpu.SemaphoreType.DMA((len(staged),))],
        compiler_params=pltpu.CompilerParams(vmem_limit_bytes=STAGE_VMEM),
        name="stage",
    )(*staged)
    far, staged = lax.optimization_barrier((far, staged))
    side_far = ch_swap(far, 1)
    own_v, w_in_v, taps_v, rates_v, gain_v = staged
    queries, gated, message = pl.pallas_call(
        front_kernel,
        out_shape=(
            jax.ShapeDtypeStruct((rows, channels), F32),
            jax.ShapeDtypeStruct((rows, channels), F32),
            jax.ShapeDtypeStruct((modes + 2 * SUBS, channels), F32),
        ),
        in_specs=vmem_specs(8),
        out_specs=tuple(vmem_specs(3)),
        scratch_shapes=[pltpu.VMEM((3 * channels // LANES, rows + HALO, LANES), F32)],
        compiler_params=pltpu.CompilerParams(vmem_limit_bytes=FRONT_VMEM),
        cost_estimate=pl.CostEstimate(flops=900_000_000, bytes_accessed=4_000_000, transcendentals=0),
        name="front",
    )(
        own_v, far, side, side_far, gain_v, w_in_v, taps_v, rates_v,
    )
    local, carry = pl.pallas_call(
        scan_kernel,
        out_shape=(
            jax.ShapeDtypeStruct((rows, channels), F32),
            jax.ShapeDtypeStruct((modes, SUBS, channels), F32),
        ),
        in_specs=vmem_specs(4),
        out_specs=tuple(vmem_specs(2)),
        compiler_params=pltpu.CompilerParams(vmem_limit_bytes=SCAN_VMEM),
        cost_estimate=pl.CostEstimate(flops=2_000_000_000, bytes_accessed=1_000_000, transcendentals=0),
        name="scan",
    )(gated, rates_v, residues, skip)
    entry, fix = scan_blocks(message, rates_v, rows)
    kept, sent = pl.pallas_call(
        back_kernel,
        out_shape=(
            jax.ShapeDtypeStruct((2, rows, width), F32),
            jax.ShapeDtypeStruct((2, rows, width), BF16),
        ),
        in_specs=vmem_specs(9),
        out_specs=tuple(vmem_specs(2)),
        scratch_shapes=[pltpu.VMEM((channels // LANES, rows, LANES), F32)],
        compiler_params=pltpu.CompilerParams(vmem_limit_bytes=BACK_VMEM),
        cost_estimate=pl.CostEstimate(flops=900_000_000, bytes_accessed=4_000_000, transcendentals=0),
        name="back",
    )(queries, local, carry, entry, fix, rates_v, residues, skip, w_out)
    both = kept + ch_swap(sent, 1).astype(F32)
    away = ch_swap(both[1].astype(BF16), 2)
    return (both[0] + away.astype(F32)).astype(BF16)


def solution(mesh):
    return jax.shard_map(
        body,
        mesh=mesh,
        in_specs=(
            P("seq", "ch"),
            P(),
            P(None, None, "ch"),
            P(None, None, "ch"),
            P(None, "ch"),
            P(None, "ch"),
            P("ch"),
            P("ch", None),
        ),
        out_specs=P("seq", "ch"),
        check_vma=False,
    )
```

time: 77.3 us -> 60.1 us (0.78)
  local copies, waits for them, and re-layouts: 13.1 us -> 4.57 us
  starting transfers between devices: 38 us -> 32 us
  waiting for transfers between devices: 17.8 us -> 15.9 us
    unnamed x29 -> x16, local copies, waits for them, and re-layouts: 9.42 us -> 4.48 us
    ppermute x6, starting transfers between devices: 20.2 us -> 15.5 us  [seq_swap(): lax.ppermute(array, 'seq', [(i, i ^ mask) for i in range(lax.axis_size('s...]
    ppermute x1 -> x0, starting transfers between devices: 3.13 us -> none  [halo_tokens(): mine = lax.ppermute(pair, ('seq', 'ch'), moves)]
    reshape x3 -> x0, local copies, waits for them, and re-layouts: 2.97 us -> none  [the longest x1 1.76 us: body(): w_in.reshape(slab, 3 * channels)]
    ppermute x7 -> x5, starting transfers between devices: 14.7 us -> 16.5 us  [ch_swap(): lax.ppermute(array, 'ch', [(i, i ^ mask) for i in range(lax.axis_size('ch...]
    pallas_call x1, Pallas kernels: 4.49 us -> 2.8 us  [body(): pl.pallas_call(front_kernel, out_shape=(jax.ShapeDtypeStruct((rows, chann...]
    pallas_call x0 -> x2, Pallas kernels: none -> 1.6 us  [the longest x1 1.39 us: body(): pl.pallas_call(scan_kernel, out_shape=(jax.ShapeDtypeStruct((rows, channe...]
    ppermute x7 -> x5, waiting for transfers between devices: 9.89 us -> 8.97 us  [ch_swap(): lax.ppermute(array, 'ch', [(i, i ^ mask) for i in range(lax.axis_size('ch...]
  transfers between devices with their start and end apart: 14 -> 11, of which waited for: 10 -> 9; matrix products, arithmetic and copies ran while one was open for 8% -> 0% of each run, Pallas kernels for 0% -> 3%
where the time goes in v2:
time: 60.1 us; the launch traced here: 59.8 us
  starting transfers between devices  32 us (53%)
  waiting for transfers between devices  15.9 us (26%)
  Pallas kernels  5.82 us (10%)
  local copies, waits for them, and re-layouts  4.57 us (8%)
  other arithmetic  1.22 us (2%)
    ppermute x5, starting transfers between devices, ch_swap(): lax.ppermute(array, 'ch', [(i, i ^ mask) for i in range(lax.axis_size('ch...  16.5 us
    ppermute x6, starting transfers between devices, seq_swap(): lax.ppermute(array, 'seq', [(i, i ^ mask) for i in range(lax.axis_size('s...  15.5 us
    ppermute x5, waiting for transfers between devices, ch_swap(): lax.ppermute(array, 'ch', [(i, i ^ mask) for i in range(lax.axis_size('ch...  8.97 us
    ppermute x6, waiting for transfers between devices, seq_swap(): lax.ppermute(array, 'seq', [(i, i ^ mask) for i in range(lax.axis_size('s...  6.91 us
    unnamed x16, local copies, waits for them, and re-layouts  4.48 us
    pallas_call x1, Pallas kernels, body(): pl.pallas_call(front_kernel, out_shape=(jax.ShapeDtypeStruct((rows, chann...  2.8 us
    pallas_call x1, Pallas kernels, body(): pl.pallas_call(back_kernel, out_shape=(jax.ShapeDtypeStruct((2, rows, wid...  1.42 us
    pallas_call x1, Pallas kernels, body(): pl.pallas_call(scan_kernel, out_shape=(jax.ShapeDtypeStruct((rows, channe...  1.39 us
  transfers between devices with their start and end apart: 11, of which 9 were waited for; matrix products, arithmetic and copies ran while one was open for 0% of the time, Pallas kernels for 3%

profile of v2, /device:TPU:1, one launch (start us, length us, event | category | flops | bytes accessed | tf_op | source)
XLA Modules:
  0.0 59.8 jit_solution(15355792167516610383)
XLA Ops:
  0.0 3.6 %collective-permute-start = (bf16[512,256]{1,0:T(8,128)(2,1)}, bf16[512,256]{1,0:T(8,128)(2,1)S(1)}, u32[]{:S(2)}, u32[]{:S(2)}) collective-permute-start(bf16[512,256]{1,0:T(8,128)(2,1)} %own.1), channel_id=1, source_target_pairs={{0,2},{1,3},{2,0},{3,1},{4,6},{5,7},{6,4},{7,5},{8,10},{9,11},{10,... | collective-permute-start | bytes 786440 | tf_op jit(solution)/shard_map/ppermute | solution.py:23
  3.6 1.0 %collective-permute-start.1 = (bf16[512,256]{1,0:T(8,128)(2,1)}, bf16[512,256]{1,0:T(8,128)(2,1)S(1)}, u32[]{:S(2)}, u32[]{:S(2)}) collective-permute-start(bf16[512,256]{1,0:T(8,128)(2,1)} %own.1), channel_id=1, source_target_pairs={{0,1},{1,0},{2,3},{3,2},{4,5},{5,4},{6,7},{7,6},{8,9},{9,8},{10,11... | collective-permute-start | bytes 786440 | tf_op jit(solution)/shard_map/ppermute | solution.py:23
  4.5 1.4 %copy-done = bf16[1024,3,256]{2,0,1:T(8,128)(2,1)S(1)} copy-done((bf16[1024,3,256]{2,0,1:T(8,128)(2,1)S(1)}, bf16[1024,3,256]{2,0,1:T(8,128)(2,1)}, u32[]{:S(2)}) %copy-start) | copy-done | bytes 1572888
  5.9 0.9 %copy-done.1 = bf16[512,256]{1,0:T(8,128)(2,1)S(1)} copy-done((bf16[512,256]{1,0:T(8,128)(2,1)S(1)}, bf16[512,256]{1,0:T(8,128)(2,1)}, u32[]{:S(2)}) %copy-start.1) | copy-done | bytes 262168
  9.2 2.1 %collective-permute-start.2 = (bf16[512,256]{1,0:T(8,128)(2,1)S(1)}, bf16[512,256]{1,0:T(8,128)(2,1)S(1)}, u32[]{:S(2)}, u32[]{:S(2)}) collective-permute-start(bf16[512,256]{1,0:T(8,128)(2,1)S(1)} %collective-permute-done.far), channel_id=1, source_target_pairs={{0,1},{1,0},{2,3},{3,2},{4,5},{5,4},{6,7},{7,6},{8,9},{9,8},{10,11... | collective-permute-start | bytes 786440 | tf_op jit(solution)/shard_map/ppermute | solution.py:23
  11.3 1.2 %collective-permute-done.2.side_far = bf16[512,256]{1,0:T(8,128)(2,1)S(1)} collective-permute-done((bf16[512,256]{1,0:T(8,128)(2,1)S(1)}, bf16[512,256]{1,0:T(8,128)(2,1)S(1)}, u32[]{:S(2)}, u32[]{:S(2)}) %collective-permute-start.2) | collective-permute-done | bytes 262176 | tf_op jit(solution)/shard_map/ppermute | solution.py:23
  12.5 2.8 %front.1 = (f32[512,256]{1,0:T(8,128)S(1)}, f32[512,256]{1,0:T(8,128)S(1)}, f32[32,256]{1,0:T(8,128)S(1)}) custom-call(bf16[512,256]{1,0:T(8,128)(2,1)S(1)} %get-tuple-element.28.own, bf16[512,256]{1,0:T(8,128)(2,1)S(1)} %collective-permute-done.far, bf16[512,256]{1,0:T(8,128)(2,1)S(1)} %collective-permute-done.1.side, ...), custom_call_target="tpu_custom_call" | custom-call | flops 900000000 | bytes 4000000 | tf_op jit(solution)/shard_map/front/pallas_call | solution.py:252
  15.3 1.3 %collective-permute-start.3 = (f32[32,256]{1,0:T(8,128)S(1)}, f32[32,256]{1,0:T(8,128)S(1)}, u32[]{:S(2)}, u32[]{:S(2)}) collective-permute-start(f32[32,256]{1,0:T(8,128)S(1)} %get-tuple-element.38), channel_id=1, source_target_pairs={{0,4},{4,0},{8,12},{12,8},{16,20},{20,16},{24,28},{28,24},{32,36},... | collective-permute-start | bytes 98312 | tf_op jit(solution)/shard_map/ppermute | solution.py:27
  16.6 1.5 %collective-permute-done.3 = f32[32,256]{1,0:T(8,128)S(1)} collective-permute-done((f32[32,256]{1,0:T(8,128)S(1)}, f32[32,256]{1,0:T(8,128)S(1)}, u32[]{:S(2)}, u32[]{:S(2)}) %collective-permute-start.3) | collective-permute-done | bytes 32800 | tf_op jit(solution)/shard_map/ppermute | solution.py:27
  18.3 2.8 %collective-permute-start.4 = (f32[32,256]{1,0:T(8,128)S(1)}, f32[32,256]{1,0:T(8,128)S(1)}, u32[]{:S(2)}, u32[]{:S(2)}) collective-permute-start(f32[32,256]{1,0:T(8,128)S(1)} %pad_maximum_fusion), channel_id=1, source_target_pairs={{0,12},{4,8},{8,4},{12,0},{16,28},{20,24},{24,20},{28,16},{32,44},... | collective-permute-start | bytes 98312 | tf_op jit(solution)/shard_map/ppermute | solution.py:27
  21.0 1.3 %collective-permute-done.4 = f32[32,256]{1,0:T(8,128)S(1)} collective-permute-done((f32[32,256]{1,0:T(8,128)S(1)}, f32[32,256]{1,0:T(8,128)S(1)}, u32[]{:S(2)}, u32[]{:S(2)}) %collective-permute-start.4) | collective-permute-done | bytes 32800 | tf_op jit(solution)/shard_map/ppermute | solution.py:27
  22.4 1.7 %collective-permute-start.5 = (f32[32,256]{1,0:T(8,128)S(1)}, f32[32,256]{1,0:T(8,128)S(1)}, u32[]{:S(2)}, u32[]{:S(2)}) collective-permute-start(f32[32,256]{1,0:T(8,128)S(1)} %pad_maximum_fusion.1), channel_id=1, source_target_pairs={{0,16},{4,20},{8,24},{12,28},{16,0},{20,4},{24,8},{28,12},{32,48},... | collective-permute-start | bytes 98312 | tf_op jit(solution)/shard_map/ppermute | solution.py:27
  24.2 1.3 %collective-permute-done.5 = f32[32,256]{1,0:T(8,128)S(1)} collective-permute-done((f32[32,256]{1,0:T(8,128)S(1)}, f32[32,256]{1,0:T(8,128)S(1)}, u32[]{:S(2)}, u32[]{:S(2)}) %collective-permute-start.5) | collective-permute-done | bytes 32800 | tf_op jit(solution)/shard_map/ppermute | solution.py:27
  25.6 3.1 %collective-permute-start.6 = (f32[32,256]{1,0:T(8,128)S(1)}, f32[32,256]{1,0:T(8,128)S(1)}, u32[]{:S(2)}, u32[]{:S(2)}) collective-permute-start(f32[32,256]{1,0:T(8,128)S(1)} %pad_maximum_fusion.2), channel_id=1, source_target_pairs={{0,32},{4,36},{8,40},{12,44},{16,48},{20,52},{24,56},{28,60},{32,0... | collective-permute-start | bytes 98312 | tf_op jit(solution)/shard_map/ppermute | solution.py:27
  28.6 1.3 %collective-permute-done.6 = f32[32,256]{1,0:T(8,128)S(1)} collective-permute-done((f32[32,256]{1,0:T(8,128)S(1)}, f32[32,256]{1,0:T(8,128)S(1)}, u32[]{:S(2)}, u32[]{:S(2)}) %collective-permute-start.6) | collective-permute-done | bytes 32800 | tf_op jit(solution)/shard_map/ppermute | solution.py:27
  30.1 5.3 %collective-permute-start.7 = (f32[32,256]{1,0:T(8,128)S(1)}, f32[32,256]{1,0:T(8,128)S(1)}, u32[]{:S(2)}, u32[]{:S(2)}) collective-permute-start(f32[32,256]{1,0:T(8,128)S(1)} %pad_maximum_fusion.3), channel_id=1, source_target_pairs={{0,96},{4,100},{8,104},{12,108},{16,112},{20,116},{24,120},{28,124... | collective-permute-start | bytes 98312 | tf_op jit(solution)/shard_map/ppermute | solution.py:27
  35.4 1.3 %collective-permute-done.7 = f32[32,256]{1,0:T(8,128)S(1)} collective-permute-done((f32[32,256]{1,0:T(8,128)S(1)}, f32[32,256]{1,0:T(8,128)S(1)}, u32[]{:S(2)}, u32[]{:S(2)}) %collective-permute-start.7) | collective-permute-done | bytes 32800 | tf_op jit(solution)/shard_map/ppermute | solution.py:27
  36.8 1.3 %collective-permute-start.8 = (f32[32,256]{1,0:T(8,128)S(1)}, f32[32,256]{1,0:T(8,128)S(1)}, u32[]{:S(2)}, u32[]{:S(2)}) collective-permute-start(f32[32,256]{1,0:T(8,128)S(1)} %pad_maximum_fusion.4), channel_id=1, source_target_pairs={{0,128},{4,132},{8,136},{12,140},{16,144},{20,148},{24,152},{28,15... | collective-permute-start | bytes 98312 | tf_op jit(solution)/shard_map/ppermute | solution.py:27
  38.1 1.4 %scan.1 = (f32[512,256]{1,0:T(8,128)S(1)}, f32[16,8,256]{2,1,0:T(8,128)S(1)}) custom-call(f32[512,256]{1,0:T(8,128)S(1)} %get-tuple-element.35.gated, f32[16,256]{1,0:T(8,128)S(1)} %get-tuple-element.33.rates, f32[16,256]{1,0:T(8,128)S(1)} %copy-done.6, f32[1,256]{1,0:T(1,128)S(1)} %bitcast.25), custom_call_target="tpu_custom_call" | custom-call | flops 2000000000 | bytes 1000000 | tf_op jit(solution)/shard_map/scan/pallas_call | solution.py:268
  39.8 1.4 %back.1 = (f32[2,512,256]{2,1,0:T(8,128)S(1)}, bf16[2,512,256]{2,1,0:T(8,128)(2,1)S(1)}) custom-call(f32[512,256]{1,0:T(8,128)S(1)} %get-tuple-element.34.queries, f32[512,256]{1,0:T(8,128)S(1)} %get-tuple-element.36.local, f32[16,8,256]{2,1,0:T(8,128)S(1)} %get-tuple-element.37.carry, f32[16,256]{1,0:T(8,128)S(1)} %add_select_fusion.entry, ...), custom_call_target="tpu_custom_call" | custom-call | flops 900000000 | bytes 4000000 | tf_op jit(solution)/shard_map/back/pallas_call | solution.py:281
  41.2 7.0 %collective-permute-start.9 = (bf16[2,512,256]{2,1,0:T(8,128)(2,1)S(1)}, bf16[2,512,256]{2,1,0:T(8,128)(2,1)S(1)}, u32[]{:S(2)}, u32[]{:S(2)}) collective-permute-start(bf16[2,512,256]{2,1,0:T(8,128)(2,1)S(1)} %get-tuple-element.40), channel_id=1, source_target_pairs={{0,1},{1,0},{2,3},{3,2},{4,5},{5,4},{6,7},{7,6},{8,9},{9,8},{10,11... | collective-permute-start | bytes 1572872 | tf_op jit(solution)/shard_map/ppermute | solution.py:23
  48.2 1.5 %collective-permute-done.9 = bf16[2,512,256]{2,1,0:T(8,128)(2,1)S(1)} collective-permute-done((bf16[2,512,256]{2,1,0:T(8,128)(2,1)S(1)}, bf16[2,512,256]{2,1,0:T(8,128)(2,1)S(1)}, u32[]{:S(2)}, u32[]{:S(2)}) %collective-permute-start.9) | collective-permute-done | bytes 524320 | tf_op jit(solution)/shard_map/ppermute | solution.py:23
  49.9 2.8 %collective-permute-start.10 = (bf16[512,256]{1,0:T(8,128)(2,1)S(1)}, bf16[512,256]{1,0:T(8,128)(2,1)S(1)}, u32[]{:S(2)}, u32[]{:S(2)}) collective-permute-start(bf16[512,256]{1,0:T(8,128)(2,1)S(1)} %fusion.2), channel_id=1, source_target_pairs={{0,2},{1,3},{2,0},{3,1},{4,6},{5,7},{6,4},{7,5},{8,10},{9,11},{10,... | collective-permute-start | bytes 786440 | tf_op jit(solution)/shard_map/ppermute | solution.py:23
  52.7 6.3 %collective-permute-done.10 = bf16[512,256]{1,0:T(8,128)(2,1)S(1)} collective-permute-done((bf16[512,256]{1,0:T(8,128)(2,1)S(1)}, bf16[512,256]{1,0:T(8,128)(2,1)S(1)}, u32[]{:S(2)}, u32[]{:S(2)}) %collective-permute-start.10) | collective-permute-done | bytes 262176 | tf_op jit(solution)/shard_map/ppermute | solution.py:23
  (61 shorter events, 3.8 us)
Async XLA Ops:
  0.0 9.2 %collective-permute-start = (bf16[512,256]{1,0:T(8,128)(2,1)}, bf16[512,256]{1,0:T(8,128)(2,1)S(1)}, u32[]{:S(2)}, u32[]{:S(2)}) collective-permute-start(bf16[512,256]{1,0:T(8,128)(2,1)} %own.1), channel_id=1, source_target_pairs={{0,2},{1,3},{2,0},{3,1},{4,6},{5,7},{6,4},{7,5},{8,10},{9,11},{10,... | collective-permute-start | bytes 786440 | tf_op jit(solution)/shard_map/ppermute | solution.py:23
  3.6 7.8 %collective-permute-start.1 = (bf16[512,256]{1,0:T(8,128)(2,1)}, bf16[512,256]{1,0:T(8,128)(2,1)S(1)}, u32[]{:S(2)}, u32[]{:S(2)}) collective-permute-start(bf16[512,256]{1,0:T(8,128)(2,1)} %own.1), channel_id=1, source_target_pairs={{0,1},{1,0},{2,3},{3,2},{4,5},{5,4},{6,7},{7,6},{8,9},{9,8},{10,11... | collective-permute-start | bytes 786440 | tf_op jit(solution)/shard_map/ppermute | solution.py:23
  4.5 1.4 %copy-start = (bf16[1024,3,256]{2,0,1:T(8,128)(2,1)S(1)}, bf16[1024,3,256]{2,0,1:T(8,128)(2,1)}, u32[]{:S(2)}) copy-start(bf16[1024,3,256]{2,0,1:T(8,128)(2,1)} %param.10) | copy-start | bytes 4718596
  5.9 0.9 %copy-start.1 = (bf16[512,256]{1,0:T(8,128)(2,1)S(1)}, bf16[512,256]{1,0:T(8,128)(2,1)}, u32[]{:S(2)}) copy-start(bf16[512,256]{1,0:T(8,128)(2,1)} %own.1) | copy-start | bytes 786436
  6.9 0.7 %copy-start.2 = (f32[16,256]{1,0:T(8,128)S(1)}, f32[16,256]{1,0:T(8,128)}, u32[]{:S(2)}) copy-start(f32[16,256]{1,0:T(8,128)} %rates.1) | copy-start | bytes 49156
  7.6 0.7 %copy-start.3 = (f32[3,3,256]{2,1,0:T(4,128)S(1)}, f32[3,3,256]{2,1,0:T(4,128)}, u32[]{:S(2)}) copy-start(f32[3,3,256]{2,1,0:T(4,128)} %taps.1) | copy-start | bytes 27652
  8.3 0.7 %copy-start.4 = (f32[1024]{0:T(1024)S(1)}, f32[1024]{0:T(1024)}, u32[]{:S(2)}) copy-start(f32[1024]{0:T(1024)} %param.9) | copy-start | bytes 12292
  9.2 3.3 %collective-permute-start.2 = (bf16[512,256]{1,0:T(8,128)(2,1)S(1)}, bf16[512,256]{1,0:T(8,128)(2,1)S(1)}, u32[]{:S(2)}, u32[]{:S(2)}) collective-permute-start(bf16[512,256]{1,0:T(8,128)(2,1)S(1)} %collective-permute-done.far), channel_id=1, source_target_pairs={{0,1},{1,0},{2,3},{3,2},{4,5},{5,4},{6,7},{7,6},{8,9},{9,8},{10,11... | collective-permute-start | bytes 786440 | tf_op jit(solution)/shard_map/ppermute | solution.py:23
  15.3 22.8 %copy-start.6 = (f32[16,256]{1,0:T(8,128)S(1)}, f32[16,256]{1,0:T(8,128)}, u32[]{:S(2)}) copy-start(f32[16,256]{1,0:T(8,128)} %residues.3) | copy-start | bytes 49156
  15.3 22.8 %copy-start.7 = (f32[256]{0:T(256)S(1)}, f32[256]{0:T(256)}, u32[]{:S(2)}) copy-start(f32[256]{0:T(256)} %param.14) | copy-start | bytes 3076
  15.3 2.9 %collective-permute-start.3 = (f32[32,256]{1,0:T(8,128)S(1)}, f32[32,256]{1,0:T(8,128)S(1)}, u32[]{:S(2)}, u32[]{:S(2)}) collective-permute-start(f32[32,256]{1,0:T(8,128)S(1)} %get-tuple-element.38), channel_id=1, source_target_pairs={{0,4},{4,0},{8,12},{12,8},{16,20},{20,16},{24,28},{28,24},{32,36},... | collective-permute-start | bytes 98312 | tf_op jit(solution)/shard_map/ppermute | solution.py:27
  18.3 4.1 %collective-permute-start.4 = (f32[32,256]{1,0:T(8,128)S(1)}, f32[32,256]{1,0:T(8,128)S(1)}, u32[]{:S(2)}, u32[]{:S(2)}) collective-permute-start(f32[32,256]{1,0:T(8,128)S(1)} %pad_maximum_fusion), channel_id=1, source_target_pairs={{0,12},{4,8},{8,4},{12,0},{16,28},{20,24},{24,20},{28,16},{32,44},... | collective-permute-start | bytes 98312 | tf_op jit(solution)/shard_map/ppermute | solution.py:27
  22.4 3.0 %collective-permute-start.5 = (f32[32,256]{1,0:T(8,128)S(1)}, f32[32,256]{1,0:T(8,128)S(1)}, u32[]{:S(2)}, u32[]{:S(2)}) collective-permute-start(f32[32,256]{1,0:T(8,128)S(1)} %pad_maximum_fusion.1), channel_id=1, source_target_pairs={{0,16},{4,20},{8,24},{12,28},{16,0},{20,4},{24,8},{28,12},{32,48},... | collective-permute-start | bytes 98312 | tf_op jit(solution)/shard_map/ppermute | solution.py:27
  25.6 4.4 %collective-permute-start.6 = (f32[32,256]{1,0:T(8,128)S(1)}, f32[32,256]{1,0:T(8,128)S(1)}, u32[]{:S(2)}, u32[]{:S(2)}) collective-permute-start(f32[32,256]{1,0:T(8,128)S(1)} %pad_maximum_fusion.2), channel_id=1, source_target_pairs={{0,32},{4,36},{8,40},{12,44},{16,48},{20,52},{24,56},{28,60},{32,0... | collective-permute-start | bytes 98312 | tf_op jit(solution)/shard_map/ppermute | solution.py:27
  30.1 6.6 %collective-permute-start.7 = (f32[32,256]{1,0:T(8,128)S(1)}, f32[32,256]{1,0:T(8,128)S(1)}, u32[]{:S(2)}, u32[]{:S(2)}) collective-permute-start(f32[32,256]{1,0:T(8,128)S(1)} %pad_maximum_fusion.3), channel_id=1, source_target_pairs={{0,96},{4,100},{8,104},{12,108},{16,112},{20,116},{24,120},{28,124... | collective-permute-start | bytes 98312 | tf_op jit(solution)/shard_map/ppermute | solution.py:27
  36.8 2.9 %collective-permute-start.8 = (f32[32,256]{1,0:T(8,128)S(1)}, f32[32,256]{1,0:T(8,128)S(1)}, u32[]{:S(2)}, u32[]{:S(2)}) collective-permute-start(f32[32,256]{1,0:T(8,128)S(1)} %pad_maximum_fusion.4), channel_id=1, source_target_pairs={{0,128},{4,132},{8,136},{12,140},{16,144},{20,148},{24,152},{28,15... | collective-permute-start | bytes 98312 | tf_op jit(solution)/shard_map/ppermute | solution.py:27
  38.1 1.7 %copy-start.5 = (bf16[256,1024]{1,0:T(8,128)(2,1)S(1)}, bf16[256,1024]{1,0:T(8,128)(2,1)}, u32[]{:S(2)}) copy-start(bf16[256,1024]{1,0:T(8,128)(2,1)} %w_out.1) | copy-start | bytes 1572868
  41.2 8.6 %collective-permute-start.9 = (bf16[2,512,256]{2,1,0:T(8,128)(2,1)S(1)}, bf16[2,512,256]{2,1,0:T(8,128)(2,1)S(1)}, u32[]{:S(2)}, u32[]{:S(2)}) collective-permute-start(bf16[2,512,256]{2,1,0:T(8,128)(2,1)S(1)} %get-tuple-element.40), channel_id=1, source_target_pairs={{0,1},{1,0},{2,3},{3,2},{4,5},{5,4},{6,7},{7,6},{8,9},{9,8},{10,11... | collective-permute-start | bytes 1572872 | tf_op jit(solution)/shard_map/ppermute | solution.py:23
  49.9 9.1 %collective-permute-start.10 = (bf16[512,256]{1,0:T(8,128)(2,1)S(1)}, bf16[512,256]{1,0:T(8,128)(2,1)S(1)}, u32[]{:S(2)}, u32[]{:S(2)}) collective-permute-start(bf16[512,256]{1,0:T(8,128)(2,1)S(1)} %fusion.2), channel_id=1, source_target_pairs={{0,2},{1,3},{2,0},{3,1},{4,6},{5,7},{6,4},{7,5},{8,10},{9,11},{10,... | collective-permute-start | bytes 786440 | tf_op jit(solution)/shard_map/ppermute | solution.py:23

commit v3 on v2

--- a/solution.py
+++ b/solution.py
@@ -16,7 +16,8 @@
 SCAN_VMEM = 8 * 1024 * 1024
 BACK_VMEM = 12 * 1024 * 1024
 
-SCAN_MASKS = (1, 3, 4, 8, 24, 32)
+SCAN_FIRST = ((1,), (3,))
+SCAN_LATER = ((4, 8, 12), (24,), (32,))
 
 
 def ch_swap(array, mask):
@@ -126,8 +127,12 @@
             message[pl.ds(to + 1, 1), lanes] = t[2] * p[3]
 
 
-def scan_kernel(gated, rates, residues, skip, local, carry):
+def scan_kernel(queries, gated, rates, residues, skip, w_out, local, pack):
     rows, width = gated.shape
+    other = 1 - jnp.right_shift(lax.axis_index("ch"), 1)
+    for column in range(2):
+        start = pl.multiple_of((2 * other + column) * width, width)
+        pack[2, column * width : (column + 1) * width, :] = w_out[:, pl.ds(start, width)]
     span = rows // SUBS
     modes = rates.shape[0]
     sub = lax.broadcasted_iota(jnp.int32, (SUBS, LANES), 0)
@@ -146,85 +151,122 @@
             return state
 
         state = lax.fori_loop(0, span, step, [jnp.zeros((SUBS, LANES), F32)] * modes, unroll=8)
+        brought = []
         for m in range(modes):
             upto = state[m]
             for reach in (1, 2, 4):
                 moved = pltpu.roll(upto, reach, 0) * jnp.exp(rate[m] * (-float(span * reach)))
                 upto = upto + jnp.where(sub >= reach, moved, 0.0)
-            carry[m, :, lanes] = jnp.where(sub >= 1, pltpu.roll(upto, 1, 0), 0.0)
-
-
-def back_kernel(
-    queries, local, carry, entry, fix, rates, residues, skip, w_out, kept, sent, mixed
-):
+            brought.append(weight[m] * decay[m] * jnp.where(sub >= 1, pltpu.roll(upto, 1, 0), 0.0))
+
+        def add(index, held):
+            both = []
+            for half in range(2):
+                at = pl.ds(pl.multiple_of((2 * index + half) * SUBS, SUBS), SUBS)
+                both.append(tree_sum(list(held) + [local[at, lanes]]))
+                local[at, lanes] = both[-1]
+                held = [decay[m] * held[m] for m in range(modes)]
+            at = pl.ds(pl.multiple_of(index * 2 * SUBS, 2 * SUBS), 2 * SUBS)
+            pack[0, at, lanes] = queries[at, lanes].astype(BF16)
+            pack[1, at, lanes] = jnp.concatenate(both, axis=0).astype(BF16)
+            return held
+
+        lax.fori_loop(0, span // 2, add, brought, unroll=2)
+
+
+def mix(read, entry, mixed):
+    tiles, rows = mixed.shape[:2]
+    span = rows // SUBS
+    modes = (entry.shape[0] - SUBS) // 2
+    sub = lax.broadcasted_iota(jnp.int32, (SUBS, LANES), 0)
+    for tile in range(tiles):
+        lanes = pl.ds(tile * LANES, LANES)
+        rate = [row(entry, modes + SUBS + m, lanes) for m in range(modes)]
+        decay = [jnp.exp(-r) for r in rate]
+        state = [jnp.exp(rate[m] * sub.astype(F32) * (-float(span))) * row(entry, m, lanes) for m in range(modes)]
+
+        def pair(index, held, more=None):
+            at = pl.ds(pl.multiple_of(index * 2 * SUBS, 2 * SUBS), 2 * SUBS)
+            query, value = read(at, lanes)
+            for half in range(2):
+                v, q = value[half * SUBS : (half + 1) * SUBS], query[half * SUBS : (half + 1) * SUBS]
+                if more is not None:
+                    v = v + jnp.where(sub == 0, more[half], 0.0)
+                    q = q + jnp.where(sub == 0, more[2 + half], 0.0)
+                token = 2 * index + half
+                mixed[tile, pl.ds(token, SUBS, stride=span), :] = q * tree_sum(list(held) + [v])
+                held = [decay[m] * held[m] for m in range(modes)]
+            return held
+
+        state = pair(0, state, [row(entry, modes + i, lanes) for i in range(4)])
+        lax.fori_loop(1, span // 2, pair, state, unroll=2)
+    return jnp.concatenate([mixed[tile] for tile in range(tiles)], axis=1).astype(BF16)
+
+
+def near_kernel(queries, local, entry, w_out, share, mixed):
     me = lax.axis_index("ch")
-    rows, width = queries.shape
-    span = rows // SUBS
+    chip, core = jnp.right_shift(me, 1), jnp.bitwise_and(me, 1)
+    width = queries.shape[1]
+    part = mix(lambda at, lanes: (queries[at, lanes], local[at, lanes]), entry, mixed)
+    for slot, column in enumerate((1 - core, core)):
+        start = pl.multiple_of((2 * chip + column) * width, width)
+        share[slot] = jnp.dot(part, w_out[:, pl.ds(start, width)], preferred_element_type=F32)
+
+
+def far_kernel(pack, entry, share, kept, sent, mixed):
+    core = jnp.bitwise_and(lax.axis_index("ch"), 1)
+    width = pack.shape[2]
+    part = mix(lambda at, lanes: (pack[0, at, lanes].astype(F32), pack[1, at, lanes].astype(F32)), entry, mixed)
+    for slot, (target, column) in enumerate(((sent, 1 - core), (kept, core))):
+        start = pl.multiple_of(column * width, width)
+        total = share[slot] + jnp.dot(part, pack[2, pl.ds(start, width), :], preferred_element_type=F32)
+        target[...] = total.astype(target.dtype)
+
+
+def join(first, second, rates, rows):
     modes = rates.shape[0]
-    sub = lax.broadcasted_iota(jnp.int32, (SUBS, LANES), 0)
-    for lane in range(0, width, LANES):
-        lanes = pl.ds(lane, LANES)
-        rate = [row(rates, m, lanes) for m in range(modes)]
-        decay = [jnp.exp(-r) for r in rate]
-        state, lead = [], []
-        for m in range(modes):
-            weight = row(residues, m, lanes) * jnp.sqrt(rate[m])
-            entering = carry[m, :, lanes]
-            entering = entering + jnp.exp(rate[m] * sub.astype(F32) * (-float(span))) * row(entry, m, lanes)
-            state.append(weight * decay[m] * entering)
-            lead.append(weight * jnp.exp(rate[m]))
-
-        def token(index, held, more_local=None, more_query=None):
-            at = pl.ds(pl.multiple_of(index * SUBS, SUBS), SUBS)
-            value, query = local[at, lanes], queries[at, lanes]
-            if more_local is not None:
-                value = value + jnp.where(sub == 0, more_local, 0.0)
-                query = query + jnp.where(sub == 0, more_query, 0.0)
-            mixed[lane // LANES, pl.ds(index, SUBS, stride=span), :] = query * tree_sum(list(held) + [value])
-            return [decay[m] * held[m] for m in range(modes)]
-
-        skip_row = row(skip, 0, lanes)
-        more = [row(fix, i, lanes) for i in range(4)]
-        state = token(0, state, skip_row * more[0] - tree_sum(lead) * more[1], more[2])
-        state = token(1, state, skip_row * more[1], more[3])
-        lax.fori_loop(2, span, token, state, unroll=2)
-    mixed_in = jnp.concatenate([mixed[tile] for tile in range(width // LANES)], axis=1).astype(BF16)
-    for order in range(4):
-        start = pl.multiple_of(jnp.bitwise_xor(me, order) * width, width)
-        share = jnp.dot(mixed_in, w_out[:, pl.ds(start, width)], preferred_element_type=F32)
-        if order % 2 == 0:
-            kept[order // 2] = share
-        else:
-            sent[order // 2] = share.astype(BF16)
-
-
-def scan_blocks(message, rates, rows):
+    start = second[modes : modes + SUBS]
+    end = first[modes + SUBS :]
+    added = start[0:2] * end[2:4] + end[0:2] * (start[2:4] + end[2:4])
+    entering = first[:modes] + jnp.exp(rates) * added[0:1] + jnp.exp(2.0 * rates) * added[1:2]
+    state = jnp.exp(-rates * float(rows)) * entering + second[:modes]
+    both = jnp.concatenate([state, first[modes : modes + SUBS], second[modes + SUBS :]], axis=0)
+    return both, entering, jnp.concatenate([added, end[4:6]], axis=0)
+
+
+def scan_blocks(held, rates, rows, steps, level):
     block = lax.axis_index("seq")
     rounds = lax.axis_size("seq").bit_length() - 1
-    modes = rates.shape[0]
-    back_one, back_two = jnp.exp(rates), jnp.exp(2.0 * rates)
-    entry = jnp.zeros_like(rates)
-    fix = jnp.zeros((4,) + rates.shape[1:], F32)
-    for level in range(rounds):
-        other = seq_swap(message, SCAN_MASKS[level])
+    message, entry, fix = held
+
+    def place(level):
         upper = jnp.bitwise_and(jnp.right_shift(block, level), 1) == 1
         ahead = jnp.bitwise_and(block, (1 << level) - 1)
-        decay_ahead = jnp.exp(-rates * (ahead.astype(F32) * float(rows)))
-        across = jnp.exp(-rates * float(rows << level))
-        first = jnp.where(upper, other, message)
-        second = jnp.where(upper, message, other)
-        start = second[modes : modes + SUBS]
-        end = first[modes + SUBS :]
-        added = start[0:2] * end[2:4] + end[0:2] * (start[2:4] + end[2:4])
-        joined = first[:modes] + back_one * added[0:1] + back_two * added[1:2]
-        entry = jnp.where(upper, entry + decay_ahead * joined, entry)
-        fix = jnp.where(
-            jnp.logical_and(upper, ahead == 0), jnp.concatenate([added, end[4:6]], axis=0), fix
-        )
-        message = jnp.concatenate(
-            [across * joined + second[:modes], first[modes : modes + SUBS], second[modes + SUBS :]], axis=0
-        )
-    return entry, fix
+        return upper, ahead
+
+    def ordered(upper, mine, other):
+        return jnp.where(upper, other, mine), jnp.where(upper, mine, other)
+
+    def enter(level, entry, fix, entering, added):
+        upper, ahead = place(level)
+        decay = jnp.exp(-rates * (ahead.astype(F32) * float(rows)))
+        entry = jnp.where(upper, entry + decay * entering, entry)
+        return entry, jnp.where(jnp.logical_and(upper, ahead == 0), added, fix)
+
+    for masks in steps:
+        if level >= rounds:
+            break
+        others = [seq_swap(message, mask) for mask in masks]
+        upper, _ = place(level)
+        message, entering, added = join(*ordered(upper, message, others[0]), rates, rows << level)
+        entry, fix = enter(level, entry, fix, entering, added)
+        if len(masks) == 3:
+            pair, _, _ = join(*ordered(upper, others[1], others[2]), rates, rows << level)
+            upper, _ = place(level + 1)
+            message, entering, added = join(*ordered(upper, message, pair), rates, rows << (level + 1))
+            entry, fix = enter(level + 1, entry, fix, entering, added)
+        level += 1 if len(masks) == 1 else 2
+    return message, entry, fix
 
 
 def body(tokens, norm_gain, w_in, short_filter, rates, residues, skip_gain, w_out):
@@ -262,38 +304,65 @@
         compiler_params=pltpu.CompilerParams(vmem_limit_bytes=FRONT_VMEM),
         cost_estimate=pl.CostEstimate(flops=900_000_000, bytes_accessed=4_000_000, transcendentals=0),
         name="front",
-    )(
-        own_v, far, side, side_far, gain_v, w_in_v, taps_v, rates_v,
-    )
-    local, carry = pl.pallas_call(
+    )(own_v, far, side, side_far, gain_v, w_in_v, taps_v, rates_v)
+    local, pack = pl.pallas_call(
         scan_kernel,
         out_shape=(
             jax.ShapeDtypeStruct((rows, channels), F32),
-            jax.ShapeDtypeStruct((modes, SUBS, channels), F32),
+            jax.ShapeDtypeStruct((3, rows, channels), BF16),
         ),
-        in_specs=vmem_specs(4),
+        in_specs=vmem_specs(6),
         out_specs=tuple(vmem_specs(2)),
         compiler_params=pltpu.CompilerParams(vmem_limit_bytes=SCAN_VMEM),
         cost_estimate=pl.CostEstimate(flops=2_000_000_000, bytes_accessed=1_000_000, transcendentals=0),
         name="scan",
-    )(gated, rates_v, residues, skip)
-    entry, fix = scan_blocks(message, rates_v, rows)
+    )(queries, gated, rates_v, residues, skip, w_out)
+    held = (message, jnp.zeros_like(rates_v), jnp.zeros((4, channels), F32))
+    held = scan_blocks(held, rates_v, rows, SCAN_FIRST[:1], 0)
+    held, local, pack = lax.optimization_barrier((held, local, pack))
+    pack_far = ch_swap(pack, 2)
+    held = scan_blocks(held, rates_v, rows, SCAN_FIRST[1:], 1)
+    once = jnp.minimum(lax.axis_index("seq") + 1, 1)
+    held = lax.fori_loop(0, once, lambda _, now: scan_blocks(now, rates_v, rows, SCAN_LATER, len(SCAN_FIRST)), held)
+    (_, entry, fix), pack_far = lax.optimization_barrier((held, pack_far))
+    weight = residues * jnp.sqrt(rates_v)
+    lead = jnp.sum(weight * jnp.exp(rates_v), axis=0, keepdims=True)
+    entry = jnp.concatenate(
+        [
+            weight * jnp.exp(-rates_v) * entry,
+            skip * fix[0:1] - lead * fix[1:2],
+            skip * fix[1:2],
+            fix[2:4],
+            jnp.zeros_like(fix),
+            rates_v,
+        ],
+        axis=0,
+    )
+    entry_far = ch_swap(entry, 2)
+    share = pl.pallas_call(
+        near_kernel,
+        out_shape=jax.ShapeDtypeStruct((2, rows, width), F32),
+        in_specs=vmem_specs(4),
+        out_specs=vmem_specs(1)[0],
+        scratch_shapes=[pltpu.VMEM((channels // LANES, rows, LANES), F32)],
+        compiler_params=pltpu.CompilerParams(vmem_limit_bytes=BACK_VMEM),
+        cost_estimate=pl.CostEstimate(flops=900_000_000, bytes_accessed=4_000_000, transcendentals=0),
+        name="near",
+    )(queries, local, entry, w_out)
     kept, sent = pl.pallas_call(
-        back_kernel,
+        far_kernel,
         out_shape=(
-            jax.ShapeDtypeStruct((2, rows, width), F32),
-            jax.ShapeDtypeStruct((2, rows, width), BF16),
+            jax.ShapeDtypeStruct((rows, width), F32),
+            jax.ShapeDtypeStruct((rows, width), BF16),
         ),
-        in_specs=vmem_specs(9),
+        in_specs=vmem_specs(3),
         out_specs=tuple(vmem_specs(2)),
         scratch_shapes=[pltpu.VMEM((channels // LANES, rows, LANES), F32)],
         compiler_params=pltpu.CompilerParams(vmem_limit_bytes=BACK_VMEM),
         cost_estimate=pl.CostEstimate(flops=900_000_000, bytes_accessed=4_000_000, transcendentals=0),
-        name="back",
-    )(queries, local, carry, entry, fix, rates_v, residues, skip, w_out)
-    both = kept + ch_swap(sent, 1).astype(F32)
-    away = ch_swap(both[1].astype(BF16), 2)
-    return (both[0] + away.astype(F32)).astype(BF16)
+        name="far",
+    )(pack_far, entry_far, share)
+    return (kept + ch_swap(sent, 1).astype(F32)).astype(BF16)
 
 
 def solution(mesh):

time: 60.1 us -> 55.6 us (0.925)
  starting transfers between devices: 32 us -> 28.2 us
  waiting for transfers between devices: 15.9 us -> 13.4 us
  Pallas kernels: 5.82 us -> 7.42 us
    ppermute x5 -> x6, waiting for transfers between devices: 8.97 us -> 4.24 us  [ch_swap(): lax.ppermute(array, 'ch', [(i, i ^ mask) for i in range(lax.axis_size('ch...]
    ppermute x6 -> x7, starting transfers between devices: 15.5 us -> 11.7 us  [seq_swap(): lax.ppermute(array, 'seq', [(i, i ^ mask) for i in range(lax.axis_size('s...]
    ppermute x6 -> x7, waiting for transfers between devices: 6.91 us -> 9.15 us  [seq_swap(): lax.ppermute(array, 'seq', [(i, i ^ mask) for i in range(lax.axis_size('s...]
    pallas_call x1 -> x2, Pallas kernels: 1.42 us -> 2.26 us  [the longest x1 1.14 us: body(): pl.pallas_call(far_kernel, out_shape=(jax.ShapeDtypeStruct((rows, width),...]
    pallas_call x1, Pallas kernels: 1.39 us -> 2.14 us  [body(): pl.pallas_call(scan_kernel, out_shape=(jax.ShapeDtypeStruct((rows, channe...]
    ppermute x5 -> x6, starting transfers between devices: 16.5 us -> 16.5 us  [ch_swap(): lax.ppermute(array, 'ch', [(i, i ^ mask) for i in range(lax.axis_size('ch...]
    unnamed x16 -> x20, local copies, waits for them, and re-layouts: 4.48 us -> 4.49 us
  transfers between devices with their start and end apart: 11 -> 13, of which waited for: 9 -> 7; matrix products, arithmetic and copies ran while one was open for 0% -> 1% of each run, Pallas kernels for 3% -> 6%
where the time goes in v3:
time: 55.6 us; the launch traced here: 55.3 us
  starting transfers between devices  28.2 us (51%)
  waiting for transfers between devices  13.4 us (24%)
  Pallas kernels  7.42 us (13%)
  local copies, waits for them, and re-layouts  4.59 us (8%)
  other arithmetic  1.17 us (2%)
    ppermute x6, starting transfers between devices, ch_swap(): lax.ppermute(array, 'ch', [(i, i ^ mask) for i in range(lax.axis_size('ch...  16.5 us
    ppermute x7, starting transfers between devices, seq_swap(): lax.ppermute(array, 'seq', [(i, i ^ mask) for i in range(lax.axis_size('s...  11.7 us
    ppermute x7, waiting for transfers between devices, seq_swap(): lax.ppermute(array, 'seq', [(i, i ^ mask) for i in range(lax.axis_size('s...  9.15 us
    unnamed x20, local copies, waits for them, and re-layouts  4.49 us
    ppermute x6, waiting for transfers between devices, ch_swap(): lax.ppermute(array, 'ch', [(i, i ^ mask) for i in range(lax.axis_size('ch...  4.24 us
    pallas_call x1, Pallas kernels, body(): pl.pallas_call(front_kernel, out_shape=(jax.ShapeDtypeStruct((rows, chann...  2.81 us
    pallas_call x1, Pallas kernels, body(): pl.pallas_call(scan_kernel, out_shape=(jax.ShapeDtypeStruct((rows, channe...  2.14 us
    pallas_call x1, Pallas kernels, body(): pl.pallas_call(far_kernel, out_shape=(jax.ShapeDtypeStruct((rows, width),...  1.14 us
  transfers between devices with their start and end apart: 13, of which 7 were waited for; matrix products, arithmetic and copies ran while one was open for 1% of the time, Pallas kernels for 6%

profile of v3, /device:TPU:1, one launch (start us, length us, event | category | flops | bytes accessed | tf_op | source)
XLA Modules:
  0.0 55.3 jit_solution(2267484553218058148)
XLA Ops:
  0.0 3.6 %collective-permute-start.5 = (bf16[512,256]{1,0:T(8,128)(2,1)}, bf16[512,256]{1,0:T(8,128)(2,1)S(1)}, u32[]{:S(2)}, u32[]{:S(2)}) collective-permute-start(bf16[512,256]{1,0:T(8,128)(2,1)} %own.1), channel_id=1, source_target_pairs={{0,2},{1,3},{2,0},{3,1},{4,6},{5,7},{6,4},{7,5},{8,10},{9,11},{10,... | collective-permute-start | bytes 786440 | tf_op jit(solution)/shard_map/ppermute | solution.py:24
  3.6 1.0 %collective-permute-start.6 = (bf16[512,256]{1,0:T(8,128)(2,1)}, bf16[512,256]{1,0:T(8,128)(2,1)S(1)}, u32[]{:S(2)}, u32[]{:S(2)}) collective-permute-start(bf16[512,256]{1,0:T(8,128)(2,1)} %own.1), channel_id=1, source_target_pairs={{0,1},{1,0},{2,3},{3,2},{4,5},{5,4},{6,7},{7,6},{8,9},{9,8},{10,11... | collective-permute-start | bytes 786440 | tf_op jit(solution)/shard_map/ppermute | solution.py:24
  4.5 1.4 %copy-done = bf16[1024,3,256]{2,0,1:T(8,128)(2,1)S(1)} copy-done((bf16[1024,3,256]{2,0,1:T(8,128)(2,1)S(1)}, bf16[1024,3,256]{2,0,1:T(8,128)(2,1)}, u32[]{:S(2)}) %copy-start) | copy-done | bytes 1572888
  5.9 0.9 %copy-done.1 = bf16[512,256]{1,0:T(8,128)(2,1)S(1)} copy-done((bf16[512,256]{1,0:T(8,128)(2,1)S(1)}, bf16[512,256]{1,0:T(8,128)(2,1)}, u32[]{:S(2)}) %copy-start.1) | copy-done | bytes 262168
  9.2 2.1 %collective-permute-start.7 = (bf16[512,256]{1,0:T(8,128)(2,1)S(1)}, bf16[512,256]{1,0:T(8,128)(2,1)S(1)}, u32[]{:S(2)}, u32[]{:S(2)}) collective-permute-start(bf16[512,256]{1,0:T(8,128)(2,1)S(1)} %collective-permute-done.5.far), channel_id=1, source_target_pairs={{0,1},{1,0},{2,3},{3,2},{4,5},{5,4},{6,7},{7,6},{8,9},{9,8},{10,11... | collective-permute-start | bytes 786440 | tf_op jit(solution)/shard_map/ppermute | solution.py:24
  11.3 1.1 %collective-permute-done.7.side_far = bf16[512,256]{1,0:T(8,128)(2,1)S(1)} collective-permute-done((bf16[512,256]{1,0:T(8,128)(2,1)S(1)}, bf16[512,256]{1,0:T(8,128)(2,1)S(1)}, u32[]{:S(2)}, u32[]{:S(2)}) %collective-permute-start.7) | collective-permute-done | bytes 262176 | tf_op jit(solution)/shard_map/ppermute | solution.py:24
  12.5 2.8 %front.1 = (f32[512,256]{1,0:T(8,128)S(1)}, f32[512,256]{1,0:T(8,128)S(1)}, f32[32,256]{1,0:T(8,128)S(1)}) custom-call(bf16[512,256]{1,0:T(8,128)(2,1)S(1)} %get-tuple-element.104.own, bf16[512,256]{1,0:T(8,128)(2,1)S(1)} %collective-permute-done.5.far, bf16[512,256]{1,0:T(8,128)(2,1)S(1)} %collective-permute-done.6.side, ...), custom_call_target="tpu_custom_call" | custom-call | flops 900000000 | bytes 4000000 | tf_op jit(solution)/shard_map/front/pallas_call | solution.py:294
  15.3 1.3 %collective-permute-start.8 = (f32[32,256]{1,0:T(8,128)S(1)}, f32[32,256]{1,0:T(8,128)S(1)}, u32[]{:S(2)}, u32[]{:S(2)}) collective-permute-start(f32[32,256]{1,0:T(8,128)S(1)} %get-tuple-element.109), channel_id=1, source_target_pairs={{0,4},{4,0},{8,12},{12,8},{16,20},{20,16},{24,28},{28,24},{32,36},... | collective-permute-start | bytes 98312 | tf_op jit(solution)/shard_map/ppermute | solution.py:28
  16.7 2.1 %scan.1 = (f32[512,256]{1,0:T(8,128)S(1)}, bf16[3,512,256]{2,1,0:T(8,128)(2,1)S(1)}) custom-call(f32[512,256]{1,0:T(8,128)S(1)} %get-tuple-element.110.queries, f32[512,256]{1,0:T(8,128)S(1)} %get-tuple-element.111.gated, f32[16,256]{1,0:T(8,128)S(1)} %get-tuple-element.332.rates, f32[16,256]{1,0:T(8,128)S(1)} %copy-done.3, f32[1,256]{1,0:T(1,128)S(1)} %bitcast.40, ...), custom_call_target="tpu_custom_call" | custom-call | flops 2000000000 | bytes 1000000 | tf_op jit(solution)/shard_map/scan/pallas_call | solution.py:308
  18.9 2.1 %collective-permute-start.9 = (f32[32,256]{1,0:T(8,128)S(1)}, f32[32,256]{1,0:T(8,128)S(1)}, u32[]{:S(2)}, u32[]{:S(2)}) collective-permute-start(f32[32,256]{1,0:T(8,128)S(1)} %pad_maximum_fusion.5), channel_id=1, source_target_pairs={{0,12},{4,8},{8,4},{12,0},{16,28},{20,24},{24,20},{28,16},{32,44},... | collective-permute-start | bytes 98312 | tf_op jit(solution)/shard_map/ppermute | solution.py:28
  21.1 2.7 %collective-permute-start.10 = (bf16[3,512,256]{2,1,0:T(8,128)(2,1)S(1)}, bf16[3,512,256]{2,1,0:T(8,128)(2,1)S(1)}, u32[]{:S(2)}, u32[]{:S(2)}) collective-permute-start(bf16[3,512,256]{2,1,0:T(8,128)(2,1)S(1)} %get-tuple-element.119), channel_id=1, source_target_pairs={{0,2},{1,3},{2,0},{3,1},{4,6},{5,7},{6,4},{7,5},{8,10},{9,11},{10,... | collective-permute-start | bytes 2359304 | tf_op jit(solution)/shard_map/ppermute | solution.py:24
  23.9 18.0 %while.15 = (s32[]{:T(128)}, f32[32,256]{1,0:T(8,128)S(1)}, f32[16,256]{1,0:T(8,128)S(1)}, f32[4,256]{1,0:T(4,128)S(1)}, s32[]{:T(128)}, /*index=5*/f32[16,256]{...) while((s32[]{:T(128)}, f32[32,256]{1,0:T(8,128)S(1)}, ...), condition=%wide.region_1.2_spmd, body=%wide.region_0.1_spmd.sunk | while | flops 436261 | bytes 2417390 | solution.py:326
  23.9 4.4 %collective-permute-start.1 = (f32[32,256]{1,0:T(8,128)S(1)}, f32[32,256]{1,0:T(8,128)S(1)}, u32[]{:S(2)}, u32[]{:S(2)}) collective-permute-start(f32[32,256]{1,0:T(8,128)S(1)} %get-tuple-element.346), channel_id=1, source_target_pairs={{0,48},{4,52},{8,56},{12,60},{16,32},{20,36},{24,40},{28,44},{32,1... | collective-permute-start | bytes 98312 | tf_op jit(solution)/shard_map/while/body/ppermute | solution.py:28
  28.8 1.2 %collective-permute-done.1 = f32[32,256]{1,0:T(8,128)S(1)} collective-permute-done((f32[32,256]{1,0:T(8,128)S(1)}, f32[32,256]{1,0:T(8,128)S(1)}, u32[]{:S(2)}, u32[]{:S(2)}) %collective-permute-start.1) | collective-permute-done | bytes 32800 | tf_op jit(solution)/shard_map/while/body/ppermute | solution.py:28
  30.0 2.6 %collective-permute-done.2 = f32[32,256]{1,0:T(8,128)S(1)} collective-permute-done((f32[32,256]{1,0:T(8,128)S(1)}, f32[32,256]{1,0:T(8,128)S(1)}, u32[]{:S(2)}, u32[]{:S(2)}) %collective-permute-start.2) | collective-permute-done | bytes 32800 | tf_op jit(solution)/shard_map/while/body/ppermute | solution.py:28
  32.9 3.4 %collective-permute-start.3 = (f32[32,256]{1,0:T(8,128)S(1)}, f32[32,256]{1,0:T(8,128)S(1)}, u32[]{:S(2)}, u32[]{:S(2)}) collective-permute-start(f32[32,256]{1,0:T(8,128)S(1)} %pad_maximum_fusion.10), channel_id=1, source_target_pairs={{0,96},{4,100},{8,104},{12,108},{16,112},{20,116},{24,120},{28,124... | collective-permute-start | bytes 98312 | tf_op jit(solution)/shard_map/while/body/ppermute | solution.py:28
  36.2 1.9 %collective-permute-done.3 = f32[32,256]{1,0:T(8,128)S(1)} collective-permute-done((f32[32,256]{1,0:T(8,128)S(1)}, f32[32,256]{1,0:T(8,128)S(1)}, u32[]{:S(2)}, u32[]{:S(2)}) %collective-permute-start.3) | collective-permute-done | bytes 32800 | tf_op jit(solution)/shard_map/while/body/ppermute | solution.py:28
  38.4 3.4 %collective-permute-done.4 = f32[32,256]{1,0:T(8,128)S(1)} collective-permute-done((f32[32,256]{1,0:T(8,128)S(1)}, f32[32,256]{1,0:T(8,128)S(1)}, u32[]{:S(2)}, u32[]{:S(2)}) %collective-permute-start.4) | collective-permute-done | bytes 32800 | tf_op jit(solution)/shard_map/while/body/ppermute | solution.py:28
  42.1 1.6 %collective-permute-start.11 = (f32[40,256]{1,0:T(8,128)S(1)}, f32[40,256]{1,0:T(8,128)S(1)}, u32[]{:S(2)}, u32[]{:S(2)}) collective-permute-start(f32[40,256]{1,0:T(8,128)S(1)} %concatenate.55.entry), channel_id=1, source_target_pairs={{0,2},{1,3},{2,0},{3,1},{4,6},{5,7},{6,4},{7,5},{8,10},{9,11},{10,... | collective-permute-start | bytes 122888 | tf_op jit(solution)/shard_map/ppermute | solution.py:24
  43.7 1.1 %near.1.share = f32[2,512,256]{2,1,0:T(8,128)S(1)} custom-call(f32[512,256]{1,0:T(8,128)S(1)} %copy-done.9, f32[512,256]{1,0:T(8,128)S(1)} %get-tuple-element.123.local, f32[40,256]{1,0:T(8,128)S(1)} %concatenate.55.entry, bf16[256,1024]{1,0:T(8,128)(2,1)S(1)} %copy-done.7), custom_call_target="tpu_custom_call" | custom-call | flops 900000000 | bytes 4000000 | tf_op jit(solution)/shard_map/near/pallas_call | solution.py:342
  44.8 1.9 %collective-permute-done.11.entry = f32[40,256]{1,0:T(8,128)S(1)} collective-permute-done((f32[40,256]{1,0:T(8,128)S(1)}, f32[40,256]{1,0:T(8,128)S(1)}, u32[]{:S(2)}, u32[]{:S(2)}) %collective-permute-start.11) | collective-permute-done | bytes 40992 | tf_op jit(solution)/shard_map/ppermute | solution.py:24
  46.7 1.1 %far.1 = (f32[512,256]{1,0:T(8,128)S(1)}, bf16[512,256]{1,0:T(8,128)(2,1)S(1)}) custom-call(bf16[3,512,256]{2,1,0:T(8,128)(2,1)S(1)} %collective-permute-done.10.pack, f32[40,256]{1,0:T(8,128)S(1)} %collective-permute-done.11.entry, f32[2,512,256]{2,1,0:T(8,128)S(1)} %near.1.share), custom_call_target="tpu_custom_call" | custom-call | flops 900000000 | bytes 4000000 | tf_op jit(solution)/shard_map/far/pallas_call | solution.py:352
  47.9 5.5 %collective-permute-start.12 = (bf16[512,256]{1,0:T(8,128)(2,1)S(1)}, bf16[512,256]{1,0:T(8,128)(2,1)S(1)}, u32[]{:S(2)}, u32[]{:S(2)}) collective-permute-start(bf16[512,256]{1,0:T(8,128)(2,1)S(1)} %get-tuple-element.125), channel_id=1, source_target_pairs={{0,1},{1,0},{2,3},{3,2},{4,5},{5,4},{6,7},{7,6},{8,9},{9,8},{10,11... | collective-permute-start | bytes 786440 | tf_op jit(solution)/shard_map/ppermute | solution.py:24
  53.4 1.2 %collective-permute-done.12 = bf16[512,256]{1,0:T(8,128)(2,1)S(1)} collective-permute-done((bf16[512,256]{1,0:T(8,128)(2,1)S(1)}, bf16[512,256]{1,0:T(8,128)(2,1)S(1)}, u32[]{:S(2)}, u32[]{:S(2)}) %collective-permute-start.12) | collective-permute-done | bytes 262176 | tf_op jit(solution)/shard_map/ppermute | solution.py:24
  (84 shorter events, 4.1 us)
Async XLA Ops:
  0.0 9.2 %collective-permute-start.5 = (bf16[512,256]{1,0:T(8,128)(2,1)}, bf16[512,256]{1,0:T(8,128)(2,1)S(1)}, u32[]{:S(2)}, u32[]{:S(2)}) collective-permute-start(bf16[512,256]{1,0:T(8,128)(2,1)} %own.1), channel_id=1, source_target_pairs={{0,2},{1,3},{2,0},{3,1},{4,6},{5,7},{6,4},{7,5},{8,10},{9,11},{10,... | collective-permute-start | bytes 786440 | tf_op jit(solution)/shard_map/ppermute | solution.py:24
  3.6 7.8 %collective-permute-start.6 = (bf16[512,256]{1,0:T(8,128)(2,1)}, bf16[512,256]{1,0:T(8,128)(2,1)S(1)}, u32[]{:S(2)}, u32[]{:S(2)}) collective-permute-start(bf16[512,256]{1,0:T(8,128)(2,1)} %own.1), channel_id=1, source_target_pairs={{0,1},{1,0},{2,3},{3,2},{4,5},{5,4},{6,7},{7,6},{8,9},{9,8},{10,11... | collective-permute-start | bytes 786440 | tf_op jit(solution)/shard_map/ppermute | solution.py:24
  4.5 1.4 %copy-start = (bf16[1024,3,256]{2,0,1:T(8,128)(2,1)S(1)}, bf16[1024,3,256]{2,0,1:T(8,128)(2,1)}, u32[]{:S(2)}) copy-start(bf16[1024,3,256]{2,0,1:T(8,128)(2,1)} %param.12) | copy-start | bytes 4718596
  5.9 0.9 %copy-start.1 = (bf16[512,256]{1,0:T(8,128)(2,1)S(1)}, bf16[512,256]{1,0:T(8,128)(2,1)}, u32[]{:S(2)}) copy-start(bf16[512,256]{1,0:T(8,128)(2,1)} %own.1) | copy-start | bytes 786436
  6.9 0.7 %copy-start.2 = (f32[16,256]{1,0:T(8,128)S(1)}, f32[16,256]{1,0:T(8,128)}, u32[]{:S(2)}) copy-start(f32[16,256]{1,0:T(8,128)} %rates.1) | copy-start | bytes 49156
  7.6 0.7 %copy-start.4 = (f32[3,3,256]{2,1,0:T(4,128)S(1)}, f32[3,3,256]{2,1,0:T(4,128)}, u32[]{:S(2)}) copy-start(f32[3,3,256]{2,1,0:T(4,128)} %taps.1) | copy-start | bytes 27652
  8.3 0.7 %copy-start.5 = (f32[1024]{0:T(1024)S(1)}, f32[1024]{0:T(1024)}, u32[]{:S(2)}) copy-start(f32[1024]{0:T(1024)} %param.11) | copy-start | bytes 12292
  9.2 3.3 %collective-permute-start.7 = (bf16[512,256]{1,0:T(8,128)(2,1)S(1)}, bf16[512,256]{1,0:T(8,128)(2,1)S(1)}, u32[]{:S(2)}, u32[]{:S(2)}) collective-permute-start(bf16[512,256]{1,0:T(8,128)(2,1)S(1)} %collective-permute-done.5.far), channel_id=1, source_target_pairs={{0,1},{1,0},{2,3},{3,2},{4,5},{5,4},{6,7},{7,6},{8,9},{9,8},{10,11... | collective-permute-start | bytes 786440 | tf_op jit(solution)/shard_map/ppermute | solution.py:24
  11.3 5.3 %copy-start.3 = (f32[16,256]{1,0:T(8,128)S(1)}, f32[16,256]{1,0:T(8,128)}, u32[]{:S(2)}) copy-start(f32[16,256]{1,0:T(8,128)} %residues.1) | copy-start | bytes 49156
  11.3 5.3 %copy-start.6 = (f32[256]{0:T(256)S(1)}, f32[256]{0:T(256)}, u32[]{:S(2)}) copy-start(f32[256]{0:T(256)} %param.16) | copy-start | bytes 3076
  11.3 5.3 %copy-start.7 = (bf16[256,1024]{1,0:T(8,128)(2,1)S(1)}, bf16[256,1024]{1,0:T(8,128)(2,1)}, u32[]{:S(2)}) copy-start(bf16[256,1024]{1,0:T(8,128)(2,1)} %w_out.3) | copy-start | bytes 1572868
  15.3 3.5 %copy-start.8 = (f32[512,256]{1,0:T(8,128)}, f32[512,256]{1,0:T(8,128)S(1)}, u32[]{:S(2)}) copy-start(f32[512,256]{1,0:T(8,128)S(1)} %get-tuple-element.110.queries) | copy-start | bytes 1572868
  15.3 3.5 %collective-permute-start.8 = (f32[32,256]{1,0:T(8,128)S(1)}, f32[32,256]{1,0:T(8,128)S(1)}, u32[]{:S(2)}, u32[]{:S(2)}) collective-permute-start(f32[32,256]{1,0:T(8,128)S(1)} %get-tuple-element.109), channel_id=1, source_target_pairs={{0,4},{4,0},{8,12},{12,8},{16,20},{20,16},{24,28},{28,24},{32,36},... | collective-permute-start | bytes 98312 | tf_op jit(solution)/shard_map/ppermute | solution.py:28
  18.9 4.9 %collective-permute-start.9 = (f32[32,256]{1,0:T(8,128)S(1)}, f32[32,256]{1,0:T(8,128)S(1)}, u32[]{:S(2)}, u32[]{:S(2)}) collective-permute-start(f32[32,256]{1,0:T(8,128)S(1)} %pad_maximum_fusion.5), channel_id=1, source_target_pairs={{0,12},{4,8},{8,4},{12,0},{16,28},{20,24},{24,20},{28,16},{32,44},... | collective-permute-start | bytes 98312 | tf_op jit(solution)/shard_map/ppermute | solution.py:28
  21.1 20.9 %collective-permute-start.10 = (bf16[3,512,256]{2,1,0:T(8,128)(2,1)S(1)}, bf16[3,512,256]{2,1,0:T(8,128)(2,1)S(1)}, u32[]{:S(2)}, u32[]{:S(2)}) collective-permute-start(bf16[3,512,256]{2,1,0:T(8,128)(2,1)S(1)} %get-tuple-element.119), channel_id=1, source_target_pairs={{0,2},{1,3},{2,0},{3,1},{4,6},{5,7},{6,4},{7,5},{8,10},{9,11},{10,... | collective-permute-start | bytes 2359304 | tf_op jit(solution)/shard_map/ppermute | solution.py:24
  23.9 19.8 %copy-start.9 = (f32[512,256]{1,0:T(8,128)S(1)}, f32[512,256]{1,0:T(8,128)}, u32[]{:S(2)}) copy-start(f32[512,256]{1,0:T(8,128)} %copy-done.8) | copy-start | bytes 1572868
  23.9 6.0 %collective-permute-start.1 = (f32[32,256]{1,0:T(8,128)S(1)}, f32[32,256]{1,0:T(8,128)S(1)}, u32[]{:S(2)}, u32[]{:S(2)}) collective-permute-start(f32[32,256]{1,0:T(8,128)S(1)} %get-tuple-element.346), channel_id=1, source_target_pairs={{0,48},{4,52},{8,56},{12,60},{16,32},{20,36},{24,40},{28,44},{32,1... | collective-permute-start | bytes 98312 | tf_op jit(solution)/shard_map/while/body/ppermute | solution.py:28
  28.4 4.2 %collective-permute-start.2 = (f32[32,256]{1,0:T(8,128)S(1)}, f32[32,256]{1,0:T(8,128)S(1)}, u32[]{:S(2)}, u32[]{:S(2)}) collective-permute-start(f32[32,256]{1,0:T(8,128)S(1)} %get-tuple-element.346), channel_id=1, source_target_pairs={{0,32},{4,36},{8,40},{12,44},{16,48},{20,52},{24,56},{28,60},{32,0... | collective-permute-start | bytes 98312 | tf_op jit(solution)/shard_map/while/body/ppermute | solution.py:28
  28.4 4.3 %collective-permute-start = (f32[32,256]{1,0:T(8,128)S(1)}, f32[32,256]{1,0:T(8,128)S(1)}, u32[]{:S(2)}, u32[]{:S(2)}) collective-permute-start(f32[32,256]{1,0:T(8,128)S(1)} %get-tuple-element.346), channel_id=1, source_target_pairs={{0,16},{4,20},{8,24},{12,28},{16,0},{20,4},{24,8},{28,12},{32,48},... | collective-permute-start | bytes 98312 | tf_op jit(solution)/shard_map/while/body/ppermute | solution.py:28
  32.9 5.3 %collective-permute-start.3 = (f32[32,256]{1,0:T(8,128)S(1)}, f32[32,256]{1,0:T(8,128)S(1)}, u32[]{:S(2)}, u32[]{:S(2)}) collective-permute-start(f32[32,256]{1,0:T(8,128)S(1)} %pad_maximum_fusion.10), channel_id=1, source_target_pairs={{0,96},{4,100},{8,104},{12,108},{16,112},{20,116},{24,120},{28,124... | collective-permute-start | bytes 98312 | tf_op jit(solution)/shard_map/while/body/ppermute | solution.py:28
  38.2 3.6 %collective-permute-start.4 = (f32[32,256]{1,0:T(8,128)S(1)}, f32[32,256]{1,0:T(8,128)S(1)}, u32[]{:S(2)}, u32[]{:S(2)}) collective-permute-start(f32[32,256]{1,0:T(8,128)S(1)} %pad_maximum_fusion.11), channel_id=1, source_target_pairs={{0,128},{4,132},{8,136},{12,140},{16,144},{20,148},{24,152},{28,15... | collective-permute-start | bytes 98312 | tf_op jit(solution)/shard_map/while/body/ppermute | solution.py:28
  42.1 4.7 %collective-permute-start.11 = (f32[40,256]{1,0:T(8,128)S(1)}, f32[40,256]{1,0:T(8,128)S(1)}, u32[]{:S(2)}, u32[]{:S(2)}) collective-permute-start(f32[40,256]{1,0:T(8,128)S(1)} %concatenate.55.entry), channel_id=1, source_target_pairs={{0,2},{1,3},{2,0},{3,1},{4,6},{5,7},{6,4},{7,5},{8,10},{9,11},{10,... | collective-permute-start | bytes 122888 | tf_op jit(solution)/shard_map/ppermute | solution.py:24
  47.9 6.7 %collective-permute-start.12 = (bf16[512,256]{1,0:T(8,128)(2,1)S(1)}, bf16[512,256]{1,0:T(8,128)(2,1)S(1)}, u32[]{:S(2)}, u32[]{:S(2)}) collective-permute-start(bf16[512,256]{1,0:T(8,128)(2,1)S(1)} %get-tuple-element.125), channel_id=1, source_target_pairs={{0,1},{1,0},{2,3},{3,2},{4,5},{5,4},{6,7},{7,6},{8,9},{9,8},{10,11... | collective-permute-start | bytes 786440 | tf_op jit(solution)/shard_map/ppermute | solution.py:24

commit v4 on v3

--- a/solution.py
+++ b/solution.py
@@ -11,21 +11,39 @@
 LANES = 128
 SUBS = 8
 HALO = 16
-STAGE_VMEM = 2 * 1024 * 1024
-FRONT_VMEM = 16 * 1024 * 1024
-SCAN_VMEM = 8 * 1024 * 1024
-BACK_VMEM = 12 * 1024 * 1024
+STAGE_VMEM = 1024 * 1024
+FRONT_VMEM = 8 * 1024 * 1024
+SCAN_VMEM = 2 * 1024 * 1024
+BACK_VMEM = 4 * 1024 * 1024
 
 SCAN_FIRST = ((1,), (3,))
-SCAN_LATER = ((4, 8, 12), (24,), (32,))
+SCAN_LATER = ((4, 8, 12), (24,))
+SCAN_LAST = 32
+
+CROSSED = 0b101101
 
 
 def ch_swap(array, mask):
     return lax.ppermute(array, "ch", [(i, i ^ mask) for i in range(lax.axis_size("ch"))])
 
 
-def seq_swap(array, mask):
-    return lax.ppermute(array, "seq", [(i, i ^ mask) for i in range(lax.axis_size("seq"))])
+def crosses(mask):
+    return bin(mask & CROSSED).count("1") % 2
+
+
+def crossed(block):
+    bits = [jnp.right_shift(block, bit) for bit in range(CROSSED.bit_length()) if CROSSED >> bit & 1]
+    total = bits[0]
+    for bit in bits[1:]:
+        total = jnp.bitwise_xor(total, bit)
+    return jnp.bitwise_and(total, 1) == 1
+
+
+def seq_swap(array, mask, chip=0):
+    blocks, chs = lax.axis_size("seq"), lax.axis_size("ch")
+    turn = 2 * chip ^ crosses(mask)
+    pairs = [(chs * b + c, chs * (b ^ mask) + (c ^ turn)) for b in range(blocks) for c in range(chs)]
+    return lax.ppermute(array, ("seq", "ch"), pairs)
 
 
 def vmem_specs(count):
@@ -42,13 +60,24 @@
     return terms[0]
 
 
-def stage_kernel(own, w_in, taps, rates, gain, own_v, w_in_v, taps_v, rates_v, gain_v, sems):
-    pairs = ((own, own_v), (w_in, w_in_v), (taps, taps_v), (rates, rates_v), (gain, gain_v))
-    copies = [pltpu.make_async_copy(src, dst, sems.at[i]) for i, (src, dst) in enumerate(pairs)]
-    for copy in copies:
-        copy.start()
-    for copy in copies:
-        copy.wait()
+def stage_kernel(*refs):
+    (own, gain), pairs, targets, sems = refs[:2], refs[2:8], refs[8:13], refs[13]
+    swapped = crossed(lax.axis_index("seq"))
+
+    def copy_all(sources):
+        copies = [pltpu.make_async_copy(src, dst, sems.at[i]) for i, (src, dst) in enumerate(zip(sources, targets))]
+        for copy in copies:
+            copy.start()
+        for copy in copies:
+            copy.wait()
+
+    @pl.when(swapped)
+    def _():
+        copy_all((own, gain, *pairs[1::2]))
+
+    @pl.when(jnp.logical_not(swapped))
+    def _():
+        copy_all((own, gain, *pairs[::2]))
 
 
 def front_kernel(
@@ -127,21 +156,38 @@
             message[pl.ds(to + 1, 1), lanes] = t[2] * p[3]
 
 
-def scan_kernel(queries, gated, rates, residues, skip, w_out, local, pack):
+def scan_kernel(
+    queries, gated, rates, residues, residues_side, skip, skip_side, w_out, w_out_side, pack, extra, w_out_v, local
+):
     rows, width = gated.shape
+    modes = rates.shape[0]
+    swapped = crossed(lax.axis_index("seq"))
+
+    def keep(weights, direct, projection):
+        extra[:modes] = weights[...]
+        extra[modes:] = jnp.concatenate([direct[...], jnp.zeros((SUBS - 1, width), F32)], axis=0)
+        w_out_v[...] = projection[...]
+
+    @pl.when(swapped)
+    def _():
+        keep(residues_side, skip_side, w_out_side)
+
+    @pl.when(jnp.logical_not(swapped))
+    def _():
+        keep(residues, skip, w_out)
+
     other = 1 - jnp.right_shift(lax.axis_index("ch"), 1)
     for column in range(2):
         start = pl.multiple_of((2 * other + column) * width, width)
-        pack[2, column * width : (column + 1) * width, :] = w_out[:, pl.ds(start, width)]
+        pack[2, column * width : (column + 1) * width, :] = w_out_v[:, pl.ds(start, width)]
     span = rows // SUBS
-    modes = rates.shape[0]
     sub = lax.broadcasted_iota(jnp.int32, (SUBS, LANES), 0)
     for lane in range(0, width, LANES):
         lanes = pl.ds(lane, LANES)
         rate = [row(rates, m, lanes) for m in range(modes)]
         decay = [jnp.exp(-r) for r in rate]
-        weight = [row(residues, m, lanes) * jnp.sqrt(rate[m]) for m in range(modes)]
-        skip_row = row(skip, 0, lanes)
+        weight = [row(extra, m, lanes) * jnp.sqrt(rate[m]) for m in range(modes)]
+        skip_row = row(extra, modes, lanes)
 
         def step(index, state):
             at = pl.ds(pl.multiple_of(index * SUBS, SUBS), SUBS)
@@ -164,7 +210,6 @@
             for half in range(2):
                 at = pl.ds(pl.multiple_of((2 * index + half) * SUBS, SUBS), SUBS)
                 both.append(tree_sum(list(held) + [local[at, lanes]]))
-                local[at, lanes] = both[-1]
                 held = [decay[m] * held[m] for m in range(modes)]
             at = pl.ds(pl.multiple_of(index * 2 * SUBS, 2 * SUBS), 2 * SUBS)
             pack[0, at, lanes] = queries[at, lanes].astype(BF16)
@@ -174,20 +219,36 @@
         lax.fori_loop(0, span // 2, add, brought, unroll=2)
 
 
-def mix(read, entry, mixed):
+def mix(read, mine, other, entry, mixed):
     tiles, rows = mixed.shape[:2]
     span = rows // SUBS
-    modes = (entry.shape[0] - SUBS) // 2
+    modes = (mine.shape[0] - 3 * SUBS) // 3
+    block, half = lax.axis_index("seq"), lax.axis_size("seq") // 2
+    upper = (block >= half).astype(F32)
+    first = (block == half).astype(F32)
+    passed = (jnp.maximum(block - half, 0) * rows).astype(F32)
+    fix, start, end = mine[modes : modes + 4], mine[modes + SUBS : modes + 2 * SUBS], other[modes + SUBS :]
+    rates = mine[modes + 2 * SUBS : 2 * modes + 2 * SUBS]
+    weights = mine[2 * modes + 2 * SUBS : 3 * modes + 2 * SUBS]
+    skip, lead = mine[3 * modes + 2 * SUBS : 3 * modes + 2 * SUBS + 1], mine[3 * modes + 2 * SUBS + 1 : 3 * modes + 2 * SUBS + 2]
+    added = start[0:2] * end[2:4] + end[0:2] * (start[2:4] + end[2:4])
+    joined = other[:modes] + jnp.exp(rates) * added[0:1] + jnp.exp(2.0 * rates) * added[1:2]
+    entry[:modes] = weights * (mine[:modes] + upper * jnp.exp(-rates * passed) * joined)
+    added = fix[0:2] + first * added
+    entry[modes : modes + 1] = skip * added[0:1] - lead * added[1:2]
+    entry[modes + 1 : modes + 2] = skip * added[1:2]
+    entry[modes + 2 : modes + 4] = fix[2:4] + first * end[4:6]
     sub = lax.broadcasted_iota(jnp.int32, (SUBS, LANES), 0)
     for tile in range(tiles):
         lanes = pl.ds(tile * LANES, LANES)
-        rate = [row(entry, modes + SUBS + m, lanes) for m in range(modes)]
+        rate = [row(mine, modes + 2 * SUBS + m, lanes) for m in range(modes)]
         decay = [jnp.exp(-r) for r in rate]
         state = [jnp.exp(rate[m] * sub.astype(F32) * (-float(span))) * row(entry, m, lanes) for m in range(modes)]
+        more = [row(entry, modes + i, lanes) for i in range(4)]
 
         def pair(index, held, more=None):
             at = pl.ds(pl.multiple_of(index * 2 * SUBS, 2 * SUBS), 2 * SUBS)
-            query, value = read(at, lanes)
+            query, value = (part.astype(F32) for part in read(at, lanes))
             for half in range(2):
                 v, q = value[half * SUBS : (half + 1) * SUBS], query[half * SUBS : (half + 1) * SUBS]
                 if more is not None:
@@ -198,29 +259,51 @@
                 held = [decay[m] * held[m] for m in range(modes)]
             return held
 
-        state = pair(0, state, [row(entry, modes + i, lanes) for i in range(4)])
+        state = pair(0, state, more)
         lax.fori_loop(1, span // 2, pair, state, unroll=2)
     return jnp.concatenate([mixed[tile] for tile in range(tiles)], axis=1).astype(BF16)
 
 
-def near_kernel(queries, local, entry, w_out, share, mixed):
+def near_kernel(pack, mine, other, w_out, share, entry, mixed):
     me = lax.axis_index("ch")
     chip, core = jnp.right_shift(me, 1), jnp.bitwise_and(me, 1)
-    width = queries.shape[1]
-    part = mix(lambda at, lanes: (queries[at, lanes], local[at, lanes]), entry, mixed)
+    width = pack.shape[2]
+    part = mix(lambda at, lanes: (pack[0, at, lanes], pack[1, at, lanes]), mine, other, entry, mixed)
     for slot, column in enumerate((1 - core, core)):
         start = pl.multiple_of((2 * chip + column) * width, width)
         share[slot] = jnp.dot(part, w_out[:, pl.ds(start, width)], preferred_element_type=F32)
 
 
-def far_kernel(pack, entry, share, kept, sent, mixed):
+def far_kernel(pack, mine, other, share, kept, sent, entry, mixed):
     core = jnp.bitwise_and(lax.axis_index("ch"), 1)
     width = pack.shape[2]
-    part = mix(lambda at, lanes: (pack[0, at, lanes].astype(F32), pack[1, at, lanes].astype(F32)), entry, mixed)
+    part = mix(lambda at, lanes: (pack[0, at, lanes], pack[1, at, lanes]), mine, other, entry, mixed)
     for slot, (target, column) in enumerate(((sent, 1 - core), (kept, core))):
         start = pl.multiple_of(column * width, width)
         total = share[slot] + jnp.dot(part, pack[2, pl.ds(start, width), :], preferred_element_type=F32)
         target[...] = total.astype(target.dtype)
+
+
+def known_kernel(entry, fix, message, rates, extra, mine, *again):
+    modes = rates.shape[0]
+    rate = rates[...]
+    weight = extra[:modes] * jnp.sqrt(rate)
+    lead = jnp.sum(weight * jnp.exp(rate), axis=0, keepdims=True)
+    pieces = (
+        entry[...],
+        jnp.concatenate([fix[...], jnp.zeros_like(fix)], axis=0),
+        message[modes : modes + SUBS],
+        rate,
+        weight * jnp.exp(-rate),
+        jnp.concatenate([extra[modes : modes + 1], lead, jnp.zeros((SUBS - 2, rate.shape[1]), F32)], axis=0),
+    )
+    for target in (mine, *again[:1]):
+        at = 0
+        for piece in pieces:
+            target[at : at + piece.shape[0]] = piece
+            at += piece.shape[0]
+    for target in again[1:]:
+        target[...] = message[...]
 
 
 def join(first, second, rates, rows):
@@ -273,24 +356,25 @@
     rows, width = tokens.shape
     channels = w_in.shape[2]
     modes = rates.shape[0]
-    skip = skip_gain.reshape(1, channels)
     far = ch_swap(tokens, 2)
     side = ch_swap(tokens, 1)
-    weights = jnp.transpose(w_in, (1, 0, 2))
-    gains = norm_gain.reshape(-1, LANES)
-    staged = (tokens, weights, short_filter, rates, gains)
+    mine = (jnp.transpose(w_in, (1, 0, 2)), short_filter, rates)
+    staged = (tokens, norm_gain.reshape(-1, LANES))
+    for array in mine:
+        staged += (array, ch_swap(array, 1))
+    kept = (0, 1, *range(2, len(staged), 2))
     staged = pl.pallas_call(
         stage_kernel,
-        out_shape=tuple(jax.ShapeDtypeStruct(a.shape, a.dtype) for a in staged),
+        out_shape=tuple(jax.ShapeDtypeStruct(staged[i].shape, staged[i].dtype) for i in kept),
         in_specs=[pl.BlockSpec(memory_space=pl.ANY)] * len(staged),
-        out_specs=tuple(vmem_specs(len(staged))),
-        scratch_shapes=[pltpu.SemaphoreType.DMA((len(staged),))],
+        out_specs=tuple(vmem_specs(len(kept))),
+        scratch_shapes=[pltpu.SemaphoreType.DMA((len(kept),))],
         compiler_params=pltpu.CompilerParams(vmem_limit_bytes=STAGE_VMEM),
         name="stage",
     )(*staged)
     far, staged = lax.optimization_barrier((far, staged))
+    own_v, gain_v, w_in_v, taps_v, rates_v = staged
     side_far = ch_swap(far, 1)
-    own_v, w_in_v, taps_v, rates_v, gain_v = staged
     queries, gated, message = pl.pallas_call(
         front_kernel,
         out_shape=(
@@ -302,66 +386,80 @@
         out_specs=tuple(vmem_specs(3)),
         scratch_shapes=[pltpu.VMEM((3 * channels // LANES, rows + HALO, LANES), F32)],
         compiler_params=pltpu.CompilerParams(vmem_limit_bytes=FRONT_VMEM),
-        cost_estimate=pl.CostEstimate(flops=900_000_000, bytes_accessed=4_000_000, transcendentals=0),
+        cost_estimate=pl.CostEstimate(flops=1_000_000, bytes_accessed=1_000, transcendentals=0),
         name="front",
     )(own_v, far, side, side_far, gain_v, w_in_v, taps_v, rates_v)
-    local, pack = pl.pallas_call(
+    skip = skip_gain.reshape(1, channels)
+    pack, extra, w_out_v = pl.pallas_call(
         scan_kernel,
         out_shape=(
-            jax.ShapeDtypeStruct((rows, channels), F32),
             jax.ShapeDtypeStruct((3, rows, channels), BF16),
+            jax.ShapeDtypeStruct((modes + SUBS, channels), F32),
+            jax.ShapeDtypeStruct(w_out.shape, BF16),
         ),
-        in_specs=vmem_specs(6),
-        out_specs=tuple(vmem_specs(2)),
+        in_specs=vmem_specs(9),
+        out_specs=tuple(vmem_specs(3)),
+        scratch_shapes=[pltpu.VMEM((rows, channels), F32)],
         compiler_params=pltpu.CompilerParams(vmem_limit_bytes=SCAN_VMEM),
         cost_estimate=pl.CostEstimate(flops=2_000_000_000, bytes_accessed=1_000_000, transcendentals=0),
         name="scan",
-    )(queries, gated, rates_v, residues, skip, w_out)
+    )(queries, gated, rates_v, residues, ch_swap(residues, 1), skip, ch_swap(skip, 1), w_out, ch_swap(w_out, 1))
     held = (message, jnp.zeros_like(rates_v), jnp.zeros((4, channels), F32))
     held = scan_blocks(held, rates_v, rows, SCAN_FIRST[:1], 0)
-    held, local, pack = lax.optimization_barrier((held, local, pack))
+    held, pack = lax.optimization_barrier((held, pack))
     pack_far = ch_swap(pack, 2)
     held = scan_blocks(held, rates_v, rows, SCAN_FIRST[1:], 1)
+    row_shape = jax.ShapeDtypeStruct((3 * modes + 3 * SUBS, channels), F32)
+
+    def known(*operands, copies=False):
+        out_shape = (row_shape, row_shape, jax.ShapeDtypeStruct(message.shape, F32))[: 3 if copies else 1]
+        return pl.pallas_call(
+            known_kernel,
+            out_shape=out_shape,
+            in_specs=vmem_specs(5),
+            out_specs=tuple(vmem_specs(len(out_shape))),
+            compiler_params=pltpu.CompilerParams(vmem_limit_bytes=STAGE_VMEM),
+            name="known",
+        )(*operands, rates_v, extra)
+
+    def later(_, now):
+        message, _, mine, _ = now
+        held = (message, mine[:modes], mine[modes : modes + 4])
+        message, entry, fix = scan_blocks(held, rates_v, rows, SCAN_LATER, len(SCAN_FIRST))
+        (mine,) = known(entry, fix, message)
+        other = seq_swap(message, SCAN_LAST)
+        other_far = seq_swap(message, SCAN_LAST, 1)
+        return other, other_far, mine, ch_swap(mine, 2)
+
     once = jnp.minimum(lax.axis_index("seq") + 1, 1)
-    held = lax.fori_loop(0, once, lambda _, now: scan_blocks(now, rates_v, rows, SCAN_LATER, len(SCAN_FIRST)), held)
-    (_, entry, fix), pack_far = lax.optimization_barrier((held, pack_far))
-    weight = residues * jnp.sqrt(rates_v)
-    lead = jnp.sum(weight * jnp.exp(rates_v), axis=0, keepdims=True)
-    entry = jnp.concatenate(
-        [
-            weight * jnp.exp(-rates_v) * entry,
-            skip * fix[0:1] - lead * fix[1:2],
-            skip * fix[1:2],
-            fix[2:4],
-            jnp.zeros_like(fix),
-            rates_v,
-        ],
-        axis=0,
-    )
-    entry_far = ch_swap(entry, 2)
+    message, entry, fix = held
+    mine, mine_again, message_again = known(entry, fix, message, copies=True)
+    now = lax.fori_loop(0, once, later, (message, message_again, mine, mine_again))
+    (other, other_far, mine, mine_far), pack_far = lax.optimization_barrier((now, pack_far))
+    scratch = [pltpu.VMEM((modes + SUBS, channels), F32), pltpu.VMEM((channels // LANES, rows, LANES), F32)]
     share = pl.pallas_call(
         near_kernel,
         out_shape=jax.ShapeDtypeStruct((2, rows, width), F32),
         in_specs=vmem_specs(4),
         out_specs=vmem_specs(1)[0],
-        scratch_shapes=[pltpu.VMEM((channels // LANES, rows, LANES), F32)],
+        scratch_shapes=scratch,
         compiler_params=pltpu.CompilerParams(vmem_limit_bytes=BACK_VMEM),
         cost_estimate=pl.CostEstimate(flops=900_000_000, bytes_accessed=4_000_000, transcendentals=0),
         name="near",
-    )(queries, local, entry, w_out)
+    )(pack, mine, other, w_out_v)
     kept, sent = pl.pallas_call(
         far_kernel,
         out_shape=(
             jax.ShapeDtypeStruct((rows, width), F32),
             jax.ShapeDtypeStruct((rows, width), BF16),
         ),
-        in_specs=vmem_specs(3),
+        in_specs=vmem_specs(4),
         out_specs=tuple(vmem_specs(2)),
-        scratch_shapes=[pltpu.VMEM((channels // LANES, rows, LANES), F32)],
+        scratch_shapes=scratch,
         compiler_params=pltpu.CompilerParams(vmem_limit_bytes=BACK_VMEM),
         cost_estimate=pl.CostEstimate(flops=900_000_000, bytes_accessed=4_000_000, transcendentals=0),
         name="far",
-    )(pack_far, entry_far, share)
+    )(pack_far, mine_far, other_far, share)
     return (kept + ch_swap(sent, 1).astype(F32)).astype(BF16)
 
 

time: 55.6 us -> 55.3 us (level)
  starting transfers between devices: 28.2 us -> 23.3 us
  waiting for transfers between devices: 13.4 us -> 15.7 us
  Pallas kernels: 7.42 us -> 9.22 us
  local copies, waits for them, and re-layouts: 4.59 us -> 5.19 us
    ppermute x6 -> x12, starting transfers between devices: 16.5 us -> 11.9 us  [ch_swap(): lax.ppermute(array, 'ch', [(i, i ^ mask) for i in range(lax.axis_size('ch...]
    ppermute x7 -> x8, waiting for transfers between devices: 9.15 us -> 10.9 us  [seq_swap(): return lax.ppermute(array, ('seq', 'ch'), pairs)]
    pallas_call x2 -> x4, Pallas kernels: 2.35 us -> 4.1 us  [the longest x1 3.2 us: body(): pl.pallas_call(scan_kernel, out_shape=(jax.ShapeDtypeStruct((3, rows, cha...]
    while x0 -> x4, local copies, waits for them, and re-layouts: none -> 0.64 us
    ppermute x6 -> x12, waiting for transfers between devices: 4.24 us -> 4.8 us  [ch_swap(): lax.ppermute(array, 'ch', [(i, i ^ mask) for i in range(lax.axis_size('ch...]
    ppermute x7 -> x8, starting transfers between devices: 11.7 us -> 11.4 us  [seq_swap(): return lax.ppermute(array, ('seq', 'ch'), pairs)]
  transfers between devices with their start and end apart: 13 -> 20, of which waited for: 7 -> 11; matrix products, arithmetic and copies ran while one was open for 1% -> 1% of each run, Pallas kernels for 6% -> 13%
where the time goes in v4:
time: 55.3 us; the launch traced here: 54.9 us
  starting transfers between devices  23.3 us (42%)
  waiting for transfers between devices  15.7 us (28%)
  Pallas kernels  9.22 us (17%)
  local copies, waits for them, and re-layouts  5.19 us (9%)
  other arithmetic  1.07 us (2%)
    ppermute x12, starting transfers between devices, ch_swap(): lax.ppermute(array, 'ch', [(i, i ^ mask) for i in range(lax.axis_size('ch...  11.9 us
    ppermute x8, starting transfers between devices, seq_swap(): return lax.ppermute(array, ('seq', 'ch'), pairs)  11.4 us
    ppermute x8, waiting for transfers between devices, seq_swap(): return lax.ppermute(array, ('seq', 'ch'), pairs)  10.9 us
    ppermute x12, waiting for transfers between devices, ch_swap(): lax.ppermute(array, 'ch', [(i, i ^ mask) for i in range(lax.axis_size('ch...  4.8 us
    unnamed x20, local copies, waits for them, and re-layouts  4.49 us
    pallas_call x1, Pallas kernels, body(): pl.pallas_call(scan_kernel, out_shape=(jax.ShapeDtypeStruct((3, rows, cha...  3.2 us
    pallas_call x1, Pallas kernels, body(): pl.pallas_call(front_kernel, out_shape=(jax.ShapeDtypeStruct((rows, chann...  2.8 us
    pallas_call x1, Pallas kernels, body(): pl.pallas_call(near_kernel, out_shape=jax.ShapeDtypeStruct((2, rows, widt...  1.17 us
  transfers between devices with their start and end apart: 20, of which 11 were waited for; matrix products, arithmetic and copies ran while one was open for 1% of the time, Pallas kernels for 13%

profile of v4, /device:TPU:1, one launch (start us, length us, event | category | flops | bytes accessed | tf_op | source)
XLA Modules:
  0.0 54.9 jit_solution(12837785460431242977)
XLA Ops:
  0.0 3.2 %collective-permute-start.8 = (bf16[3,1024,256]{2,1,0:T(8,128)(2,1)}, bf16[3,1024,256]{2,1,0:T(8,128)(2,1)S(1)}, u32[]{:S(2)}, u32[]{:S(2)}) collective-permute-start(bf16[3,1024,256]{2,1,0:T(8,128)(2,1)} %bitcast.31), channel_id=1, source_target_pairs={{0,1},{1,0},{2,3},{3,2},{4,5},{5,4},{6,7},{7,6},{8,9},{9,8},{10,11... | collective-permute-start | bytes 4718600 | tf_op jit(solution)/shard_map/ppermute | solution.py:27
  3.2 1.0 %collective-permute-start.7 = (bf16[512,256]{1,0:T(8,128)(2,1)}, bf16[512,256]{1,0:T(8,128)(2,1)S(1)}, u32[]{:S(2)}, u32[]{:S(2)}) collective-permute-start(bf16[512,256]{1,0:T(8,128)(2,1)} %refs_0_.1), channel_id=1, source_target_pairs={{0,2},{1,3},{2,0},{3,1},{4,6},{5,7},{6,4},{7,5},{8,10},{9,11},{10,... | collective-permute-start | bytes 786440 | tf_op jit(solution)/shard_map/ppermute | solution.py:27
  5.0 1.5 %collective-permute-done.9.refs_5_ = f32[3,3,256]{2,1,0:T(4,128)S(1)} collective-permute-done((f32[3,3,256]{2,1,0:T(4,128)}, f32[3,3,256]{2,1,0:T(4,128)S(1)}, u32[]{:S(2)}, u32[]{:S(2)}) %collective-permute-start.9) | collective-permute-done | bytes 9248 | tf_op jit(solution)/shard_map/ppermute | solution.py:27
  7.0 1.4 %copy-done = bf16[1024,3,256]{2,0,1:T(8,128)(2,1)S(1)} copy-done((bf16[1024,3,256]{2,0,1:T(8,128)(2,1)S(1)}, bf16[1024,3,256]{2,0,1:T(8,128)(2,1)}, u32[]{:S(2)}) %copy-start) | copy-done | bytes 1572888
  8.4 0.9 %copy-done.1 = bf16[512,256]{1,0:T(8,128)(2,1)S(1)} copy-done((bf16[512,256]{1,0:T(8,128)(2,1)S(1)}, bf16[512,256]{1,0:T(8,128)(2,1)}, u32[]{:S(2)}) %copy-start.1) | copy-done | bytes 262168
  11.7 1.2 %collective-permute-done.7.far = bf16[512,256]{1,0:T(8,128)(2,1)S(1)} collective-permute-done((bf16[512,256]{1,0:T(8,128)(2,1)}, bf16[512,256]{1,0:T(8,128)(2,1)S(1)}, u32[]{:S(2)}, u32[]{:S(2)}) %collective-permute-start.7) | collective-permute-done | bytes 262176 | tf_op jit(solution)/shard_map/ppermute | solution.py:27
  12.9 0.8 %collective-permute-start.12 = (bf16[512,256]{1,0:T(8,128)(2,1)S(1)}, bf16[512,256]{1,0:T(8,128)(2,1)S(1)}, u32[]{:S(2)}, u32[]{:S(2)}) collective-permute-start(bf16[512,256]{1,0:T(8,128)(2,1)S(1)} %collective-permute-done.7.far), channel_id=1, source_target_pairs={{0,1},{1,0},{2,3},{3,2},{4,5},{5,4},{6,7},{7,6},{8,9},{9,8},{10,11... | collective-permute-start | bytes 786440 | tf_op jit(solution)/shard_map/ppermute | solution.py:27
  14.8 2.8 %front.1 = (f32[512,256]{1,0:T(8,128)S(1)}, f32[512,256]{1,0:T(8,128)S(1)}, f32[32,256]{1,0:T(8,128)S(1)}) custom-call(bf16[512,256]{1,0:T(8,128)(2,1)S(1)} %get-tuple-element.122.own, bf16[512,256]{1,0:T(8,128)(2,1)S(1)} %collective-permute-done.7.far, bf16[512,256]{1,0:T(8,128)(2,1)S(1)} %collective-permute-done.11.side, ...), custom_call_target="tpu_custom_call" | custom-call | flops 1000000 | bytes 1000 | tf_op jit(solution)/shard_map/front/pallas_call | solution.py:378
  17.8 3.2 %scan.1 = (bf16[3,512,256]{2,1,0:T(8,128)(2,1)S(1)}, f32[24,256]{1,0:T(8,128)S(1)}, bf16[256,1024]{1,0:T(8,128)(2,1)S(1)}) custom-call(f32[512,256]{1,0:T(8,128)S(1)} %get-tuple-element.128.queries, f32[512,256]{1,0:T(8,128)S(1)} %get-tuple-element.129.gated, f32[16,256]{1,0:T(8,128)S(1)} %get-tuple-element.342.rates, f32[16,256]{1,0:T(8,128)S(1)} %copy-done.6, ...), custom_call_target="tpu_custom_call" | custom-call | flops 2000000000 | bytes 1000000 | tf_op jit(solution)/shard_map/scan/pallas_call | solution.py:393
  21.2 1.7 %collective-permute-start.17 = (f32[32,256]{1,0:T(8,128)S(1)}, f32[32,256]{1,0:T(8,128)S(1)}, u32[]{:S(2)}, u32[]{:S(2)}) collective-permute-start(f32[32,256]{1,0:T(8,128)S(1)} %pad_maximum_fusion.4), channel_id=1, source_target_pairs={{0,13},{1,12},{2,15},{3,14},{4,9},{5,8},{6,11},{7,10},{8,5},{9,4},... | collective-permute-start | bytes 98312 | tf_op jit(solution)/shard_map/ppermute | solution.py:46
  22.9 2.7 %collective-permute-start.18 = (bf16[3,512,256]{2,1,0:T(8,128)(2,1)S(1)}, bf16[3,512,256]{2,1,0:T(8,128)(2,1)S(1)}, u32[]{:S(2)}, u32[]{:S(2)}) collective-permute-start(bf16[3,512,256]{2,1,0:T(8,128)(2,1)S(1)} %get-tuple-element.142.pack), channel_id=1, source_target_pairs={{0,2},{1,3},{2,0},{3,1},{4,6},{5,7},{6,4},{7,5},{8,10},{9,11},{10,... | collective-permute-start | bytes 2359304 | tf_op jit(solution)/shard_map/ppermute | solution.py:27
  26.7 23.5 %while.17 = (s32[]{:T(128)}, f32[32,256]{1,0:T(8,128)S(1)}, f32[32,256]{1,0:T(8,128)}, f32[72,256]{1,0:T(8,128)S(1)}, f32[72,256]{1,0:T(8,128)}, /*index=5*/s32[...) while((s32[]{:T(128)}, f32[32,256]{1,0:T(8,128)S(1)}, ...), condition=%wide.region_1.2_spmd, body=%wide.region_0.1_spmd.sunk | while | flops 333853 | bytes 2884386 | solution.py:437
  26.7 4.1 %collective-permute-start.1 = (f32[32,256]{1,0:T(8,128)S(1)}, f32[32,256]{1,0:T(8,128)S(1)}, u32[]{:S(2)}, u32[]{:S(2)}) collective-permute-start(f32[32,256]{1,0:T(8,128)S(1)} %get-tuple-element.355), channel_id=1, source_target_pairs={{0,48},{1,49},{2,50},{3,51},{4,52},{5,53},{6,54},{7,55},{8,56},{9,... | collective-permute-start | bytes 98312 | tf_op jit(solution)/shard_map/while/body/ppermute | solution.py:46
  31.4 1.0 %collective-permute-done.1 = f32[32,256]{1,0:T(8,128)S(1)} collective-permute-done((f32[32,256]{1,0:T(8,128)S(1)}, f32[32,256]{1,0:T(8,128)S(1)}, u32[]{:S(2)}, u32[]{:S(2)}) %collective-permute-start.1) | collective-permute-done | bytes 32800 | tf_op jit(solution)/shard_map/while/body/ppermute | solution.py:46
  32.4 3.1 %collective-permute-done.2 = f32[32,256]{1,0:T(8,128)S(1)} collective-permute-done((f32[32,256]{1,0:T(8,128)S(1)}, f32[32,256]{1,0:T(8,128)S(1)}, u32[]{:S(2)}, u32[]{:S(2)}) %collective-permute-start.2) | collective-permute-done | bytes 32800 | tf_op jit(solution)/shard_map/while/body/ppermute | solution.py:46
  35.8 3.5 %collective-permute-start.3 = (f32[32,256]{1,0:T(8,128)S(1)}, f32[32,256]{1,0:T(8,128)S(1)}, u32[]{:S(2)}, u32[]{:S(2)}) collective-permute-start(f32[32,256]{1,0:T(8,128)S(1)} %pad_maximum_fusion.8), channel_id=1, source_target_pairs={{0,97},{1,96},{2,99},{3,98},{4,101},{5,100},{6,103},{7,102},{8,105... | collective-permute-start | bytes 98312 | tf_op jit(solution)/shard_map/while/body/ppermute | solution.py:46
  39.2 2.6 %collective-permute-done.3 = f32[32,256]{1,0:T(8,128)S(1)} collective-permute-done((f32[32,256]{1,0:T(8,128)S(1)}, f32[32,256]{1,0:T(8,128)S(1)}, u32[]{:S(2)}, u32[]{:S(2)}) %collective-permute-start.3) | collective-permute-done | bytes 32800 | tf_op jit(solution)/shard_map/while/body/ppermute | solution.py:46
  42.0 2.2 %collective-permute-start.6 = (f32[72,256]{1,0:T(8,128)S(1)}, f32[72,256]{1,0:T(8,128)S(1)}, u32[]{:S(2)}, u32[]{:S(2)}) collective-permute-start(f32[72,256]{1,0:T(8,128)S(1)} %known.4), channel_id=1, source_target_pairs={{0,2},{1,3},{2,0},{3,1},{4,6},{5,7},{6,4},{7,5},{8,10},{9,11},{10,... | collective-permute-start | bytes 221192 | tf_op jit(solution)/shard_map/while/body/ppermute | solution.py:27
  44.2 0.8 %collective-permute-start.4 = (f32[32,256]{1,0:T(8,128)S(1)}, f32[32,256]{1,0:T(8,128)S(1)}, u32[]{:S(2)}, u32[]{:S(2)}) collective-permute-start(f32[32,256]{1,0:T(8,128)S(1)} %pad_maximum_fusion.9.message), channel_id=1, source_target_pairs={{0,129},{1,128},{2,131},{3,130},{4,133},{5,132},{6,135},{7,134},{8... | collective-permute-start | bytes 98312 | tf_op jit(solution)/shard_map/while/body/ppermute | solution.py:46
  45.7 2.6 %collective-permute-done.4 = f32[32,256]{1,0:T(8,128)S(1)} collective-permute-done((f32[32,256]{1,0:T(8,128)S(1)}, f32[32,256]{1,0:T(8,128)S(1)}, u32[]{:S(2)}, u32[]{:S(2)}) %collective-permute-start.4) | collective-permute-done | bytes 32800 | tf_op jit(solution)/shard_map/while/body/ppermute | solution.py:46
  48.3 1.3 %collective-permute-done.5 = f32[32,256]{1,0:T(8,128)S(1)} collective-permute-done((f32[32,256]{1,0:T(8,128)S(1)}, f32[32,256]{1,0:T(8,128)S(1)}, u32[]{:S(2)}, u32[]{:S(2)}) %collective-permute-start.5) | collective-permute-done | bytes 32800 | tf_op jit(solution)/shard_map/while/body/ppermute | solution.py:46
  50.2 1.2 %near.1.share = f32[2,512,256]{2,1,0:T(8,128)S(1)} custom-call(bf16[3,512,256]{2,1,0:T(8,128)(2,1)S(1)} %get-tuple-element.142.pack, f32[72,256]{1,0:T(8,128)S(1)} %get-tuple-element.146.mine, f32[32,256]{1,0:T(8,128)S(1)} %get-tuple-element.147.other, bf16[256,1024]{1,0:T(8,128)(2,1)S(1)} %get-tuple-element.148.w_out), custom_call_target="tpu_custom_call" | custom-call | flops 900000000 | bytes 4000000 | tf_op jit(solution)/shard_map/near/pallas_call | solution.py:440
  51.4 1.2 %far.1 = (f32[512,256]{1,0:T(8,128)S(1)}, bf16[512,256]{1,0:T(8,128)(2,1)S(1)}) custom-call(bf16[3,512,256]{2,1,0:T(8,128)(2,1)S(1)} %collective-permute-done.18.pack, f32[72,256]{1,0:T(8,128)S(1)} %copy-done.9, f32[32,256]{1,0:T(8,128)S(1)} %copy-done.11, f32[2,512,256]{2,1,0:T(8,128)S(1)} %near.1.share), custom_call_target="tpu_custom_call" | custom-call | flops 900000000 | bytes 4000000 | tf_op jit(solution)/shard_map/far/pallas_call | solution.py:450
  52.8 1.4 %collective-permute-done.19 = bf16[512,256]{1,0:T(8,128)(2,1)S(1)} collective-permute-done((bf16[512,256]{1,0:T(8,128)(2,1)S(1)}, bf16[512,256]{1,0:T(8,128)(2,1)S(1)}, u32[]{:S(2)}, u32[]{:S(2)}) %collective-permute-start.19) | collective-permute-done | bytes 262176 | tf_op jit(solution)/shard_map/ppermute | solution.py:27
  (92 shorter events, 9.1 us)
Async XLA Ops:
  0.0 7.0 %collective-permute-start.8 = (bf16[3,1024,256]{2,1,0:T(8,128)(2,1)}, bf16[3,1024,256]{2,1,0:T(8,128)(2,1)S(1)}, u32[]{:S(2)}, u32[]{:S(2)}) collective-permute-start(bf16[3,1024,256]{2,1,0:T(8,128)(2,1)} %bitcast.31), channel_id=1, source_target_pairs={{0,1},{1,0},{2,3},{3,2},{4,5},{5,4},{6,7},{7,6},{8,9},{9,8},{10,11... | collective-permute-start | bytes 4718600 | tf_op jit(solution)/shard_map/ppermute | solution.py:27
  3.2 9.7 %collective-permute-start.7 = (bf16[512,256]{1,0:T(8,128)(2,1)}, bf16[512,256]{1,0:T(8,128)(2,1)S(1)}, u32[]{:S(2)}, u32[]{:S(2)}) collective-permute-start(bf16[512,256]{1,0:T(8,128)(2,1)} %refs_0_.1), channel_id=1, source_target_pairs={{0,2},{1,3},{2,0},{3,1},{4,6},{5,7},{6,4},{7,5},{8,10},{9,11},{10,... | collective-permute-start | bytes 786440 | tf_op jit(solution)/shard_map/ppermute | solution.py:27
  4.2 13.5 %collective-permute-start.16 = (bf16[256,1024]{1,0:T(8,128)(2,1)}, bf16[256,1024]{1,0:T(8,128)(2,1)}, u32[]{:S(2)}, u32[]{:S(2)}) collective-permute-start(bf16[256,1024]{1,0:T(8,128)(2,1)} %w_out.1), channel_id=1, source_target_pairs={{0,1},{1,0},{2,3},{3,2},{4,5},{5,4},{6,7},{7,6},{8,9},{9,8},{10,11... | collective-permute-start | bytes 1572872 | tf_op jit(solution)/shard_map/ppermute | solution.py:27
  4.5 2.4 %collective-permute-start.10 = (f32[16,256]{1,0:T(8,128)}, f32[16,256]{1,0:T(8,128)S(1)}, u32[]{:S(2)}, u32[]{:S(2)}) collective-permute-start(f32[16,256]{1,0:T(8,128)} %refs_6_.1), channel_id=1, source_target_pairs={{0,1},{1,0},{2,3},{3,2},{4,5},{5,4},{6,7},{7,6},{8,9},{9,8},{10,11... | collective-permute-start | bytes 49160 | tf_op jit(solution)/shard_map/ppermute | solution.py:27
  4.8 1.8 %collective-permute-start.9 = (f32[3,3,256]{2,1,0:T(4,128)}, f32[3,3,256]{2,1,0:T(4,128)S(1)}, u32[]{:S(2)}, u32[]{:S(2)}) collective-permute-start(f32[3,3,256]{2,1,0:T(4,128)} %refs_4_.1), channel_id=1, source_target_pairs={{0,1},{1,0},{2,3},{3,2},{4,5},{5,4},{6,7},{7,6},{8,9},{9,8},{10,11... | collective-permute-start | bytes 27656 | tf_op jit(solution)/shard_map/ppermute | solution.py:27
  6.6 7.6 %collective-permute-start.11 = (bf16[512,256]{1,0:T(8,128)(2,1)}, bf16[512,256]{1,0:T(8,128)(2,1)S(1)}, u32[]{:S(2)}, u32[]{:S(2)}) collective-permute-start(bf16[512,256]{1,0:T(8,128)(2,1)} %refs_0_.1), channel_id=1, source_target_pairs={{0,1},{1,0},{2,3},{3,2},{4,5},{5,4},{6,7},{7,6},{8,9},{9,8},{10,11... | collective-permute-start | bytes 786440 | tf_op jit(solution)/shard_map/ppermute | solution.py:27
  7.0 1.4 %copy-start = (bf16[1024,3,256]{2,0,1:T(8,128)(2,1)S(1)}, bf16[1024,3,256]{2,0,1:T(8,128)(2,1)}, u32[]{:S(2)}) copy-start(bf16[1024,3,256]{2,0,1:T(8,128)(2,1)} %param.12) | copy-start | bytes 4718596
  11.4 2.3 %copy-start.6 = (f32[16,256]{1,0:T(8,128)S(1)}, f32[16,256]{1,0:T(8,128)}, u32[]{:S(2)}) copy-start(f32[16,256]{1,0:T(8,128)} %residues.1) | copy-start | bytes 49156
  11.4 2.3 %copy-start.7 = (f32[256]{0:T(256)S(1)}, f32[256]{0:T(256)}, u32[]{:S(2)}) copy-start(f32[256]{0:T(256)} %param.16) | copy-start | bytes 3076
  11.6 6.1 %copy-start.5 = (bf16[256,1024]{1,0:T(8,128)(2,1)S(1)}, bf16[256,1024]{1,0:T(8,128)(2,1)}, u32[]{:S(2)}) copy-start(bf16[256,1024]{1,0:T(8,128)(2,1)} %w_out.1) | copy-start | bytes 1572868
  12.9 1.9 %collective-permute-start.12 = (bf16[512,256]{1,0:T(8,128)(2,1)S(1)}, bf16[512,256]{1,0:T(8,128)(2,1)S(1)}, u32[]{:S(2)}, u32[]{:S(2)}) collective-permute-start(bf16[512,256]{1,0:T(8,128)(2,1)S(1)} %collective-permute-done.7.far), channel_id=1, source_target_pairs={{0,1},{1,0},{2,3},{3,2},{4,5},{5,4},{6,7},{7,6},{8,9},{9,8},{10,11... | collective-permute-start | bytes 786440 | tf_op jit(solution)/shard_map/ppermute | solution.py:27
  13.7 4.1 %collective-permute-start.14 = (f32[16,256]{1,0:T(8,128)S(1)}, f32[16,256]{1,0:T(8,128)S(1)}, u32[]{:S(2)}, u32[]{:S(2)}) collective-permute-start(f32[16,256]{1,0:T(8,128)S(1)} %copy-done.6), channel_id=1, source_target_pairs={{0,1},{1,0},{2,3},{3,2},{4,5},{5,4},{6,7},{7,6},{8,9},{9,8},{10,11... | collective-permute-start | bytes 49160 | tf_op jit(solution)/shard_map/ppermute | solution.py:27
  13.7 4.1 %collective-permute-start.15 = (f32[1,256]{1,0:T(1,128)S(1)}, f32[1,256]{1,0:T(1,128)S(1)}, u32[]{:S(2)}, u32[]{:S(2)}) collective-permute-start(f32[1,256]{1,0:T(1,128)S(1)} %bitcast.34), channel_id=1, source_target_pairs={{0,1},{1,0},{2,3},{3,2},{4,5},{5,4},{6,7},{7,6},{8,9},{9,8},{10,11... | collective-permute-start | bytes 3080 | tf_op jit(solution)/shard_map/ppermute | solution.py:27
  17.6 3.5 %collective-permute-start.13 = (f32[32,256]{1,0:T(8,128)S(1)}, f32[32,256]{1,0:T(8,128)S(1)}, u32[]{:S(2)}, u32[]{:S(2)}) collective-permute-start(f32[32,256]{1,0:T(8,128)S(1)} %get-tuple-element.127), channel_id=1, source_target_pairs={{0,5},{1,4},{2,7},{3,6},{4,1},{5,0},{6,3},{7,2},{8,13},{9,12},{10,... | collective-permute-start | bytes 98312 | tf_op jit(solution)/shard_map/ppermute | solution.py:46
  21.2 4.7 %collective-permute-start.17 = (f32[32,256]{1,0:T(8,128)S(1)}, f32[32,256]{1,0:T(8,128)S(1)}, u32[]{:S(2)}, u32[]{:S(2)}) collective-permute-start(f32[32,256]{1,0:T(8,128)S(1)} %pad_maximum_fusion.4), channel_id=1, source_target_pairs={{0,13},{1,12},{2,15},{3,14},{4,9},{5,8},{6,11},{7,10},{8,5},{9,4},... | collective-permute-start | bytes 98312 | tf_op jit(solution)/shard_map/ppermute | solution.py:46
  22.9 27.3 %collective-permute-start.18 = (bf16[3,512,256]{2,1,0:T(8,128)(2,1)S(1)}, bf16[3,512,256]{2,1,0:T(8,128)(2,1)S(1)}, u32[]{:S(2)}, u32[]{:S(2)}) collective-permute-start(bf16[3,512,256]{2,1,0:T(8,128)(2,1)S(1)} %get-tuple-element.142.pack), channel_id=1, source_target_pairs={{0,2},{1,3},{2,0},{3,1},{4,6},{5,7},{6,4},{7,5},{8,10},{9,11},{10,... | collective-permute-start | bytes 2359304 | tf_op jit(solution)/shard_map/ppermute | solution.py:27
  26.7 5.7 %collective-permute-start.1 = (f32[32,256]{1,0:T(8,128)S(1)}, f32[32,256]{1,0:T(8,128)S(1)}, u32[]{:S(2)}, u32[]{:S(2)}) collective-permute-start(f32[32,256]{1,0:T(8,128)S(1)} %get-tuple-element.355), channel_id=1, source_target_pairs={{0,48},{1,49},{2,50},{3,51},{4,52},{5,53},{6,54},{7,55},{8,56},{9,... | collective-permute-start | bytes 98312 | tf_op jit(solution)/shard_map/while/body/ppermute | solution.py:46
  30.8 4.7 %collective-permute-start.2 = (f32[32,256]{1,0:T(8,128)S(1)}, f32[32,256]{1,0:T(8,128)S(1)}, u32[]{:S(2)}, u32[]{:S(2)}) collective-permute-start(f32[32,256]{1,0:T(8,128)S(1)} %get-tuple-element.355), channel_id=1, source_target_pairs={{0,33},{1,32},{2,35},{3,34},{4,37},{5,36},{6,39},{7,38},{8,41},{9,... | collective-permute-start | bytes 98312 | tf_op jit(solution)/shard_map/while/body/ppermute | solution.py:46
  30.8 4.7 %collective-permute-start = (f32[32,256]{1,0:T(8,128)S(1)}, f32[32,256]{1,0:T(8,128)S(1)}, u32[]{:S(2)}, u32[]{:S(2)}) collective-permute-start(f32[32,256]{1,0:T(8,128)S(1)} %get-tuple-element.355), channel_id=1, source_target_pairs={{0,17},{1,16},{2,19},{3,18},{4,21},{5,20},{6,23},{7,22},{8,25},{9,... | collective-permute-start | bytes 98312 | tf_op jit(solution)/shard_map/while/body/ppermute | solution.py:46
  35.8 6.1 %collective-permute-start.3 = (f32[32,256]{1,0:T(8,128)S(1)}, f32[32,256]{1,0:T(8,128)S(1)}, u32[]{:S(2)}, u32[]{:S(2)}) collective-permute-start(f32[32,256]{1,0:T(8,128)S(1)} %pad_maximum_fusion.8), channel_id=1, source_target_pairs={{0,97},{1,96},{2,99},{3,98},{4,101},{5,100},{6,103},{7,102},{8,105... | collective-permute-start | bytes 98312 | tf_op jit(solution)/shard_map/while/body/ppermute | solution.py:46
  42.0 7.5 %collective-permute-start.6 = (f32[72,256]{1,0:T(8,128)S(1)}, f32[72,256]{1,0:T(8,128)S(1)}, u32[]{:S(2)}, u32[]{:S(2)}) collective-permute-start(f32[72,256]{1,0:T(8,128)S(1)} %known.4), channel_id=1, source_target_pairs={{0,2},{1,3},{2,0},{3,1},{4,6},{5,7},{6,4},{7,5},{8,10},{9,11},{10,... | collective-permute-start | bytes 221192 | tf_op jit(solution)/shard_map/while/body/ppermute | solution.py:27
  44.2 4.1 %collective-permute-start.4 = (f32[32,256]{1,0:T(8,128)S(1)}, f32[32,256]{1,0:T(8,128)S(1)}, u32[]{:S(2)}, u32[]{:S(2)}) collective-permute-start(f32[32,256]{1,0:T(8,128)S(1)} %pad_maximum_fusion.9.message), channel_id=1, source_target_pairs={{0,129},{1,128},{2,131},{3,130},{4,133},{5,132},{6,135},{7,134},{8... | collective-permute-start | bytes 98312 | tf_op jit(solution)/shard_map/while/body/ppermute | solution.py:46
  45.0 4.6 %collective-permute-start.5 = (f32[32,256]{1,0:T(8,128)S(1)}, f32[32,256]{1,0:T(8,128)S(1)}, u32[]{:S(2)}, u32[]{:S(2)}) collective-permute-start(f32[32,256]{1,0:T(8,128)S(1)} %pad_maximum_fusion.9.message), channel_id=1, source_target_pairs={{0,131},{1,130},{2,129},{3,128},{4,135},{5,134},{6,133},{7,132},{8... | collective-permute-start | bytes 98312 | tf_op jit(solution)/shard_map/while/body/ppermute | solution.py:46
  52.6 1.6 %collective-permute-start.19 = (bf16[512,256]{1,0:T(8,128)(2,1)S(1)}, bf16[512,256]{1,0:T(8,128)(2,1)S(1)}, u32[]{:S(2)}, u32[]{:S(2)}) collective-permute-start(bf16[512,256]{1,0:T(8,128)(2,1)S(1)} %get-tuple-element.150), channel_id=1, source_target_pairs={{0,1},{1,0},{2,3},{3,2},{4,5},{5,4},{6,7},{7,6},{8,9},{9,8},{10,11... | collective-permute-start | bytes 786440 | tf_op jit(solution)/shard_map/ppermute | solution.py:27
  (8 other events, 6.7 us)

commit v5 on v4

--- a/solution.py
+++ b/solution.py
@@ -157,16 +157,26 @@
 
 
 def scan_kernel(
-    queries, gated, rates, residues, residues_side, skip, skip_side, w_out, w_out_side, pack, extra, w_out_v, local
+    queries, gated, rates, residues, residues_side, skip, skip_side, w_out, w_out_side, pack, extra, w_out_v, local, sems
 ):
     rows, width = gated.shape
     modes = rates.shape[0]
     swapped = crossed(lax.axis_index("seq"))
 
+    other = 1 - jnp.right_shift(lax.axis_index("ch"), 1)
+
+    def projection_copies(projection):
+        pairs = [(projection, w_out_v)]
+        for column in range(2):
+            start = pl.multiple_of((2 * other + column) * width, width)
+            pairs.append((projection.at[:, pl.ds(start, width)], pack.at[2, pl.ds(column * width, width), :]))
+        return [pltpu.make_async_copy(src, dst, sems.at[i]) for i, (src, dst) in enumerate(pairs)]
+
     def keep(weights, direct, projection):
+        for copy in projection_copies(projection):
+            copy.start()
         extra[:modes] = weights[...]
         extra[modes:] = jnp.concatenate([direct[...], jnp.zeros((SUBS - 1, width), F32)], axis=0)
-        w_out_v[...] = projection[...]
 
     @pl.when(swapped)
     def _():
@@ -176,10 +186,6 @@
     def _():
         keep(residues, skip, w_out)
 
-    other = 1 - jnp.right_shift(lax.axis_index("ch"), 1)
-    for column in range(2):
-        start = pl.multiple_of((2 * other + column) * width, width)
-        pack[2, column * width : (column + 1) * width, :] = w_out_v[:, pl.ds(start, width)]
     span = rows // SUBS
     sub = lax.broadcasted_iota(jnp.int32, (SUBS, LANES), 0)
     for lane in range(0, width, LANES):
@@ -217,6 +223,16 @@
             return held
 
         lax.fori_loop(0, span // 2, add, brought, unroll=2)
+
+    @pl.when(swapped)
+    def _():
+        for copy in projection_copies(w_out_side):
+            copy.wait()
+
+    @pl.when(jnp.logical_not(swapped))
+    def _():
+        for copy in projection_copies(w_out):
+            copy.wait()
 
 
 def mix(read, mine, other, entry, mixed):
@@ -397,9 +413,9 @@
             jax.ShapeDtypeStruct((modes + SUBS, channels), F32),
             jax.ShapeDtypeStruct(w_out.shape, BF16),
         ),
-        in_specs=vmem_specs(9),
+        in_specs=vmem_specs(7) + [pl.BlockSpec(memory_space=pl.ANY)] * 2,
         out_specs=tuple(vmem_specs(3)),
-        scratch_shapes=[pltpu.VMEM((rows, channels), F32)],
+        scratch_shapes=[pltpu.VMEM((rows, channels), F32), pltpu.SemaphoreType.DMA((3,))],
         compiler_params=pltpu.CompilerParams(vmem_limit_bytes=SCAN_VMEM),
         cost_estimate=pl.CostEstimate(flops=2_000_000_000, bytes_accessed=1_000_000, transcendentals=0),
         name="scan",

time: 55.3 us -> 54.3 us (0.982)
  Pallas kernels: 9.22 us -> 8.26 us
  starting transfers between devices: 23.3 us -> 22.4 us
  waiting for transfers between devices: 15.7 us -> 16.6 us
    pallas_call x1, Pallas kernels: 3.2 us -> 2.23 us  [body(): pl.pallas_call(scan_kernel, out_shape=(jax.ShapeDtypeStruct((3, rows, cha...]
    ppermute x8, waiting for transfers between devices: 10.9 us -> 11.8 us  [seq_swap(): return lax.ppermute(array, ('seq', 'ch'), pairs)]
    ppermute x12, starting transfers between devices: 11.9 us -> 11.2 us  [ch_swap(): lax.ppermute(array, 'ch', [(i, i ^ mask) for i in range(lax.axis_size('ch...]
  transfers between devices with their start and end apart: 20 -> 20, of which waited for: 11 -> 11; matrix products, arithmetic and copies ran while one was open for 1% -> 1% of each run, Pallas kernels for 13% -> 11%
where the time goes in v5:
time: 54.3 us; the launch traced here: 53.9 us
  starting transfers between devices  22.4 us (41%)
  waiting for transfers between devices  16.6 us (31%)
  Pallas kernels  8.26 us (15%)
  local copies, waits for them, and re-layouts  5.19 us (10%)
  other arithmetic  1.07 us (2%)
    ppermute x8, waiting for transfers between devices, seq_swap(): return lax.ppermute(array, ('seq', 'ch'), pairs)  11.8 us
    ppermute x12, starting transfers between devices, ch_swap(): lax.ppermute(array, 'ch', [(i, i ^ mask) for i in range(lax.axis_size('ch...  11.2 us
    ppermute x8, starting transfers between devices, seq_swap(): return lax.ppermute(array, ('seq', 'ch'), pairs)  11.1 us
    ppermute x12, waiting for transfers between devices, ch_swap(): lax.ppermute(array, 'ch', [(i, i ^ mask) for i in range(lax.axis_size('ch...  4.8 us
    unnamed x20, local copies, waits for them, and re-layouts  4.49 us
    pallas_call x1, Pallas kernels, body(): pl.pallas_call(front_kernel, out_shape=(jax.ShapeDtypeStruct((rows, chann...  2.8 us
    pallas_call x1, Pallas kernels, body(): pl.pallas_call(scan_kernel, out_shape=(jax.ShapeDtypeStruct((3, rows, cha...  2.23 us
    pallas_call x1, Pallas kernels, body(): pl.pallas_call(near_kernel, out_shape=jax.ShapeDtypeStruct((2, rows, widt...  1.17 us
  transfers between devices with their start and end apart: 20, of which 11 were waited for; matrix products, arithmetic and copies ran while one was open for 1% of the time, Pallas kernels for 11%

profile of v5, /device:TPU:1, one launch (start us, length us, event | category | flops | bytes accessed | tf_op | source)
XLA Modules:
  0.0 53.9 jit_solution(18317209591573561692)
XLA Ops:
  0.0 3.2 %collective-permute-start.8 = (bf16[3,1024,256]{2,1,0:T(8,128)(2,1)}, bf16[3,1024,256]{2,1,0:T(8,128)(2,1)S(1)}, u32[]{:S(2)}, u32[]{:S(2)}) collective-permute-start(bf16[3,1024,256]{2,1,0:T(8,128)(2,1)} %bitcast.31), channel_id=1, source_target_pairs={{0,1},{1,0},{2,3},{3,2},{4,5},{5,4},{6,7},{7,6},{8,9},{9,8},{10,11... | collective-permute-start | bytes 4718600 | tf_op jit(solution)/shard_map/ppermute | solution.py:27
  3.2 1.0 %collective-permute-start.7 = (bf16[512,256]{1,0:T(8,128)(2,1)}, bf16[512,256]{1,0:T(8,128)(2,1)S(1)}, u32[]{:S(2)}, u32[]{:S(2)}) collective-permute-start(bf16[512,256]{1,0:T(8,128)(2,1)} %refs_0_.1), channel_id=1, source_target_pairs={{0,2},{1,3},{2,0},{3,1},{4,6},{5,7},{6,4},{7,5},{8,10},{9,11},{10,... | collective-permute-start | bytes 786440 | tf_op jit(solution)/shard_map/ppermute | solution.py:27
  5.0 1.5 %collective-permute-done.9.refs_5_ = f32[3,3,256]{2,1,0:T(4,128)S(1)} collective-permute-done((f32[3,3,256]{2,1,0:T(4,128)}, f32[3,3,256]{2,1,0:T(4,128)S(1)}, u32[]{:S(2)}, u32[]{:S(2)}) %collective-permute-start.9) | collective-permute-done | bytes 9248 | tf_op jit(solution)/shard_map/ppermute | solution.py:27
  7.0 1.4 %copy-done = bf16[1024,3,256]{2,0,1:T(8,128)(2,1)S(1)} copy-done((bf16[1024,3,256]{2,0,1:T(8,128)(2,1)S(1)}, bf16[1024,3,256]{2,0,1:T(8,128)(2,1)}, u32[]{:S(2)}) %copy-start) | copy-done | bytes 1572888
  8.4 0.9 %copy-done.1 = bf16[512,256]{1,0:T(8,128)(2,1)S(1)} copy-done((bf16[512,256]{1,0:T(8,128)(2,1)S(1)}, bf16[512,256]{1,0:T(8,128)(2,1)}, u32[]{:S(2)}) %copy-start.1) | copy-done | bytes 262168
  11.7 1.2 %collective-permute-done.7.far = bf16[512,256]{1,0:T(8,128)(2,1)S(1)} collective-permute-done((bf16[512,256]{1,0:T(8,128)(2,1)}, bf16[512,256]{1,0:T(8,128)(2,1)S(1)}, u32[]{:S(2)}, u32[]{:S(2)}) %collective-permute-start.7) | collective-permute-done | bytes 262176 | tf_op jit(solution)/shard_map/ppermute | solution.py:27
  14.8 2.8 %front.1 = (f32[512,256]{1,0:T(8,128)S(1)}, f32[512,256]{1,0:T(8,128)S(1)}, f32[32,256]{1,0:T(8,128)S(1)}) custom-call(bf16[512,256]{1,0:T(8,128)(2,1)S(1)} %get-tuple-element.122.own, bf16[512,256]{1,0:T(8,128)(2,1)S(1)} %collective-permute-done.7.far, bf16[512,256]{1,0:T(8,128)(2,1)S(1)} %collective-permute-done.11.side, ...), custom_call_target="tpu_custom_call" | custom-call | flops 1000000 | bytes 1000 | tf_op jit(solution)/shard_map/front/pallas_call | solution.py:394
  17.8 2.2 %scan.1 = (bf16[3,512,256]{2,1,0:T(8,128)(2,1)S(1)}, f32[24,256]{1,0:T(8,128)S(1)}, bf16[256,1024]{1,0:T(8,128)(2,1)S(1)}) custom-call(f32[512,256]{1,0:T(8,128)S(1)} %get-tuple-element.128.queries, f32[512,256]{1,0:T(8,128)S(1)} %get-tuple-element.129.gated, f32[16,256]{1,0:T(8,128)S(1)} %get-tuple-element.342.rates, f32[16,256]{1,0:T(8,128)S(1)} %copy-done.6, ...), custom_call_target="tpu_custom_call" | custom-call | flops 2000000000 | bytes 1000000 | tf_op jit(solution)/shard_map/scan/pallas_call | solution.py:409
  20.0 1.1 %collective-permute-done.13 = f32[32,256]{1,0:T(8,128)S(1)} collective-permute-done((f32[32,256]{1,0:T(8,128)S(1)}, f32[32,256]{1,0:T(8,128)S(1)}, u32[]{:S(2)}, u32[]{:S(2)}) %collective-permute-start.13) | collective-permute-done | bytes 32800 | tf_op jit(solution)/shard_map/ppermute | solution.py:46
  21.2 1.3 %collective-permute-start.17 = (f32[32,256]{1,0:T(8,128)S(1)}, f32[32,256]{1,0:T(8,128)S(1)}, u32[]{:S(2)}, u32[]{:S(2)}) collective-permute-start(f32[32,256]{1,0:T(8,128)S(1)} %pad_maximum_fusion.4), channel_id=1, source_target_pairs={{0,13},{1,12},{2,15},{3,14},{4,9},{5,8},{6,11},{7,10},{8,5},{9,4},... | collective-permute-start | bytes 98312 | tf_op jit(solution)/shard_map/ppermute | solution.py:46
  22.6 2.8 %collective-permute-start.18 = (bf16[3,512,256]{2,1,0:T(8,128)(2,1)S(1)}, bf16[3,512,256]{2,1,0:T(8,128)(2,1)S(1)}, u32[]{:S(2)}, u32[]{:S(2)}) collective-permute-start(bf16[3,512,256]{2,1,0:T(8,128)(2,1)S(1)} %get-tuple-element.142.pack), channel_id=1, source_target_pairs={{0,2},{1,3},{2,0},{3,1},{4,6},{5,7},{6,4},{7,5},{8,10},{9,11},{10,... | collective-permute-start | bytes 2359304 | tf_op jit(solution)/shard_map/ppermute | solution.py:27
  26.7 22.5 %while.17 = (s32[]{:T(128)}, f32[32,256]{1,0:T(8,128)S(1)}, f32[32,256]{1,0:T(8,128)}, f32[72,256]{1,0:T(8,128)S(1)}, f32[72,256]{1,0:T(8,128)}, /*index=5*/s32[...) while((s32[]{:T(128)}, f32[32,256]{1,0:T(8,128)S(1)}, ...), condition=%wide.region_1.2_spmd, body=%wide.region_0.1_spmd.sunk | while | flops 333853 | bytes 2884386 | solution.py:453
  26.7 3.8 %collective-permute-start.1 = (f32[32,256]{1,0:T(8,128)S(1)}, f32[32,256]{1,0:T(8,128)S(1)}, u32[]{:S(2)}, u32[]{:S(2)}) collective-permute-start(f32[32,256]{1,0:T(8,128)S(1)} %get-tuple-element.355), channel_id=1, source_target_pairs={{0,48},{1,49},{2,50},{3,51},{4,52},{5,53},{6,54},{7,55},{8,56},{9,... | collective-permute-start | bytes 98312 | tf_op jit(solution)/shard_map/while/body/ppermute | solution.py:46
  31.0 1.0 %collective-permute-done.1 = f32[32,256]{1,0:T(8,128)S(1)} collective-permute-done((f32[32,256]{1,0:T(8,128)S(1)}, f32[32,256]{1,0:T(8,128)S(1)}, u32[]{:S(2)}, u32[]{:S(2)}) %collective-permute-start.1) | collective-permute-done | bytes 32800 | tf_op jit(solution)/shard_map/while/body/ppermute | solution.py:46
  32.1 3.3 %collective-permute-done.2 = f32[32,256]{1,0:T(8,128)S(1)} collective-permute-done((f32[32,256]{1,0:T(8,128)S(1)}, f32[32,256]{1,0:T(8,128)S(1)}, u32[]{:S(2)}, u32[]{:S(2)}) %collective-permute-start.2) | collective-permute-done | bytes 32800 | tf_op jit(solution)/shard_map/while/body/ppermute | solution.py:46
  35.6 3.3 %collective-permute-start.3 = (f32[32,256]{1,0:T(8,128)S(1)}, f32[32,256]{1,0:T(8,128)S(1)}, u32[]{:S(2)}, u32[]{:S(2)}) collective-permute-start(f32[32,256]{1,0:T(8,128)S(1)} %pad_maximum_fusion.8), channel_id=1, source_target_pairs={{0,97},{1,96},{2,99},{3,98},{4,101},{5,100},{6,103},{7,102},{8,105... | collective-permute-start | bytes 98312 | tf_op jit(solution)/shard_map/while/body/ppermute | solution.py:46
  38.9 2.6 %collective-permute-done.3 = f32[32,256]{1,0:T(8,128)S(1)} collective-permute-done((f32[32,256]{1,0:T(8,128)S(1)}, f32[32,256]{1,0:T(8,128)S(1)}, u32[]{:S(2)}, u32[]{:S(2)}) %collective-permute-start.3) | collective-permute-done | bytes 32800 | tf_op jit(solution)/shard_map/while/body/ppermute | solution.py:46
  41.7 1.5 %collective-permute-start.6 = (f32[72,256]{1,0:T(8,128)S(1)}, f32[72,256]{1,0:T(8,128)S(1)}, u32[]{:S(2)}, u32[]{:S(2)}) collective-permute-start(f32[72,256]{1,0:T(8,128)S(1)} %known.4), channel_id=1, source_target_pairs={{0,2},{1,3},{2,0},{3,1},{4,6},{5,7},{6,4},{7,5},{8,10},{9,11},{10,... | collective-permute-start | bytes 221192 | tf_op jit(solution)/shard_map/while/body/ppermute | solution.py:27
  44.0 1.3 %collective-permute-start.5 = (f32[32,256]{1,0:T(8,128)S(1)}, f32[32,256]{1,0:T(8,128)S(1)}, u32[]{:S(2)}, u32[]{:S(2)}) collective-permute-start(f32[32,256]{1,0:T(8,128)S(1)} %pad_maximum_fusion.9.message), channel_id=1, source_target_pairs={{0,131},{1,130},{2,129},{3,128},{4,135},{5,134},{6,133},{7,132},{8... | collective-permute-start | bytes 98312 | tf_op jit(solution)/shard_map/while/body/ppermute | solution.py:46
  45.3 2.0 %collective-permute-done.4 = f32[32,256]{1,0:T(8,128)S(1)} collective-permute-done((f32[32,256]{1,0:T(8,128)S(1)}, f32[32,256]{1,0:T(8,128)S(1)}, u32[]{:S(2)}, u32[]{:S(2)}) %collective-permute-start.4) | collective-permute-done | bytes 32800 | tf_op jit(solution)/shard_map/while/body/ppermute | solution.py:46
  47.3 1.3 %collective-permute-done.5 = f32[32,256]{1,0:T(8,128)S(1)} collective-permute-done((f32[32,256]{1,0:T(8,128)S(1)}, f32[32,256]{1,0:T(8,128)S(1)}, u32[]{:S(2)}, u32[]{:S(2)}) %collective-permute-start.5) | collective-permute-done | bytes 32800 | tf_op jit(solution)/shard_map/while/body/ppermute | solution.py:46
  49.2 1.2 %near.1.share = f32[2,512,256]{2,1,0:T(8,128)S(1)} custom-call(bf16[3,512,256]{2,1,0:T(8,128)(2,1)S(1)} %get-tuple-element.142.pack, f32[72,256]{1,0:T(8,128)S(1)} %get-tuple-element.146.mine, f32[32,256]{1,0:T(8,128)S(1)} %get-tuple-element.147.other, bf16[256,1024]{1,0:T(8,128)(2,1)S(1)} %get-tuple-element.148.w_out), custom_call_target="tpu_custom_call" | custom-call | flops 900000000 | bytes 4000000 | tf_op jit(solution)/shard_map/near/pallas_call | solution.py:456
  50.4 1.2 %far.1 = (f32[512,256]{1,0:T(8,128)S(1)}, bf16[512,256]{1,0:T(8,128)(2,1)S(1)}) custom-call(bf16[3,512,256]{2,1,0:T(8,128)(2,1)S(1)} %collective-permute-done.18.pack, f32[72,256]{1,0:T(8,128)S(1)} %copy-done.9, f32[32,256]{1,0:T(8,128)S(1)} %copy-done.11, f32[2,512,256]{2,1,0:T(8,128)S(1)} %near.1.share), custom_call_target="tpu_custom_call" | custom-call | flops 900000000 | bytes 4000000 | tf_op jit(solution)/shard_map/far/pallas_call | solution.py:466
  51.8 1.4 %collective-permute-done.19 = bf16[512,256]{1,0:T(8,128)(2,1)S(1)} collective-permute-done((bf16[512,256]{1,0:T(8,128)(2,1)S(1)}, bf16[512,256]{1,0:T(8,128)(2,1)S(1)}, u32[]{:S(2)}, u32[]{:S(2)}) %collective-permute-start.19) | collective-permute-done | bytes 262176 | tf_op jit(solution)/shard_map/ppermute | solution.py:27
  (92 shorter events, 10.2 us)
Async XLA Ops:
  0.0 7.0 %collective-permute-start.8 = (bf16[3,1024,256]{2,1,0:T(8,128)(2,1)}, bf16[3,1024,256]{2,1,0:T(8,128)(2,1)S(1)}, u32[]{:S(2)}, u32[]{:S(2)}) collective-permute-start(bf16[3,1024,256]{2,1,0:T(8,128)(2,1)} %bitcast.31), channel_id=1, source_target_pairs={{0,1},{1,0},{2,3},{3,2},{4,5},{5,4},{6,7},{7,6},{8,9},{9,8},{10,11... | collective-permute-start | bytes 4718600 | tf_op jit(solution)/shard_map/ppermute | solution.py:27
  3.2 9.7 %collective-permute-start.7 = (bf16[512,256]{1,0:T(8,128)(2,1)}, bf16[512,256]{1,0:T(8,128)(2,1)S(1)}, u32[]{:S(2)}, u32[]{:S(2)}) collective-permute-start(bf16[512,256]{1,0:T(8,128)(2,1)} %refs_0_.1), channel_id=1, source_target_pairs={{0,2},{1,3},{2,0},{3,1},{4,6},{5,7},{6,4},{7,5},{8,10},{9,11},{10,... | collective-permute-start | bytes 786440 | tf_op jit(solution)/shard_map/ppermute | solution.py:27
  4.2 13.5 %collective-permute-start.16 = (bf16[256,1024]{1,0:T(8,128)(2,1)}, bf16[256,1024]{1,0:T(8,128)(2,1)}, u32[]{:S(2)}, u32[]{:S(2)}) collective-permute-start(bf16[256,1024]{1,0:T(8,128)(2,1)} %w_out.1), channel_id=1, source_target_pairs={{0,1},{1,0},{2,3},{3,2},{4,5},{5,4},{6,7},{7,6},{8,9},{9,8},{10,11... | collective-permute-start | bytes 1572872 | tf_op jit(solution)/shard_map/ppermute | solution.py:27
  4.5 2.4 %collective-permute-start.10 = (f32[16,256]{1,0:T(8,128)}, f32[16,256]{1,0:T(8,128)S(1)}, u32[]{:S(2)}, u32[]{:S(2)}) collective-permute-start(f32[16,256]{1,0:T(8,128)} %refs_6_.1), channel_id=1, source_target_pairs={{0,1},{1,0},{2,3},{3,2},{4,5},{5,4},{6,7},{7,6},{8,9},{9,8},{10,11... | collective-permute-start | bytes 49160 | tf_op jit(solution)/shard_map/ppermute | solution.py:27
  4.8 1.8 %collective-permute-start.9 = (f32[3,3,256]{2,1,0:T(4,128)}, f32[3,3,256]{2,1,0:T(4,128)S(1)}, u32[]{:S(2)}, u32[]{:S(2)}) collective-permute-start(f32[3,3,256]{2,1,0:T(4,128)} %refs_4_.1), channel_id=1, source_target_pairs={{0,1},{1,0},{2,3},{3,2},{4,5},{5,4},{6,7},{7,6},{8,9},{9,8},{10,11... | collective-permute-start | bytes 27656 | tf_op jit(solution)/shard_map/ppermute | solution.py:27
  6.6 7.6 %collective-permute-start.11 = (bf16[512,256]{1,0:T(8,128)(2,1)}, bf16[512,256]{1,0:T(8,128)(2,1)S(1)}, u32[]{:S(2)}, u32[]{:S(2)}) collective-permute-start(bf16[512,256]{1,0:T(8,128)(2,1)} %refs_0_.1), channel_id=1, source_target_pairs={{0,1},{1,0},{2,3},{3,2},{4,5},{5,4},{6,7},{7,6},{8,9},{9,8},{10,11... | collective-permute-start | bytes 786440 | tf_op jit(solution)/shard_map/ppermute | solution.py:27
  7.0 1.4 %copy-start = (bf16[1024,3,256]{2,0,1:T(8,128)(2,1)S(1)}, bf16[1024,3,256]{2,0,1:T(8,128)(2,1)}, u32[]{:S(2)}) copy-start(bf16[1024,3,256]{2,0,1:T(8,128)(2,1)} %param.12) | copy-start | bytes 4718596
  11.4 2.3 %copy-start.6 = (f32[16,256]{1,0:T(8,128)S(1)}, f32[16,256]{1,0:T(8,128)}, u32[]{:S(2)}) copy-start(f32[16,256]{1,0:T(8,128)} %residues.1) | copy-start | bytes 49156
  11.4 2.3 %copy-start.7 = (f32[256]{0:T(256)S(1)}, f32[256]{0:T(256)}, u32[]{:S(2)}) copy-start(f32[256]{0:T(256)} %param.16) | copy-start | bytes 3076
  11.6 6.1 %copy-start.5 = (bf16[256,1024]{1,0:T(8,128)(2,1)S(1)}, bf16[256,1024]{1,0:T(8,128)(2,1)}, u32[]{:S(2)}) copy-start(bf16[256,1024]{1,0:T(8,128)(2,1)} %w_out.1) | copy-start | bytes 1572868
  12.9 1.9 %collective-permute-start.12 = (bf16[512,256]{1,0:T(8,128)(2,1)S(1)}, bf16[512,256]{1,0:T(8,128)(2,1)S(1)}, u32[]{:S(2)}, u32[]{:S(2)}) collective-permute-start(bf16[512,256]{1,0:T(8,128)(2,1)S(1)} %collective-permute-done.7.far), channel_id=1, source_target_pairs={{0,1},{1,0},{2,3},{3,2},{4,5},{5,4},{6,7},{7,6},{8,9},{9,8},{10,11... | collective-permute-start | bytes 786440 | tf_op jit(solution)/shard_map/ppermute | solution.py:27
  13.7 4.1 %collective-permute-start.14 = (f32[16,256]{1,0:T(8,128)S(1)}, f32[16,256]{1,0:T(8,128)S(1)}, u32[]{:S(2)}, u32[]{:S(2)}) collective-permute-start(f32[16,256]{1,0:T(8,128)S(1)} %copy-done.6), channel_id=1, source_target_pairs={{0,1},{1,0},{2,3},{3,2},{4,5},{5,4},{6,7},{7,6},{8,9},{9,8},{10,11... | collective-permute-start | bytes 49160 | tf_op jit(solution)/shard_map/ppermute | solution.py:27
  13.7 4.1 %collective-permute-start.15 = (f32[1,256]{1,0:T(1,128)S(1)}, f32[1,256]{1,0:T(1,128)S(1)}, u32[]{:S(2)}, u32[]{:S(2)}) collective-permute-start(f32[1,256]{1,0:T(1,128)S(1)} %bitcast.34), channel_id=1, source_target_pairs={{0,1},{1,0},{2,3},{3,2},{4,5},{5,4},{6,7},{7,6},{8,9},{9,8},{10,11... | collective-permute-start | bytes 3080 | tf_op jit(solution)/shard_map/ppermute | solution.py:27
  17.6 3.5 %collective-permute-start.13 = (f32[32,256]{1,0:T(8,128)S(1)}, f32[32,256]{1,0:T(8,128)S(1)}, u32[]{:S(2)}, u32[]{:S(2)}) collective-permute-start(f32[32,256]{1,0:T(8,128)S(1)} %get-tuple-element.127), channel_id=1, source_target_pairs={{0,5},{1,4},{2,7},{3,6},{4,1},{5,0},{6,3},{7,2},{8,13},{9,12},{10,... | collective-permute-start | bytes 98312 | tf_op jit(solution)/shard_map/ppermute | solution.py:46
  21.2 4.7 %collective-permute-start.17 = (f32[32,256]{1,0:T(8,128)S(1)}, f32[32,256]{1,0:T(8,128)S(1)}, u32[]{:S(2)}, u32[]{:S(2)}) collective-permute-start(f32[32,256]{1,0:T(8,128)S(1)} %pad_maximum_fusion.4), channel_id=1, source_target_pairs={{0,13},{1,12},{2,15},{3,14},{4,9},{5,8},{6,11},{7,10},{8,5},{9,4},... | collective-permute-start | bytes 98312 | tf_op jit(solution)/shard_map/ppermute | solution.py:46
  22.6 26.6 %collective-permute-start.18 = (bf16[3,512,256]{2,1,0:T(8,128)(2,1)S(1)}, bf16[3,512,256]{2,1,0:T(8,128)(2,1)S(1)}, u32[]{:S(2)}, u32[]{:S(2)}) collective-permute-start(bf16[3,512,256]{2,1,0:T(8,128)(2,1)S(1)} %get-tuple-element.142.pack), channel_id=1, source_target_pairs={{0,2},{1,3},{2,0},{3,1},{4,6},{5,7},{6,4},{7,5},{8,10},{9,11},{10,... | collective-permute-start | bytes 2359304 | tf_op jit(solution)/shard_map/ppermute | solution.py:27
  26.7 5.4 %collective-permute-start.1 = (f32[32,256]{1,0:T(8,128)S(1)}, f32[32,256]{1,0:T(8,128)S(1)}, u32[]{:S(2)}, u32[]{:S(2)}) collective-permute-start(f32[32,256]{1,0:T(8,128)S(1)} %get-tuple-element.355), channel_id=1, source_target_pairs={{0,48},{1,49},{2,50},{3,51},{4,52},{5,53},{6,54},{7,55},{8,56},{9,... | collective-permute-start | bytes 98312 | tf_op jit(solution)/shard_map/while/body/ppermute | solution.py:46
  30.5 4.9 %collective-permute-start.2 = (f32[32,256]{1,0:T(8,128)S(1)}, f32[32,256]{1,0:T(8,128)S(1)}, u32[]{:S(2)}, u32[]{:S(2)}) collective-permute-start(f32[32,256]{1,0:T(8,128)S(1)} %get-tuple-element.355), channel_id=1, source_target_pairs={{0,33},{1,32},{2,35},{3,34},{4,37},{5,36},{6,39},{7,38},{8,41},{9,... | collective-permute-start | bytes 98312 | tf_op jit(solution)/shard_map/while/body/ppermute | solution.py:46
  30.5 4.9 %collective-permute-start = (f32[32,256]{1,0:T(8,128)S(1)}, f32[32,256]{1,0:T(8,128)S(1)}, u32[]{:S(2)}, u32[]{:S(2)}) collective-permute-start(f32[32,256]{1,0:T(8,128)S(1)} %get-tuple-element.355), channel_id=1, source_target_pairs={{0,17},{1,16},{2,19},{3,18},{4,21},{5,20},{6,23},{7,22},{8,25},{9,... | collective-permute-start | bytes 98312 | tf_op jit(solution)/shard_map/while/body/ppermute | solution.py:46
  35.6 5.9 %collective-permute-start.3 = (f32[32,256]{1,0:T(8,128)S(1)}, f32[32,256]{1,0:T(8,128)S(1)}, u32[]{:S(2)}, u32[]{:S(2)}) collective-permute-start(f32[32,256]{1,0:T(8,128)S(1)} %pad_maximum_fusion.8), channel_id=1, source_target_pairs={{0,97},{1,96},{2,99},{3,98},{4,101},{5,100},{6,103},{7,102},{8,105... | collective-permute-start | bytes 98312 | tf_op jit(solution)/shard_map/while/body/ppermute | solution.py:46
  41.7 6.9 %collective-permute-start.6 = (f32[72,256]{1,0:T(8,128)S(1)}, f32[72,256]{1,0:T(8,128)S(1)}, u32[]{:S(2)}, u32[]{:S(2)}) collective-permute-start(f32[72,256]{1,0:T(8,128)S(1)} %known.4), channel_id=1, source_target_pairs={{0,2},{1,3},{2,0},{3,1},{4,6},{5,7},{6,4},{7,5},{8,10},{9,11},{10,... | collective-permute-start | bytes 221192 | tf_op jit(solution)/shard_map/while/body/ppermute | solution.py:27
  43.2 4.0 %collective-permute-start.4 = (f32[32,256]{1,0:T(8,128)S(1)}, f32[32,256]{1,0:T(8,128)S(1)}, u32[]{:S(2)}, u32[]{:S(2)}) collective-permute-start(f32[32,256]{1,0:T(8,128)S(1)} %pad_maximum_fusion.9.message), channel_id=1, source_target_pairs={{0,129},{1,128},{2,131},{3,130},{4,133},{5,132},{6,135},{7,134},{8... | collective-permute-start | bytes 98312 | tf_op jit(solution)/shard_map/while/body/ppermute | solution.py:46
  44.0 4.6 %collective-permute-start.5 = (f32[32,256]{1,0:T(8,128)S(1)}, f32[32,256]{1,0:T(8,128)S(1)}, u32[]{:S(2)}, u32[]{:S(2)}) collective-permute-start(f32[32,256]{1,0:T(8,128)S(1)} %pad_maximum_fusion.9.message), channel_id=1, source_target_pairs={{0,131},{1,130},{2,129},{3,128},{4,135},{5,134},{6,133},{7,132},{8... | collective-permute-start | bytes 98312 | tf_op jit(solution)/shard_map/while/body/ppermute | solution.py:46
  51.5 1.6 %collective-permute-start.19 = (bf16[512,256]{1,0:T(8,128)(2,1)S(1)}, bf16[512,256]{1,0:T(8,128)(2,1)S(1)}, u32[]{:S(2)}, u32[]{:S(2)}) collective-permute-start(bf16[512,256]{1,0:T(8,128)(2,1)S(1)} %get-tuple-element.150), channel_id=1, source_target_pairs={{0,1},{1,0},{2,3},{3,2},{4,5},{5,4},{6,7},{7,6},{8,9},{9,8},{10,11... | collective-permute-start | bytes 786440 | tf_op jit(solution)/shard_map/ppermute | solution.py:27
  (8 other events, 6.7 us)

commit v6 on v5

--- a/solution.py
+++ b/solution.py
@@ -114,7 +114,7 @@
         total = total.astype(BF16).astype(F32)
         for tile in range(tiles):
             projected[group * tiles + tile, :HALO] = jnp.zeros((HALO, LANES), F32)
-            projected[group * tiles + tile, HALO:] = total[:, tile * LANES : (tile + 1) * LANES]
+            projected[group * tiles + tile, HALO : HALO + rows] = total[:, tile * LANES : (tile + 1) * LANES]
 
     sub = lax.broadcasted_iota(jnp.int32, (SUBS, LANES), 0)
     message[...] = jnp.zeros_like(message)
@@ -236,7 +236,7 @@
 
 
 def mix(read, mine, other, entry, mixed):
-    tiles, rows = mixed.shape[:2]
+    tiles, rows = mixed.shape[0], mixed.shape[1] * SUBS // (SUBS + 1)
     span = rows // SUBS
     modes = (mine.shape[0] - 3 * SUBS) // 3
     block, half = lax.axis_index("seq"), lax.axis_size("seq") // 2
@@ -277,7 +277,7 @@
 
         state = pair(0, state, more)
         lax.fori_loop(1, span // 2, pair, state, unroll=2)
-    return jnp.concatenate([mixed[tile] for tile in range(tiles)], axis=1).astype(BF16)
+    return jnp.concatenate([mixed[tile, :rows] for tile in range(tiles)], axis=1).astype(BF16)
 
 
 def near_kernel(pack, mine, other, w_out, share, entry, mixed):
@@ -400,7 +400,7 @@
         ),
         in_specs=vmem_specs(8),
         out_specs=tuple(vmem_specs(3)),
-        scratch_shapes=[pltpu.VMEM((3 * channels // LANES, rows + HALO, LANES), F32)],
+        scratch_shapes=[pltpu.VMEM((3 * channels // LANES, rows + rows // SUBS + HALO, LANES), F32)],
         compiler_params=pltpu.CompilerParams(vmem_limit_bytes=FRONT_VMEM),
         cost_estimate=pl.CostEstimate(flops=1_000_000, bytes_accessed=1_000, transcendentals=0),
         name="front",
@@ -452,7 +452,7 @@
     mine, mine_again, message_again = known(entry, fix, message, copies=True)
     now = lax.fori_loop(0, once, later, (message, message_again, mine, mine_again))
     (other, other_far, mine, mine_far), pack_far = lax.optimization_barrier((now, pack_far))
-    scratch = [pltpu.VMEM((modes + SUBS, channels), F32), pltpu.VMEM((channels // LANES, rows, LANES), F32)]
+    scratch = [pltpu.VMEM((modes + SUBS, channels), F32), pltpu.VMEM((channels // LANES, rows + rows // SUBS, LANES), F32)]
     share = pl.pallas_call(
         near_kernel,
         out_shape=jax.ShapeDtypeStruct((2, rows, width), F32),

time: 54.3 us -> 54.3 us (level)
  no operation moved by 1% of the time
where the time goes in v6:
time: 54.3 us; the launch traced here: 53.9 us
  starting transfers between devices  22.4 us (41%)
  waiting for transfers between devices  16.6 us (31%)
  Pallas kernels  8.26 us (15%)
  local copies, waits for them, and re-layouts  5.19 us (10%)
  other arithmetic  1.07 us (2%)
    ppermute x8, waiting for transfers between devices, seq_swap(): return lax.ppermute(array, ('seq', 'ch'), pairs)  11.8 us
    ppermute x12, starting transfers between devices, ch_swap(): lax.ppermute(array, 'ch', [(i, i ^ mask) for i in range(lax.axis_size('ch...  11.2 us
    ppermute x8, starting transfers between devices, seq_swap(): return lax.ppermute(array, ('seq', 'ch'), pairs)  11.1 us
    ppermute x12, waiting for transfers between devices, ch_swap(): lax.ppermute(array, 'ch', [(i, i ^ mask) for i in range(lax.axis_size('ch...  4.8 us
    unnamed x20, local copies, waits for them, and re-layouts  4.49 us
    pallas_call x1, Pallas kernels, body(): pl.pallas_call(front_kernel, out_shape=(jax.ShapeDtypeStruct((rows, chann...  2.8 us
    pallas_call x1, Pallas kernels, body(): pl.pallas_call(scan_kernel, out_shape=(jax.ShapeDtypeStruct((3, rows, cha...  2.23 us
    pallas_call x1, Pallas kernels, body(): pl.pallas_call(near_kernel, out_shape=jax.ShapeDtypeStruct((2, rows, widt...  1.17 us
  transfers between devices with their start and end apart: 20, of which 11 were waited for; matrix products, arithmetic and copies ran while one was open for 1% of the time, Pallas kernels for 11%

profile of v6, /device:TPU:1, one launch (start us, length us, event | category | flops | bytes accessed | tf_op | source)
XLA Modules:
  0.0 53.9 jit_solution(11078876877316680954)
XLA Ops:
  0.0 3.2 %collective-permute-start.8 = (bf16[3,1024,256]{2,1,0:T(8,128)(2,1)}, bf16[3,1024,256]{2,1,0:T(8,128)(2,1)S(1)}, u32[]{:S(2)}, u32[]{:S(2)}) collective-permute-start(bf16[3,1024,256]{2,1,0:T(8,128)(2,1)} %bitcast.31), channel_id=1, source_target_pairs={{0,1},{1,0},{2,3},{3,2},{4,5},{5,4},{6,7},{7,6},{8,9},{9,8},{10,11... | collective-permute-start | bytes 4718600 | tf_op jit(solution)/shard_map/ppermute | solution.py:27
  3.2 1.0 %collective-permute-start.7 = (bf16[512,256]{1,0:T(8,128)(2,1)}, bf16[512,256]{1,0:T(8,128)(2,1)S(1)}, u32[]{:S(2)}, u32[]{:S(2)}) collective-permute-start(bf16[512,256]{1,0:T(8,128)(2,1)} %refs_0_.1), channel_id=1, source_target_pairs={{0,2},{1,3},{2,0},{3,1},{4,6},{5,7},{6,4},{7,5},{8,10},{9,11},{10,... | collective-permute-start | bytes 786440 | tf_op jit(solution)/shard_map/ppermute | solution.py:27
  5.0 1.5 %collective-permute-done.9.refs_5_ = f32[3,3,256]{2,1,0:T(4,128)S(1)} collective-permute-done((f32[3,3,256]{2,1,0:T(4,128)}, f32[3,3,256]{2,1,0:T(4,128)S(1)}, u32[]{:S(2)}, u32[]{:S(2)}) %collective-permute-start.9) | collective-permute-done | bytes 9248 | tf_op jit(solution)/shard_map/ppermute | solution.py:27
  7.0 1.4 %copy-done = bf16[1024,3,256]{2,0,1:T(8,128)(2,1)S(1)} copy-done((bf16[1024,3,256]{2,0,1:T(8,128)(2,1)S(1)}, bf16[1024,3,256]{2,0,1:T(8,128)(2,1)}, u32[]{:S(2)}) %copy-start) | copy-done | bytes 1572888
  8.4 0.9 %copy-done.1 = bf16[512,256]{1,0:T(8,128)(2,1)S(1)} copy-done((bf16[512,256]{1,0:T(8,128)(2,1)S(1)}, bf16[512,256]{1,0:T(8,128)(2,1)}, u32[]{:S(2)}) %copy-start.1) | copy-done | bytes 262168
  11.7 1.2 %collective-permute-done.7.far = bf16[512,256]{1,0:T(8,128)(2,1)S(1)} collective-permute-done((bf16[512,256]{1,0:T(8,128)(2,1)}, bf16[512,256]{1,0:T(8,128)(2,1)S(1)}, u32[]{:S(2)}, u32[]{:S(2)}) %collective-permute-start.7) | collective-permute-done | bytes 262176 | tf_op jit(solution)/shard_map/ppermute | solution.py:27
  14.8 2.8 %front.1 = (f32[512,256]{1,0:T(8,128)S(1)}, f32[512,256]{1,0:T(8,128)S(1)}, f32[32,256]{1,0:T(8,128)S(1)}) custom-call(bf16[512,256]{1,0:T(8,128)(2,1)S(1)} %get-tuple-element.122.own, bf16[512,256]{1,0:T(8,128)(2,1)S(1)} %collective-permute-done.7.far, bf16[512,256]{1,0:T(8,128)(2,1)S(1)} %collective-permute-done.11.side, ...), custom_call_target="tpu_custom_call" | custom-call | flops 1000000 | bytes 1000 | tf_op jit(solution)/shard_map/front/pallas_call | solution.py:394
  17.8 2.2 %scan.1 = (bf16[3,512,256]{2,1,0:T(8,128)(2,1)S(1)}, f32[24,256]{1,0:T(8,128)S(1)}, bf16[256,1024]{1,0:T(8,128)(2,1)S(1)}) custom-call(f32[512,256]{1,0:T(8,128)S(1)} %get-tuple-element.128.queries, f32[512,256]{1,0:T(8,128)S(1)} %get-tuple-element.129.gated, f32[16,256]{1,0:T(8,128)S(1)} %get-tuple-element.342.rates, f32[16,256]{1,0:T(8,128)S(1)} %copy-done.6, ...), custom_call_target="tpu_custom_call" | custom-call | flops 2000000000 | bytes 1000000 | tf_op jit(solution)/shard_map/scan/pallas_call | solution.py:409
  20.0 1.1 %collective-permute-done.13 = f32[32,256]{1,0:T(8,128)S(1)} collective-permute-done((f32[32,256]{1,0:T(8,128)S(1)}, f32[32,256]{1,0:T(8,128)S(1)}, u32[]{:S(2)}, u32[]{:S(2)}) %collective-permute-start.13) | collective-permute-done | bytes 32800 | tf_op jit(solution)/shard_map/ppermute | solution.py:46
  21.2 1.3 %collective-permute-start.17 = (f32[32,256]{1,0:T(8,128)S(1)}, f32[32,256]{1,0:T(8,128)S(1)}, u32[]{:S(2)}, u32[]{:S(2)}) collective-permute-start(f32[32,256]{1,0:T(8,128)S(1)} %pad_maximum_fusion.4), channel_id=1, source_target_pairs={{0,13},{1,12},{2,15},{3,14},{4,9},{5,8},{6,11},{7,10},{8,5},{9,4},... | collective-permute-start | bytes 98312 | tf_op jit(solution)/shard_map/ppermute | solution.py:46
  22.6 2.8 %collective-permute-start.18 = (bf16[3,512,256]{2,1,0:T(8,128)(2,1)S(1)}, bf16[3,512,256]{2,1,0:T(8,128)(2,1)S(1)}, u32[]{:S(2)}, u32[]{:S(2)}) collective-permute-start(bf16[3,512,256]{2,1,0:T(8,128)(2,1)S(1)} %get-tuple-element.142.pack), channel_id=1, source_target_pairs={{0,2},{1,3},{2,0},{3,1},{4,6},{5,7},{6,4},{7,5},{8,10},{9,11},{10,... | collective-permute-start | bytes 2359304 | tf_op jit(solution)/shard_map/ppermute | solution.py:27
  26.7 22.5 %while.17 = (s32[]{:T(128)}, f32[32,256]{1,0:T(8,128)S(1)}, f32[32,256]{1,0:T(8,128)}, f32[72,256]{1,0:T(8,128)S(1)}, f32[72,256]{1,0:T(8,128)}, /*index=5*/s32[...) while((s32[]{:T(128)}, f32[32,256]{1,0:T(8,128)S(1)}, ...), condition=%wide.region_1.2_spmd, body=%wide.region_0.1_spmd.sunk | while | flops 333853 | bytes 2884386 | solution.py:453
  26.7 3.8 %collective-permute-start.1 = (f32[32,256]{1,0:T(8,128)S(1)}, f32[32,256]{1,0:T(8,128)S(1)}, u32[]{:S(2)}, u32[]{:S(2)}) collective-permute-start(f32[32,256]{1,0:T(8,128)S(1)} %get-tuple-element.355), channel_id=1, source_target_pairs={{0,48},{1,49},{2,50},{3,51},{4,52},{5,53},{6,54},{7,55},{8,56},{9,... | collective-permute-start | bytes 98312 | tf_op jit(solution)/shard_map/while/body/ppermute | solution.py:46
  31.0 1.0 %collective-permute-done.1 = f32[32,256]{1,0:T(8,128)S(1)} collective-permute-done((f32[32,256]{1,0:T(8,128)S(1)}, f32[32,256]{1,0:T(8,128)S(1)}, u32[]{:S(2)}, u32[]{:S(2)}) %collective-permute-start.1) | collective-permute-done | bytes 32800 | tf_op jit(solution)/shard_map/while/body/ppermute | solution.py:46
  32.1 3.3 %collective-permute-done.2 = f32[32,256]{1,0:T(8,128)S(1)} collective-permute-done((f32[32,256]{1,0:T(8,128)S(1)}, f32[32,256]{1,0:T(8,128)S(1)}, u32[]{:S(2)}, u32[]{:S(2)}) %collective-permute-start.2) | collective-permute-done | bytes 32800 | tf_op jit(solution)/shard_map/while/body/ppermute | solution.py:46
  35.6 3.3 %collective-permute-start.3 = (f32[32,256]{1,0:T(8,128)S(1)}, f32[32,256]{1,0:T(8,128)S(1)}, u32[]{:S(2)}, u32[]{:S(2)}) collective-permute-start(f32[32,256]{1,0:T(8,128)S(1)} %pad_maximum_fusion.8), channel_id=1, source_target_pairs={{0,97},{1,96},{2,99},{3,98},{4,101},{5,100},{6,103},{7,102},{8,105... | collective-permute-start | bytes 98312 | tf_op jit(solution)/shard_map/while/body/ppermute | solution.py:46
  38.9 2.6 %collective-permute-done.3 = f32[32,256]{1,0:T(8,128)S(1)} collective-permute-done((f32[32,256]{1,0:T(8,128)S(1)}, f32[32,256]{1,0:T(8,128)S(1)}, u32[]{:S(2)}, u32[]{:S(2)}) %collective-permute-start.3) | collective-permute-done | bytes 32800 | tf_op jit(solution)/shard_map/while/body/ppermute | solution.py:46
  41.7 1.5 %collective-permute-start.6 = (f32[72,256]{1,0:T(8,128)S(1)}, f32[72,256]{1,0:T(8,128)S(1)}, u32[]{:S(2)}, u32[]{:S(2)}) collective-permute-start(f32[72,256]{1,0:T(8,128)S(1)} %known.4), channel_id=1, source_target_pairs={{0,2},{1,3},{2,0},{3,1},{4,6},{5,7},{6,4},{7,5},{8,10},{9,11},{10,... | collective-permute-start | bytes 221192 | tf_op jit(solution)/shard_map/while/body/ppermute | solution.py:27
  44.0 1.3 %collective-permute-start.5 = (f32[32,256]{1,0:T(8,128)S(1)}, f32[32,256]{1,0:T(8,128)S(1)}, u32[]{:S(2)}, u32[]{:S(2)}) collective-permute-start(f32[32,256]{1,0:T(8,128)S(1)} %pad_maximum_fusion.9.message), channel_id=1, source_target_pairs={{0,131},{1,130},{2,129},{3,128},{4,135},{5,134},{6,133},{7,132},{8... | collective-permute-start | bytes 98312 | tf_op jit(solution)/shard_map/while/body/ppermute | solution.py:46
  45.3 2.0 %collective-permute-done.4 = f32[32,256]{1,0:T(8,128)S(1)} collective-permute-done((f32[32,256]{1,0:T(8,128)S(1)}, f32[32,256]{1,0:T(8,128)S(1)}, u32[]{:S(2)}, u32[]{:S(2)}) %collective-permute-start.4) | collective-permute-done | bytes 32800 | tf_op jit(solution)/shard_map/while/body/ppermute | solution.py:46
  47.3 1.3 %collective-permute-done.5 = f32[32,256]{1,0:T(8,128)S(1)} collective-permute-done((f32[32,256]{1,0:T(8,128)S(1)}, f32[32,256]{1,0:T(8,128)S(1)}, u32[]{:S(2)}, u32[]{:S(2)}) %collective-permute-start.5) | collective-permute-done | bytes 32800 | tf_op jit(solution)/shard_map/while/body/ppermute | solution.py:46
  49.2 1.2 %near.1.share = f32[2,512,256]{2,1,0:T(8,128)S(1)} custom-call(bf16[3,512,256]{2,1,0:T(8,128)(2,1)S(1)} %get-tuple-element.142.pack, f32[72,256]{1,0:T(8,128)S(1)} %get-tuple-element.146.mine, f32[32,256]{1,0:T(8,128)S(1)} %get-tuple-element.147.other, bf16[256,1024]{1,0:T(8,128)(2,1)S(1)} %get-tuple-element.148.w_out), custom_call_target="tpu_custom_call" | custom-call | flops 900000000 | bytes 4000000 | tf_op jit(solution)/shard_map/near/pallas_call | solution.py:456
  50.4 1.2 %far.1 = (f32[512,256]{1,0:T(8,128)S(1)}, bf16[512,256]{1,0:T(8,128)(2,1)S(1)}) custom-call(bf16[3,512,256]{2,1,0:T(8,128)(2,1)S(1)} %collective-permute-done.18.pack, f32[72,256]{1,0:T(8,128)S(1)} %copy-done.9, f32[32,256]{1,0:T(8,128)S(1)} %copy-done.11, f32[2,512,256]{2,1,0:T(8,128)S(1)} %near.1.share), custom_call_target="tpu_custom_call" | custom-call | flops 900000000 | bytes 4000000 | tf_op jit(solution)/shard_map/far/pallas_call | solution.py:466
  51.8 1.4 %collective-permute-done.19 = bf16[512,256]{1,0:T(8,128)(2,1)S(1)} collective-permute-done((bf16[512,256]{1,0:T(8,128)(2,1)S(1)}, bf16[512,256]{1,0:T(8,128)(2,1)S(1)}, u32[]{:S(2)}, u32[]{:S(2)}) %collective-permute-start.19) | collective-permute-done | bytes 262176 | tf_op jit(solution)/shard_map/ppermute | solution.py:27
  (92 shorter events, 10.2 us)
Async XLA Ops:
  0.0 7.0 %collective-permute-start.8 = (bf16[3,1024,256]{2,1,0:T(8,128)(2,1)}, bf16[3,1024,256]{2,1,0:T(8,128)(2,1)S(1)}, u32[]{:S(2)}, u32[]{:S(2)}) collective-permute-start(bf16[3,1024,256]{2,1,0:T(8,128)(2,1)} %bitcast.31), channel_id=1, source_target_pairs={{0,1},{1,0},{2,3},{3,2},{4,5},{5,4},{6,7},{7,6},{8,9},{9,8},{10,11... | collective-permute-start | bytes 4718600 | tf_op jit(solution)/shard_map/ppermute | solution.py:27
  3.2 9.7 %collective-permute-start.7 = (bf16[512,256]{1,0:T(8,128)(2,1)}, bf16[512,256]{1,0:T(8,128)(2,1)S(1)}, u32[]{:S(2)}, u32[]{:S(2)}) collective-permute-start(bf16[512,256]{1,0:T(8,128)(2,1)} %refs_0_.1), channel_id=1, source_target_pairs={{0,2},{1,3},{2,0},{3,1},{4,6},{5,7},{6,4},{7,5},{8,10},{9,11},{10,... | collective-permute-start | bytes 786440 | tf_op jit(solution)/shard_map/ppermute | solution.py:27
  4.2 13.5 %collective-permute-start.16 = (bf16[256,1024]{1,0:T(8,128)(2,1)}, bf16[256,1024]{1,0:T(8,128)(2,1)}, u32[]{:S(2)}, u32[]{:S(2)}) collective-permute-start(bf16[256,1024]{1,0:T(8,128)(2,1)} %w_out.1), channel_id=1, source_target_pairs={{0,1},{1,0},{2,3},{3,2},{4,5},{5,4},{6,7},{7,6},{8,9},{9,8},{10,11... | collective-permute-start | bytes 1572872 | tf_op jit(solution)/shard_map/ppermute | solution.py:27
  4.5 2.4 %collective-permute-start.10 = (f32[16,256]{1,0:T(8,128)}, f32[16,256]{1,0:T(8,128)S(1)}, u32[]{:S(2)}, u32[]{:S(2)}) collective-permute-start(f32[16,256]{1,0:T(8,128)} %refs_6_.1), channel_id=1, source_target_pairs={{0,1},{1,0},{2,3},{3,2},{4,5},{5,4},{6,7},{7,6},{8,9},{9,8},{10,11... | collective-permute-start | bytes 49160 | tf_op jit(solution)/shard_map/ppermute | solution.py:27
  4.8 1.8 %collective-permute-start.9 = (f32[3,3,256]{2,1,0:T(4,128)}, f32[3,3,256]{2,1,0:T(4,128)S(1)}, u32[]{:S(2)}, u32[]{:S(2)}) collective-permute-start(f32[3,3,256]{2,1,0:T(4,128)} %refs_4_.1), channel_id=1, source_target_pairs={{0,1},{1,0},{2,3},{3,2},{4,5},{5,4},{6,7},{7,6},{8,9},{9,8},{10,11... | collective-permute-start | bytes 27656 | tf_op jit(solution)/shard_map/ppermute | solution.py:27
  6.6 7.6 %collective-permute-start.11 = (bf16[512,256]{1,0:T(8,128)(2,1)}, bf16[512,256]{1,0:T(8,128)(2,1)S(1)}, u32[]{:S(2)}, u32[]{:S(2)}) collective-permute-start(bf16[512,256]{1,0:T(8,128)(2,1)} %refs_0_.1), channel_id=1, source_target_pairs={{0,1},{1,0},{2,3},{3,2},{4,5},{5,4},{6,7},{7,6},{8,9},{9,8},{10,11... | collective-permute-start | bytes 786440 | tf_op jit(solution)/shard_map/ppermute | solution.py:27
  7.0 1.4 %copy-start = (bf16[1024,3,256]{2,0,1:T(8,128)(2,1)S(1)}, bf16[1024,3,256]{2,0,1:T(8,128)(2,1)}, u32[]{:S(2)}) copy-start(bf16[1024,3,256]{2,0,1:T(8,128)(2,1)} %param.12) | copy-start | bytes 4718596
  11.4 2.3 %copy-start.6 = (f32[16,256]{1,0:T(8,128)S(1)}, f32[16,256]{1,0:T(8,128)}, u32[]{:S(2)}) copy-start(f32[16,256]{1,0:T(8,128)} %residues.1) | copy-start | bytes 49156
  11.4 2.3 %copy-start.7 = (f32[256]{0:T(256)S(1)}, f32[256]{0:T(256)}, u32[]{:S(2)}) copy-start(f32[256]{0:T(256)} %param.16) | copy-start | bytes 3076
  11.6 6.1 %copy-start.5 = (bf16[256,1024]{1,0:T(8,128)(2,1)S(1)}, bf16[256,1024]{1,0:T(8,128)(2,1)}, u32[]{:S(2)}) copy-start(bf16[256,1024]{1,0:T(8,128)(2,1)} %w_out.1) | copy-start | bytes 1572868
  12.9 1.9 %collective-permute-start.12 = (bf16[512,256]{1,0:T(8,128)(2,1)S(1)}, bf16[512,256]{1,0:T(8,128)(2,1)S(1)}, u32[]{:S(2)}, u32[]{:S(2)}) collective-permute-start(bf16[512,256]{1,0:T(8,128)(2,1)S(1)} %collective-permute-done.7.far), channel_id=1, source_target_pairs={{0,1},{1,0},{2,3},{3,2},{4,5},{5,4},{6,7},{7,6},{8,9},{9,8},{10,11... | collective-permute-start | bytes 786440 | tf_op jit(solution)/shard_map/ppermute | solution.py:27
  13.7 4.1 %collective-permute-start.14 = (f32[16,256]{1,0:T(8,128)S(1)}, f32[16,256]{1,0:T(8,128)S(1)}, u32[]{:S(2)}, u32[]{:S(2)}) collective-permute-start(f32[16,256]{1,0:T(8,128)S(1)} %copy-done.6), channel_id=1, source_target_pairs={{0,1},{1,0},{2,3},{3,2},{4,5},{5,4},{6,7},{7,6},{8,9},{9,8},{10,11... | collective-permute-start | bytes 49160 | tf_op jit(solution)/shard_map/ppermute | solution.py:27
  13.7 4.1 %collective-permute-start.15 = (f32[1,256]{1,0:T(1,128)S(1)}, f32[1,256]{1,0:T(1,128)S(1)}, u32[]{:S(2)}, u32[]{:S(2)}) collective-permute-start(f32[1,256]{1,0:T(1,128)S(1)} %bitcast.34), channel_id=1, source_target_pairs={{0,1},{1,0},{2,3},{3,2},{4,5},{5,4},{6,7},{7,6},{8,9},{9,8},{10,11... | collective-permute-start | bytes 3080 | tf_op jit(solution)/shard_map/ppermute | solution.py:27
  17.6 3.5 %collective-permute-start.13 = (f32[32,256]{1,0:T(8,128)S(1)}, f32[32,256]{1,0:T(8,128)S(1)}, u32[]{:S(2)}, u32[]{:S(2)}) collective-permute-start(f32[32,256]{1,0:T(8,128)S(1)} %get-tuple-element.127), channel_id=1, source_target_pairs={{0,5},{1,4},{2,7},{3,6},{4,1},{5,0},{6,3},{7,2},{8,13},{9,12},{10,... | collective-permute-start | bytes 98312 | tf_op jit(solution)/shard_map/ppermute | solution.py:46
  21.2 4.7 %collective-permute-start.17 = (f32[32,256]{1,0:T(8,128)S(1)}, f32[32,256]{1,0:T(8,128)S(1)}, u32[]{:S(2)}, u32[]{:S(2)}) collective-permute-start(f32[32,256]{1,0:T(8,128)S(1)} %pad_maximum_fusion.4), channel_id=1, source_target_pairs={{0,13},{1,12},{2,15},{3,14},{4,9},{5,8},{6,11},{7,10},{8,5},{9,4},... | collective-permute-start | bytes 98312 | tf_op jit(solution)/shard_map/ppermute | solution.py:46
  22.6 26.6 %collective-permute-start.18 = (bf16[3,512,256]{2,1,0:T(8,128)(2,1)S(1)}, bf16[3,512,256]{2,1,0:T(8,128)(2,1)S(1)}, u32[]{:S(2)}, u32[]{:S(2)}) collective-permute-start(bf16[3,512,256]{2,1,0:T(8,128)(2,1)S(1)} %get-tuple-element.142.pack), channel_id=1, source_target_pairs={{0,2},{1,3},{2,0},{3,1},{4,6},{5,7},{6,4},{7,5},{8,10},{9,11},{10,... | collective-permute-start | bytes 2359304 | tf_op jit(solution)/shard_map/ppermute | solution.py:27
  26.7 5.4 %collective-permute-start.1 = (f32[32,256]{1,0:T(8,128)S(1)}, f32[32,256]{1,0:T(8,128)S(1)}, u32[]{:S(2)}, u32[]{:S(2)}) collective-permute-start(f32[32,256]{1,0:T(8,128)S(1)} %get-tuple-element.355), channel_id=1, source_target_pairs={{0,48},{1,49},{2,50},{3,51},{4,52},{5,53},{6,54},{7,55},{8,56},{9,... | collective-permute-start | bytes 98312 | tf_op jit(solution)/shard_map/while/body/ppermute | solution.py:46
  30.5 4.9 %collective-permute-start.2 = (f32[32,256]{1,0:T(8,128)S(1)}, f32[32,256]{1,0:T(8,128)S(1)}, u32[]{:S(2)}, u32[]{:S(2)}) collective-permute-start(f32[32,256]{1,0:T(8,128)S(1)} %get-tuple-element.355), channel_id=1, source_target_pairs={{0,33},{1,32},{2,35},{3,34},{4,37},{5,36},{6,39},{7,38},{8,41},{9,... | collective-permute-start | bytes 98312 | tf_op jit(solution)/shard_map/while/body/ppermute | solution.py:46
  30.5 4.9 %collective-permute-start = (f32[32,256]{1,0:T(8,128)S(1)}, f32[32,256]{1,0:T(8,128)S(1)}, u32[]{:S(2)}, u32[]{:S(2)}) collective-permute-start(f32[32,256]{1,0:T(8,128)S(1)} %get-tuple-element.355), channel_id=1, source_target_pairs={{0,17},{1,16},{2,19},{3,18},{4,21},{5,20},{6,23},{7,22},{8,25},{9,... | collective-permute-start | bytes 98312 | tf_op jit(solution)/shard_map/while/body/ppermute | solution.py:46
  35.6 5.9 %collective-permute-start.3 = (f32[32,256]{1,0:T(8,128)S(1)}, f32[32,256]{1,0:T(8,128)S(1)}, u32[]{:S(2)}, u32[]{:S(2)}) collective-permute-start(f32[32,256]{1,0:T(8,128)S(1)} %pad_maximum_fusion.8), channel_id=1, source_target_pairs={{0,97},{1,96},{2,99},{3,98},{4,101},{5,100},{6,103},{7,102},{8,105... | collective-permute-start | bytes 98312 | tf_op jit(solution)/shard_map/while/body/ppermute | solution.py:46
  41.7 6.9 %collective-permute-start.6 = (f32[72,256]{1,0:T(8,128)S(1)}, f32[72,256]{1,0:T(8,128)S(1)}, u32[]{:S(2)}, u32[]{:S(2)}) collective-permute-start(f32[72,256]{1,0:T(8,128)S(1)} %known.4), channel_id=1, source_target_pairs={{0,2},{1,3},{2,0},{3,1},{4,6},{5,7},{6,4},{7,5},{8,10},{9,11},{10,... | collective-permute-start | bytes 221192 | tf_op jit(solution)/shard_map/while/body/ppermute | solution.py:27
  43.2 4.0 %collective-permute-start.4 = (f32[32,256]{1,0:T(8,128)S(1)}, f32[32,256]{1,0:T(8,128)S(1)}, u32[]{:S(2)}, u32[]{:S(2)}) collective-permute-start(f32[32,256]{1,0:T(8,128)S(1)} %pad_maximum_fusion.9.message), channel_id=1, source_target_pairs={{0,129},{1,128},{2,131},{3,130},{4,133},{5,132},{6,135},{7,134},{8... | collective-permute-start | bytes 98312 | tf_op jit(solution)/shard_map/while/body/ppermute | solution.py:46
  44.0 4.6 %collective-permute-start.5 = (f32[32,256]{1,0:T(8,128)S(1)}, f32[32,256]{1,0:T(8,128)S(1)}, u32[]{:S(2)}, u32[]{:S(2)}) collective-permute-start(f32[32,256]{1,0:T(8,128)S(1)} %pad_maximum_fusion.9.message), channel_id=1, source_target_pairs={{0,131},{1,130},{2,129},{3,128},{4,135},{5,134},{6,133},{7,132},{8... | collective-permute-start | bytes 98312 | tf_op jit(solution)/shard_map/while/body/ppermute | solution.py:46
  51.5 1.6 %collective-permute-start.19 = (bf16[512,256]{1,0:T(8,128)(2,1)S(1)}, bf16[512,256]{1,0:T(8,128)(2,1)S(1)}, u32[]{:S(2)}, u32[]{:S(2)}) collective-permute-start(bf16[512,256]{1,0:T(8,128)(2,1)S(1)} %get-tuple-element.150), channel_id=1, source_target_pairs={{0,1},{1,0},{2,3},{3,2},{4,5},{5,4},{6,7},{7,6},{8,9},{9,8},{10,11... | collective-permute-start | bytes 786440 | tf_op jit(solution)/shard_map/ppermute | solution.py:27
  (8 other events, 6.7 us)
